TPU v7x, 512 devices: a whole 4x4x16 slice. The times are simulated.
512 devices in a mesh: rep: 8 (over y, core), exp: 64 (over x, z).
Axes of the slice: x: 4, y: 4, z: 16, core: 2. Of those that a mesh axis runs over, the one named last changes fastest.
Arguments:
- grad_out: bfloat16 [65536, 2048], P(('rep', 'exp')), may hold values from -6 to 6
- expert_ids: int32 [65536, 8], P(('rep', 'exp')), may hold values from 0 to 63, all different within a row; in each aligned block of 128 rows (0 to 127, 128 to 255, ...) at most 20 rows name the same one
- gates: float32 [65536, 8], P(('rep', 'exp')), may hold values from 0.02 to 0.5
- hidden: bfloat16 [8, 64, 1280, 768], P('rep', 'exp'), may hold values from -6 to 6
- w_down: bfloat16 [64, 768, 2048], P('exp', 'rep'), may hold values from -0.21875 to 0.21875
- q_start: float32 [64, 2048, 32], P('exp'), may hold values from -6 to 6
Outputs:
- grad_hidden: bfloat16 [65536, 8, 768], P(('rep', 'exp'))
- p_basis: float32 [64, 768, 32], P('exp')
- q_factor: float32 [64, 2048, 32], P('exp')
Inputs may be any that keep to these rules, and one draw needn't show every extreme that they name: `expert_ids`: within the 128 rows of one device no expert is named more than 20 times, a bound that some block reaches.
All inputs are finite; a program needn't handle non-finite values.
Results may differ from a plain program's by a relative error of at most 0.0049.
Values may be sent and summed in bfloat16 or wider, within the bound.
No kernel may reach another device: no remote copies, remote signals or barrier semaphores. Data moves between devices by JAX's collectives and lax.ppermute only.
A program may use at most 128 MiB of HBM per device.

v0:
```python
import math

import jax
import jax.numpy as jnp
from jax import lax
from jax.sharding import PartitionSpec as P


def orthonormal(p_sum):
    gram_matrix = jnp.dot(p_sum.T, p_sum, precision=lax.Precision.HIGHEST)
    factor = jnp.linalg.cholesky(gram_matrix)
    return jax.scipy.linalg.solve_triangular(factor, p_sum.T, lower=True).T


def shards(grad_out, expert_ids, gates, hidden, w_down, q_start):
    n_exp = lax.axis_size("exp")
    n_rep = lax.axis_size("rep")
    tok_rows, top_count = expert_ids.shape
    model_width = grad_out.shape[1]
    slot_total = hidden.shape[2]
    hidden_units = hidden.shape[3]
    capacity = slot_total // n_exp
    pair_count = tok_rows * top_count
    flat_ids = expert_ids.reshape(pair_count)
    onehot = (flat_ids[:, None] == jnp.arange(n_exp, dtype=jnp.int32)[None, :]).astype(jnp.int32)
    slot_index = jnp.sum(onehot * (jnp.cumsum(onehot, axis=0) - 1), axis=1)
    where_to = flat_ids * capacity + slot_index
    scaled = (grad_out.astype(jnp.float32)[:, None, :] * gates[:, :, None]).astype(jnp.bfloat16)
    scaled = scaled.reshape(pair_count, model_width)
    outbox = jnp.zeros((n_exp * capacity, model_width), jnp.bfloat16).at[where_to].set(scaled)
    outbox = outbox.reshape(n_exp, capacity, model_width)
    inbox = lax.all_to_all(outbox, "exp", split_axis=0, concat_axis=0, tiled=True)
    expert_rows = inbox.reshape(slot_total, model_width)
    back_rows = jnp.einsum(
        "sd,fd->sf",
        expert_rows,
        lax.all_gather(w_down, "rep", axis=1, tiled=True)[0],
        preferred_element_type=jnp.float32,
    ).astype(jnp.bfloat16)
    returned = lax.all_to_all(
        back_rows.reshape(n_exp, capacity, hidden_units),
        "exp",
        split_axis=0,
        concat_axis=0,
        tiled=True,
    )
    grad_hidden = returned.reshape(n_exp * capacity, hidden_units)[where_to]
    grad_hidden = grad_hidden.reshape(tok_rows, top_count, hidden_units)
    stored = hidden[0, 0].astype(jnp.float32)
    rows_wide = expert_rows.astype(jnp.float32)
    projected = jnp.dot(rows_wide, q_start[0], precision=lax.Precision.HIGHEST)
    p_part = jnp.dot(stored.T, projected, precision=lax.Precision.HIGHEST)
    p_sum = lax.psum(p_part, "rep")
    factor_basis = orthonormal(p_sum)
    mapped = jnp.dot(stored, factor_basis, precision=lax.Precision.HIGHEST)
    q_part = jnp.dot(rows_wide.T, mapped, precision=lax.Precision.HIGHEST)
    q_factor = lax.psum(q_part, "rep") / n_rep
    p_basis = factor_basis * math.sqrt(hidden_units)
    return (grad_hidden, p_basis[None], q_factor[None])


def solution(mesh):
    in_specs = (
        P(("rep", "exp"), None),
        P(("rep", "exp"), None),
        P(("rep", "exp"), None),
        P("rep", "exp", None, None),
        P("exp", "rep", None),
        P("exp", None, None),
    )
    out_specs = (P(("rep", "exp"), None, None), P("exp", None, None), P("exp", None, None))
    return jax.shard_map(shards, mesh=mesh, in_specs=in_specs, out_specs=out_specs, check_vma=False)
```

profile of v0, /device:TPU:1, one launch (start us, length us, event | category | flops | bytes accessed | tf_op | source)
XLA Modules:
  0.0 569.3 jit_solution(6224450402453734526)
XLA Ops:
  7.2 0.0 copy-start
  7.2 0.9 copy.11
  8.1 0.1 eq.29
  8.2 0.1 eq.25
  8.3 0.7 broadcast_multiply_fusion
  9.0 18.0 %reduce-window.6 = s32[64,8,128]{2,1,0:T(8,128)S(1)} reduce-window(s32[64,8,128]{2,1,0:T(8,128)S(1)} %fusion.18, s32[]{:T(128)} %constant.55.clone.1), window={size=1x1x128 pad=0_0x0_0x127_0}, to_apply=%region_0.0 | reduce-window | flops 8323072 | bytes 524292 | tf_op jit(solution)/shard_map/reduce-window
  27.0 0.1 slice.22
  27.1 0.1 copy.13
  27.3 0.1 copy.14
  27.4 0.1 add_add_fusion
  27.6 0.1 copy.10
  27.7 0.1 mul.48
  27.8 1.1 convert_element_type.18
  28.9 0.8 copy.15
  29.7 0.1 mul.52
  29.8 0.1 fusion.15
  29.9 10.0 %scatter_custom_fusion = bf16[1280,2048]{1,0:T(8,128)(2,1)} fusion(s32[1024]{0:T(1024)S(1)} %bitcast.65, f32[1024]{0:T(1024)S(1)} %mul.52, f32[128,2048]{1,0:T(8,128)S(1)} %convert_element_type.18, bf16[]{:T(256)} %constant.53.clone.1), kind=kCustom, calls=%fused_computation.4 | custom fusion | flops 4194304 | bytes 6295554 | tf_op jit(solution)/shard_map/scatter | solution.py:30
  39.9 8.9 %reshape.86 = bf16[64,20,2048]{2,1,0:T(8,128)(2,1)} reshape(bf16[1280,2048]{1,0:T(8,128)(2,1)} %scatter_custom_fusion) | data formatting | bytes 10485760 | tf_op jit(solution)/shard_map/reshape | solution.py:31
  48.8 19.3 %all-to-all-start = ((bf16[64,20,2048]{2,1,0:T(8,128)(2,1)}), bf16[64,20,2048]{2,1,0:T(8,128)(2,1)}, u32[]{:S(2)}, u32[]{:S(2)}) async-start(bf16[64,20,2048]{2,1,0:T(8,128)(2,1)} %reshape.86), calls=%async_computation | async-start | bytes 12582912 | tf_op jit(solution)/shard_map/all_to_all | solution.py:32
  68.2 0.0 all-gather.2.cloned.1.call-start
  68.2 0.7 all-gather.2.cloned.1.call-update
  68.9 272.6 %all-to-all-done = bf16[64,20,2048]{2,1,0:T(8,128)(2,1)} async-done(((bf16[64,20,2048]{2,1,0:T(8,128)(2,1)}), bf16[64,20,2048]{2,1,0:T(8,128)(2,1)}, u32[]{:S(2)}, u32[]{:S(2)}) %all-to-all-start) | async-done | bytes 5242912 | tf_op jit(solution)/shard_map/all_to_all | solution.py:32
  341.5 9.0 %reshape.87 = bf16[1280,2048]{1,0:T(8,128)(2,1)} reshape(bf16[64,20,2048]{2,1,0:T(8,128)(2,1)} %all-to-all-done) | data formatting | bytes 10485760 | tf_op jit(solution)/shard_map/reshape | solution.py:33
  350.5 0.0 all-gather.2.cloned.1.call-done
  350.5 9.0 %convolution_convert_fusion = bf16[1280,768]{1,0:T(8,128)(2,1)} fusion(bf16[1280,2048]{1,0:T(8,128)(2,1)} %reshape.87, bf16[1,768,2048]{2,1,0:T(8,128)(2,1)} %all-gather.2.cloned.1.call-done), kind=kOutput, calls=%fused_computation.7 | convolution fusion | flops 4027514880 | bytes 10354688 | tf_op jit(solution)/shard_map/sd,fd->sf/dot_general | solution.py:34
  359.5 0.0 copy-start.1
  359.5 4.0 reshape.88
  363.5 11.6 %all-to-all-start.1 = ((bf16[64,20,768]{2,1,0:T(8,128)(2,1)}), bf16[64,20,768]{2,1,0:T(8,128)(2,1)}, u32[]{:S(2)}, u32[]{:S(2)}) async-start(bf16[64,20,768]{2,1,0:T(8,128)(2,1)} %reshape.88), calls=%async_computation.1 | async-start | bytes 4718592 | tf_op jit(solution)/shard_map/all_to_all | solution.py:40
  375.1 0.0 all-reduce.3.cloned.1.call-start
  375.1 0.0 copy-done.1
  375.2 6.1 %fusion.16 = f32[1280,32]{1,0:T(8,128)S(1)} fusion(bf16[1280,2048]{1,0:T(8,128)(2,1)} %reshape.87, f32[1,2048,32]{1,2,0:T(8,128)S(1)} %copy-done.1), kind=kOutput, calls=%fused_computation.18 | convolution fusion | flops 1006632960 | bytes 5668864 | tf_op jit(solution)/shard_map/dot_general | solution.py:51
  381.3 0.0 copy-done
  381.3 1.8 fusion.11
  383.1 0.0 all-reduce.3.cloned.1.call-update
  383.1 0.0 all-reduce.5.cloned.1.call-start
  383.2 75.8 %all-reduce.3.cloned.1.call-done = f32[768,32]{0,1:T(8,128)} async-done(((f32[768,32]{0,1:T(8,128)}), f32[768,32]{0,1:T(8,128)}) %all-reduce.3.cloned.1.call-update) | async-done | bytes 98320 | tf_op jit(solution)/shard_map/psum | solution.py:53
  458.9 1.2 fusion.23
  460.1 0.1 copy.16
  460.2 2.9 cholesky.16
  463.2 0.6 compare_reduce_fusion
  463.8 0.7 fusion.19
  464.5 2.4 custom-call.7
  466.9 1.2 fusion.20
  468.1 1.8 fusion.7
  469.9 5.9 %fusion.24 = f32[2048,32]{0,1:T(8,128)} fusion(bf16[1280,2048]{1,0:T(8,128)(2,1)} %reshape.87, f32[32,1280]{1,0:T(8,128)S(1)} %fusion.7), kind=kOutput, calls=%fused_computation.40 | convolution fusion | flops 1006632960 | bytes 5668864 | tf_op jit(solution)/shard_map/dot_general | solution.py:56
  475.8 0.0 all-reduce.5.cloned.1.call-update
  475.8 0.7 multiply_bitcast_fusion.1
  476.4 73.3 %all-reduce.5.cloned.1.call-done = f32[2048,32]{0,1:T(8,128)} async-done(((f32[2048,32]{0,1:T(8,128)}), f32[2048,32]{0,1:T(8,128)}) %all-reduce.5.cloned.1.call-update) | async-done | bytes 262160 | tf_op jit(solution)/shard_map/psum | solution.py:57
  549.8 1.7 multiply_bitcast_fusion
  551.4 0.0 all-to-all-done.1
  551.4 3.9 reshape.89
  555.4 7.4 %gather_fusion = bf16[1024,768]{1,0:T(8,128)(2,1)} fusion(bf16[1280,768]{1,0:T(8,128)(2,1)} %reshape.89, s32[1024]{0:T(1024)S(1)} %broadcast_clamp_fusion), kind=kCustom, calls=%fused_computation | custom fusion | bytes 3149824 | tf_op jit(solution)/shard_map/gather | solution.py:47
  (7 shorter events, 0.1 us)
Async XLA Ops:
  7.2 374.1 %copy-start = (bf16[1,1,1280,768]{3,2,1,0:T(8,128)(2,1)S(1)}, bf16[1,1,1280,768]{3,2,1,0:T(8,128)(2,1)}, u32[]{:S(2)}) copy-start(bf16[1,1,1280,768]{3,2,1,0:T(8,128)(2,1)} %param.9) | copy-start | bytes 5898244
  48.8 292.7 %all-to-all-start = ((bf16[64,20,2048]{2,1,0:T(8,128)(2,1)}), bf16[64,20,2048]{2,1,0:T(8,128)(2,1)}, u32[]{:S(2)}, u32[]{:S(2)}) async-start(bf16[64,20,2048]{2,1,0:T(8,128)(2,1)} %reshape.86), calls=%async_computation | async-start | bytes 12582912 | tf_op jit(solution)/shard_map/all_to_all | solution.py:32
  68.2 282.3 %all-gather.2.cloned.1.call-start = ((), (), s32[]{:S(2)}) async-start(), calls=%async_computation.2 | async-start | bytes 3538944 | tf_op jit(solution)/shard_map/all_gather | solution.py:37
  359.5 15.6 %copy-start.1 = (f32[1,2048,32]{1,2,0:T(8,128)S(1)}, f32[1,2048,32]{1,2,0:T(8,128)}, u32[]{:S(2)}) copy-start(f32[1,2048,32]{1,2,0:T(8,128)} %param.11) | copy-start | bytes 786436
  363.5 188.0 %all-to-all-start.1 = ((bf16[64,20,768]{2,1,0:T(8,128)(2,1)}), bf16[64,20,768]{2,1,0:T(8,128)(2,1)}, u32[]{:S(2)}, u32[]{:S(2)}) async-start(bf16[64,20,768]{2,1,0:T(8,128)(2,1)} %reshape.88), calls=%async_computation.1 | async-start | bytes 4718592 | tf_op jit(solution)/shard_map/all_to_all | solution.py:40
  375.1 83.8 %all-reduce.3.cloned.1.call-start = ((), (), s32[]{:S(2)}) async-start(), calls=%async_computation.3 | async-start | bytes 196608 | tf_op jit(solution)/shard_map/psum | solution.py:53
  383.1 166.7 %all-reduce.5.cloned.1.call-start = ((), (), s32[]{:S(2)}) async-start(), calls=%async_computation.4 | async-start | bytes 524288 | tf_op jit(solution)/shard_map/psum | solution.py:57
Sparse Core Ops, SparseCore 0:
  71.1 37.1 all-gather.1
  383.2 75.6 all-reduce.2
  475.9 73.8 all-reduce.4
where the time goes:
time: 571 us; the launch traced here: 569 us
  waiting for transfers between devices  422 us (74%)
  other arithmetic  39.1 us (7%)
  local copies, waits for them, and re-layouts  35.8 us (6%)
  starting transfers between devices  31.1 us (5%)
  matrix products  27 us (5%)
  between operations  13.9 us (2%)
    all_to_all x1, waiting for transfers between devices, shards(): lax.all_to_all(outbox, 'exp', split_axis=0, concat_axis=0, tiled=True)  273 us
    psum x1, waiting for transfers between devices, shards(): p_sum = lax.psum(p_part, 'rep')  75.8 us
    psum x1, waiting for transfers between devices, shards(): q_factor = lax.psum(q_part, 'rep') / n_rep  73.3 us
    all_to_all x1, starting transfers between devices, shards(): lax.all_to_all(outbox, 'exp', split_axis=0, concat_axis=0, tiled=True)  19.3 us
    another operation x2, other arithmetic  18 us
    all_to_all x1, starting transfers between devices, shards(): lax.all_to_all(back_rows.reshape(n_exp, capacity, hidden_units), 'exp', s...  11.6 us
  transfers between devices with their start and end apart: 5, of which 3 were waited for; matrix products, arithmetic and copies ran while one was open for 6% of the time, Pallas kernels for 0%

commit v1 on v0

v1 whole, which is shorter than its diff:
```python
import math

import jax
import jax.numpy as jnp
from jax import lax
from jax.experimental import pallas as pl
from jax.experimental.pallas import tpu as pltpu
from jax.sharding import Mesh
from jax.sharding import PartitionSpec as P

N_X = 4
N_Z = 16
N_REP = 8
CAP = 20
TOK = 128
D = 2048
FF = 768
RANK = 32
GROUP = 4
BF = jnp.bfloat16
F32 = jnp.float32
NT = (((1,), (1,)), ((), ()))
NN = (((1,), (0,)), ((), ()))


def dot(a, b, dims=NN):
    return lax.dot_general(a, b, dims, preferred_element_type=F32)


def three(a):
    high = a.astype(BF)
    rest = a - high.astype(F32)
    mid = rest.astype(BF)
    low = (rest - mid.astype(F32)).astype(BF)
    return jnp.concatenate([high, mid, low], axis=0)


def fold(a):
    n = a.shape[0] // 3
    return a[:n] + a[n : 2 * n] + a[2 * n :]


def rows_kernel(z_ref, tokens_ref, meta_ref, rows_ref):
    z = z_ref[0]
    earlier = (
        lax.broadcasted_iota(jnp.int32, (TOK, TOK), 0) < lax.broadcasted_iota(jnp.int32, (TOK, TOK), 1)
    ).astype(F32).astype(BF)
    named, scale = [], []
    for x in range(N_X):
        expert = (x * N_Z + z).astype(F32)
        for b in range(GROUP):
            hit = meta_ref[b, 0:8, :] == expert
            named.append(jnp.sum(jnp.where(hit, 1.0, 0.0), axis=0, keepdims=True))
            scale.append(jnp.sum(jnp.where(hit, meta_ref[b, 8:16, :], 0.0), axis=0, keepdims=True))
    named_all = jnp.concatenate(named, axis=0)
    rank = dot(named_all.astype(BF), earlier)
    slot_of = lax.broadcasted_iota(jnp.int32, (GROUP * CAP, TOK), 0).astype(F32)
    picks, factors = [], []
    for x in range(N_X):
        parts = []
        factor = jnp.zeros((GROUP * CAP, 1), F32)
        for b in range(GROUP):
            i = x * GROUP + b
            target = jnp.where(named[i] > 0.5, rank[i : i + 1, :] + float(b * CAP), -1.0)
            hit = slot_of == target
            parts.append(jnp.where(hit, 1.0, 0.0).astype(BF))
            factor += jnp.sum(jnp.where(hit, scale[i], 0.0), axis=1, keepdims=True)
        picks.append(jnp.concatenate(parts, axis=1))
        factors.append(factor)
    for x in range(N_X):
        for c in range(0, D, 512):
            taken = dot(picks[x], tokens_ref[:, c : c + 512])
            rows_ref[x, :, c : c + 512] = (taken * factors[x]).astype(BF)


def make_rows(z, tokens, meta):
    return pl.pallas_call(
        rows_kernel,
        grid_spec=pltpu.PrefetchScalarGridSpec(
            num_scalar_prefetch=1,
            grid=(N_Z // GROUP,),
            in_specs=[
                pl.BlockSpec((GROUP * TOK, D), lambda g, s: (g, 0)),
                pl.BlockSpec((GROUP, 16, TOK), lambda g, s: (g, 0, 0)),
            ],
            out_specs=pl.BlockSpec((N_X, GROUP * CAP, D), lambda g, s: (0, g, 0)),
        ),
        out_shape=jax.ShapeDtypeStruct((N_X, N_Z * CAP, D), BF),
        compiler_params=pltpu.CompilerParams(vmem_limit_bytes=40 << 20),
        cost_estimate=pl.CostEstimate(flops=3 * 10**9, bytes_accessed=14 << 20, transcendentals=0),
        name="rows",
    )(z, tokens, meta)


def left_kernel(rows_ref, warm_ref, hidden_ref, part_ref):
    projected = fold(dot(three(warm_ref[0]), rows_ref[0], NT))
    part_ref[0] = fold(dot(three(projected), hidden_ref[0]))


def left_part(rows, warm, hidden):
    slots = N_Z * CAP
    return pl.pallas_call(
        left_kernel,
        grid=(N_X,),
        in_specs=[
            pl.BlockSpec((1, slots, D), lambda x: (x, 0, 0)),
            pl.BlockSpec((1, RANK, D), lambda x: (x, 0, 0)),
            pl.BlockSpec((1, slots, FF), lambda x: (x, 0, 0)),
        ],
        out_specs=pl.BlockSpec((1, RANK, FF), lambda x: (x, 0, 0)),
        out_shape=jax.ShapeDtypeStruct((N_X, RANK, FF), F32),
        compiler_params=pltpu.CompilerParams(vmem_limit_bytes=40 << 20),
        cost_estimate=pl.CostEstimate(flops=10**9, bytes_accessed=9 << 20, transcendentals=0),
        name="left",
    )(rows, warm, hidden)


def back_kernel(rows_ref, weight_ref, back_ref, held_ref):
    x = pl.program_id(0)
    for c in range(0, FF, 256):
        held_ref[pl.ds(x, 1), :, c : c + 256] = dot(rows_ref[0], weight_ref[0, c : c + 256, :], NT).astype(BF)[None]

    @pl.when(x == N_X - 1)
    def _():
        span = GROUP * CAP
        n = N_X * span
        to = lax.broadcasted_iota(jnp.int32, (n, n), 0)
        of = lax.broadcasted_iota(jnp.int32, (n, n), 1)
        of_x, of_b, of_c = of // span, (of % span) // CAP, of % CAP
        move = jnp.where(to == of_b * (N_X * CAP) + of_x * CAP + of_c, 1.0, 0.0).astype(BF)
        for g in range(N_Z // GROUP):
            source = jnp.concatenate([held_ref[i, g * span : (g + 1) * span, :] for i in range(N_X)], axis=0)
            moved = dot(move, source).astype(BF)
            for b in range(GROUP):
                back_ref[g * GROUP + b] = moved[b * N_X * CAP : (b + 1) * N_X * CAP]


def back_rows(rows, weights):
    slots = N_Z * CAP
    return pl.pallas_call(
        back_kernel,
        grid=(N_X,),
        in_specs=[
            pl.BlockSpec((1, slots, D), lambda x: (x, 0, 0)),
            pl.BlockSpec((1, FF, D), lambda x: (x, 0, 0)),
        ],
        out_specs=pl.BlockSpec((N_Z, N_X * CAP, FF), lambda x: (0, 0, 0)),
        out_shape=jax.ShapeDtypeStruct((N_Z, N_X * CAP, FF), BF),
        scratch_shapes=[pltpu.VMEM((N_X, slots, FF), BF)],
        compiler_params=pltpu.CompilerParams(vmem_limit_bytes=48 << 20),
        cost_estimate=pl.CostEstimate(flops=5 * 10**9, bytes_accessed=20 << 20, transcendentals=0),
        name="back",
    )(rows, weights)


def right_kernel(basis_ref, hidden_ref, rows_ref, part_ref):
    mapped = fold(dot(three(basis_ref[0]), hidden_ref[0], NT))
    part_ref[0] = fold(dot(three(mapped), rows_ref[0]))


def right_part(basis, hidden, rows):
    slots = N_Z * CAP
    return pl.pallas_call(
        right_kernel,
        grid=(N_X,),
        in_specs=[
            pl.BlockSpec((1, RANK, FF), lambda x: (x, 0, 0)),
            pl.BlockSpec((1, slots, FF), lambda x: (x, 0, 0)),
            pl.BlockSpec((1, slots, D), lambda x: (x, 0, 0)),
        ],
        out_specs=pl.BlockSpec((1, RANK, D), lambda x: (x, 0, 0)),
        out_shape=jax.ShapeDtypeStruct((N_X, RANK, D), F32),
        compiler_params=pltpu.CompilerParams(vmem_limit_bytes=40 << 20),
        cost_estimate=pl.CostEstimate(flops=10**9, bytes_accessed=9 << 20, transcendentals=0),
        name="right",
    )(basis, hidden, rows)


def spread_kernel(place_ref, rows_ref, out_ref):
    count = rows_ref.shape[0]
    pairs = place_ref.shape[0]
    pick = jnp.where(lax.broadcasted_iota(jnp.int32, (pairs, count), 1) == place_ref[...], 1.0, 0.0).astype(BF)
    out_ref[...] = dot(pick, rows_ref[...]).astype(BF).reshape(out_ref.shape)


def spread(place, rows):
    count = rows.shape[0]
    pairs = 256
    return pl.pallas_call(
        spread_kernel,
        grid=(TOK * 8 // pairs,),
        in_specs=[
            pl.BlockSpec((pairs, 1), lambda i: (i, 0)),
            pl.BlockSpec((count, FF), lambda i: (0, 0)),
        ],
        out_specs=pl.BlockSpec((pairs // 8, 8, FF), lambda i: (i, 0, 0)),
        out_shape=jax.ShapeDtypeStruct((TOK, 8, FF), BF),
        compiler_params=pltpu.CompilerParams(vmem_limit_bytes=40 << 20),
        cost_estimate=pl.CostEstimate(flops=2 * 10**9, bytes_accessed=4 << 20, transcendentals=0),
        name="spread",
    )(place, rows)


def gather_tokens(own, z):
    ahead = [(i, (i + 1) % N_Z) for i in range(N_Z)]
    behind = [(i, (i - 1) % N_Z) for i in range(N_Z)]
    tokens = jnp.zeros((N_Z * TOK, D), BF)
    tokens = lax.dynamic_update_slice(tokens, own, (z * TOK, 0))
    right = left = own
    half = TOK // 2
    for step in range(1, N_Z // 2):
        right = lax.ppermute(right, "z", ahead)
        left = lax.ppermute(left, "z", behind)
        tokens = lax.dynamic_update_slice(tokens, right, (lax.rem(z - step + N_Z, N_Z) * TOK, 0))
        tokens = lax.dynamic_update_slice(tokens, left, (lax.rem(z + step, N_Z) * TOK, 0))
    at = lax.rem(z + N_Z // 2, N_Z) * TOK
    tokens = lax.dynamic_update_slice(tokens, lax.ppermute(right[:half], "z", ahead), (at, 0))
    return lax.dynamic_update_slice(tokens, lax.ppermute(left[half:], "z", behind), (at + half, 0))


def places(expert_ids):
    ids = expert_ids
    hit = ids[:, :, None] == jnp.arange(N_X * N_Z, dtype=jnp.int32)[None, None, :]
    named = jnp.any(hit, axis=1)
    earlier = jnp.tril(jnp.ones((TOK, TOK), BF), -1)
    rank = dot(earlier, named.astype(BF))
    slot = jnp.sum(jnp.where(hit, rank[:, None, :], 0.0), axis=2).astype(jnp.int32)
    place = (ids % N_Z) * (N_X * CAP) + (ids // N_Z) * CAP + slot
    return place.reshape(TOK * 8, 1)


def orthonormal(p_sum_t):
    gram = lax.dot_general(
        p_sum_t, p_sum_t, (((2,), (2,)), ((0,), (0,))), precision=lax.Precision.HIGHEST
    )
    factor = jnp.linalg.cholesky(gram)
    return lax.linalg.triangular_solve(factor, p_sum_t, left_side=True, lower=True)


def shards(grad_out, expert_ids, gates, hidden, w_down, q_start):
    x = lax.axis_index("x")
    z = lax.axis_index("z")
    plane = ("x", "y", "c")
    weights = lax.all_gather(w_down[0], plane, axis=0, tiled=True).reshape(N_X, FF, D)
    meta = jnp.concatenate([expert_ids.T.astype(F32), gates.T], axis=0)
    meta = lax.all_gather(meta, "z", axis=0)
    warm = lax.all_gather(q_start[0].T, "x", axis=0)
    stored = lax.all_to_all(hidden.reshape(N_X, N_Z * CAP, FF), "x", split_axis=0, concat_axis=0, tiled=True)
    place = places(expert_ids)
    tokens = gather_tokens(grad_out, z)
    rows = make_rows(z.reshape(1), tokens, meta)
    p_part = left_part(rows, warm, stored)
    back = back_rows(rows, weights)
    returned = lax.all_to_all(back, "z", split_axis=0, concat_axis=0, tiled=True)
    shares = lax.all_to_all(
        p_part.reshape(N_X * N_REP, RANK // N_REP, FF), plane, split_axis=0, concat_axis=0, tiled=True
    )
    p_sum = lax.all_gather(jnp.sum(shares, axis=0), plane, axis=0, tiled=True).reshape(N_X, RANK, FF)
    basis = orthonormal(p_sum)
    q_part = right_part(basis, stored, rows)
    shares = lax.all_to_all(
        q_part.reshape(N_X * N_REP, RANK // N_REP, D), plane, split_axis=0, concat_axis=0, tiled=True
    )
    q_sum = lax.all_gather(jnp.sum(shares, axis=0), ("y", "c"), axis=0, tiled=True)
    p_basis = lax.dynamic_index_in_dim(basis, x, 0, keepdims=False).T * math.sqrt(FF)
    grad_hidden = spread(place, returned.reshape(N_Z * N_X * CAP, FF))
    return (grad_hidden, p_basis[None], (q_sum.T / N_REP)[None])


def solution(mesh):
    fine = Mesh(mesh.devices.reshape(4, 2, N_X, N_Z), ("y", "c", "x", "z"))
    rep, exp = ("y", "c"), ("x", "z")
    in_specs = (
        P(rep + exp, None),
        P(rep + exp, None),
        P(rep + exp, None),
        P(rep, exp, None, None),
        P(exp, rep, None),
        P(exp, None, None),
    )
    out_specs = (P(rep + exp, None, None), P(exp, None, None), P(exp, None, None))
    return jax.shard_map(shards, mesh=fine, in_specs=in_specs, out_specs=out_specs, check_vma=False)
```

time: 571 us -> 388 us (0.68)
  waiting for transfers between devices: 422 us -> 137 us
  starting transfers between devices: 31.1 us -> 99.2 us
  blocking collectives: 0 us -> 62.6 us
  Pallas kernels: 0 us -> 29.3 us
  matrix products: 27 us -> 1.22 us
  local copies, waits for them, and re-layouts: 35.8 us -> 13.8 us
  other arithmetic: 39.1 us -> 27 us
    all_to_all x2 -> x4, waiting for transfers between devices: 273 us -> 86.2 us  [the longest x1 70.1 us: shards(): lax.all_to_all(back, 'z', split_axis=0, concat_axis=0, tiled=True)]
    psum x2 -> x0, waiting for transfers between devices: 149 us -> none  [the longest x1 75.8 us: shards(): p_sum = lax.psum(p_part, 'rep')]
    all_gather x0 -> x3, blocking collectives: none -> 62.6 us  [the longest x1 26.7 us: shards(): meta = lax.all_gather(meta, 'z', axis=0)]
    ppermute x0 -> x16, starting transfers between devices: none -> 61.2 us  [the longest x7 38.2 us: gather_tokens(): left = lax.ppermute(left, 'z', behind)]
    ppermute x0 -> x16, waiting for transfers between devices: none -> 49.7 us  [the longest x7 44.8 us: gather_tokens(): right = lax.ppermute(right, 'z', ahead)]
    pallas_call x0 -> x5, Pallas kernels: none -> 29.3 us  [the longest x1 11 us: back_rows(): pl.pallas_call(back_kernel, grid=(N_X,), in_specs=[pl.BlockSpec((1, slots...]
    dot_general x6 -> x2, matrix products: 25.8 us -> 0.67 us  [the longest x1 0.47 us: orthonormal(): lax.dot_general(p_sum_t, p_sum_t, (((2,), (2,)), ((0,), (0,))), precision...]
    reshape x4, local copies, waits for them, and re-layouts: 25.8 us -> 2.46 us  [the longest x1 1.27 us: shards(): q_part.reshape(N_X * N_REP, RANK // N_REP, D)]
  transfers between devices with their start and end apart: 5 -> 22, of which waited for: 3 -> 11; matrix products, arithmetic and copies ran while one was open for 6% -> 9% of each run, Pallas kernels for 0% -> 7%
where the time goes in v1:
time: 388 us; the launch traced here: 385 us
  waiting for transfers between devices  137 us (35%)
  starting transfers between devices  99.2 us (26%)
  blocking collectives  62.6 us (16%)
  Pallas kernels  29.3 us (8%)
  other arithmetic  27 us (7%)
  between operations  14.5 us (4%)
  local copies, waits for them, and re-layouts  13.8 us (4%)
    all_to_all x1, waiting for transfers between devices, shards(): lax.all_to_all(back, 'z', split_axis=0, concat_axis=0, tiled=True)  70.1 us
    ppermute x7, waiting for transfers between devices, gather_tokens(): right = lax.ppermute(right, 'z', ahead)  44.8 us
    ppermute x7, starting transfers between devices, gather_tokens(): left = lax.ppermute(left, 'z', behind)  38.2 us
    all_gather x1, blocking collectives, shards(): meta = lax.all_gather(meta, 'z', axis=0)  26.7 us
    all_gather x1, blocking collectives, shards(): lax.all_gather(jnp.sum(shares, axis=0), plane, axis=0, tiled=True)  22.8 us
    all_to_all x1, starting transfers between devices, shards(): lax.all_to_all(p_part.reshape(N_X * N_REP, RANK // N_REP, FF), plane, spl...  20.7 us
    ppermute x7, starting transfers between devices, gather_tokens(): right = lax.ppermute(right, 'z', ahead)  15.8 us
    all_gather x1, blocking collectives, shards(): lax.all_gather(jnp.sum(shares, axis=0), ('y', 'c'), axis=0, tiled=True)  13.1 us
  transfers between devices with their start and end apart: 22, of which 11 were waited for; matrix products, arithmetic and copies ran while one was open for 9% of the time, Pallas kernels for 7%

profile of v1, /device:TPU:1, one launch (start us, length us, event | category | flops | bytes accessed | tf_op | source)
XLA Modules:
  0.0 385.1 jit_solution(4380724707818927214)
XLA Ops:
  7.2 0.7 all-gather.10.cloned.1.call-update
  8.0 0.7 all-gather.8.cloned.1.call-update
  8.7 4.4 %collective-permute-start = (bf16[128,2048]{1,0:T(8,128)(2,1)}, bf16[128,2048]{1,0:T(8,128)(2,1)S(1)}, u32[]{:S(2)}, u32[]{:S(2)}) collective-permute-start(bf16[128,2048]{1,0:T(8,128)(2,1)} %param.6), channel_id=1, source_target_pairs={{0,1},{1,2},{2,3},{3,4},{4,5},{5,6},{6,7},{7,8},{8,9},{9,10},{10,1... | collective-permute-start | bytes 1572872 | tf_op jit(solution)/shard_map/ppermute | solution.py:212
  13.0 9.5 %collective-permute-start.1 = (bf16[128,2048]{1,0:T(8,128)(2,1)}, bf16[128,2048]{1,0:T(8,128)(2,1)S(1)}, u32[]{:S(2)}, u32[]{:S(2)}) collective-permute-start(bf16[128,2048]{1,0:T(8,128)(2,1)} %param.6), channel_id=1, source_target_pairs={{0,15},{1,0},{2,1},{3,2},{4,3},{5,4},{6,5},{7,6},{8,7},{9,8},{10,9... | collective-permute-start | bytes 1572872 | tf_op jit(solution)/shard_map/ppermute | solution.py:213
  22.5 4.0 %all-to-all-start.1 = ((bf16[4,320,768]{2,1,0:T(8,128)(2,1)}), bf16[4,320,768]{2,1,0:T(8,128)(2,1)S(1)}, u32[]{:S(2)}, u32[]{:S(2)}) async-start(bf16[4,320,768]{2,1,0:T(8,128)(2,1)} %bitcast.40), calls=%async_computation.1 | async-start | bytes 3932160 | tf_op jit(solution)/shard_map/all_to_all | solution.py:248
  26.6 5.9 %collective-permute-done = bf16[128,2048]{1,0:T(8,128)(2,1)S(1)} collective-permute-done((bf16[128,2048]{1,0:T(8,128)(2,1)}, bf16[128,2048]{1,0:T(8,128)(2,1)S(1)}, u32[]{:S(2)}, u32[]{:S(2)}) %collective-permute-start) | collective-permute-done | bytes 524320 | tf_op jit(solution)/shard_map/ppermute | solution.py:212
  32.5 1.9 collective-permute-start.2
  34.4 4.6 %collective-permute-start.3 = (bf16[128,2048]{1,0:T(8,128)(2,1)S(1)}, bf16[128,2048]{1,0:T(8,128)(2,1)S(1)}, u32[]{:S(2)}, u32[]{:S(2)}) collective-permute-start(bf16[128,2048]{1,0:T(8,128)(2,1)S(1)} %collective-permute-done.1), channel_id=1, source_target_pairs={{0,15},{1,0},{2,1},{3,2},{4,3},{5,4},{6,5},{7,6},{8,7},{9,8},{10,9... | collective-permute-start | bytes 1572872 | tf_op jit(solution)/shard_map/ppermute | solution.py:213
  39.0 0.7 fusion
  39.7 0.2 fusion.5
  39.9 0.7 select_reduce_fusion
  40.7 7.2 %collective-permute-done.2 = bf16[128,2048]{1,0:T(8,128)(2,1)S(1)} collective-permute-done((bf16[128,2048]{1,0:T(8,128)(2,1)S(1)}, bf16[128,2048]{1,0:T(8,128)(2,1)S(1)}, u32[]{:S(2)}, u32[]{:S(2)}) %collective-permute-start.2) | collective-permute-done | bytes 524320 | tf_op jit(solution)/shard_map/ppermute | solution.py:212
  47.8 1.9 collective-permute-start.4
  49.8 4.6 %collective-permute-start.5 = (bf16[128,2048]{1,0:T(8,128)(2,1)S(1)}, bf16[128,2048]{1,0:T(8,128)(2,1)S(1)}, u32[]{:S(2)}, u32[]{:S(2)}) collective-permute-start(bf16[128,2048]{1,0:T(8,128)(2,1)S(1)} %collective-permute-done.3), channel_id=1, source_target_pairs={{0,15},{1,0},{2,1},{3,2},{4,3},{5,4},{6,5},{7,6},{8,7},{9,8},{10,9... | collective-permute-start | bytes 1572872 | tf_op jit(solution)/shard_map/ppermute | solution.py:213
  54.4 0.8 convert_bitcast_fusion
  55.1 0.7 pad_maximum_fusion
  55.8 26.7 %all-gather = f32[256,128]{1,0:T(8,128)S(1)} all-gather(f32[16,128]{1,0:T(8,128)S(1)} %pad_maximum_fusion), channel_id=2, replica_groups=mesh['y'=4,'c'=2,'x'=4,'z'=16] {'z'}, dimensions={0}, use_global_device_ids=true | all-gather | bytes 139264 | tf_op jit(solution)/shard_map/all_gather | solution.py:246
  82.5 1.1 broadcast_in_dim.39
  83.6 1.9 collective-permute-start.6
  85.6 4.6 %collective-permute-start.7 = (bf16[128,2048]{1,0:T(8,128)(2,1)S(1)}, bf16[128,2048]{1,0:T(8,128)(2,1)S(1)}, u32[]{:S(2)}, u32[]{:S(2)}) collective-permute-start(bf16[128,2048]{1,0:T(8,128)(2,1)S(1)} %collective-permute-done.5), channel_id=1, source_target_pairs={{0,15},{1,0},{2,1},{3,2},{4,3},{5,4},{6,5},{7,6},{8,7},{9,8},{10,9... | collective-permute-start | bytes 1572872 | tf_op jit(solution)/shard_map/ppermute | solution.py:213
  90.3 4.5 %collective-permute-done.6 = bf16[128,2048]{1,0:T(8,128)(2,1)S(1)} collective-permute-done((bf16[128,2048]{1,0:T(8,128)(2,1)S(1)}, bf16[128,2048]{1,0:T(8,128)(2,1)S(1)}, u32[]{:S(2)}, u32[]{:S(2)}) %collective-permute-start.6) | collective-permute-done | bytes 524320 | tf_op jit(solution)/shard_map/ppermute | solution.py:212
  94.9 1.9 collective-permute-start.8
  96.8 4.6 %collective-permute-start.9 = (bf16[128,2048]{1,0:T(8,128)(2,1)S(1)}, bf16[128,2048]{1,0:T(8,128)(2,1)S(1)}, u32[]{:S(2)}, u32[]{:S(2)}) collective-permute-start(bf16[128,2048]{1,0:T(8,128)(2,1)S(1)} %collective-permute-done.7), channel_id=1, source_target_pairs={{0,15},{1,0},{2,1},{3,2},{4,3},{5,4},{6,5},{7,6},{8,7},{9,8},{10,9... | collective-permute-start | bytes 1572872 | tf_op jit(solution)/shard_map/ppermute | solution.py:213
  101.5 8.5 %collective-permute-done.8 = bf16[128,2048]{1,0:T(8,128)(2,1)S(1)} collective-permute-done((bf16[128,2048]{1,0:T(8,128)(2,1)S(1)}, bf16[128,2048]{1,0:T(8,128)(2,1)S(1)}, u32[]{:S(2)}, u32[]{:S(2)}) %collective-permute-start.8) | collective-permute-done | bytes 524320 | tf_op jit(solution)/shard_map/ppermute | solution.py:212
  110.0 1.9 collective-permute-start.10
  111.9 5.3 %collective-permute-start.11 = (bf16[128,2048]{1,0:T(8,128)(2,1)S(1)}, bf16[128,2048]{1,0:T(8,128)(2,1)S(1)}, u32[]{:S(2)}, u32[]{:S(2)}) collective-permute-start(bf16[128,2048]{1,0:T(8,128)(2,1)S(1)} %collective-permute-done.9), channel_id=1, source_target_pairs={{0,15},{1,0},{2,1},{3,2},{4,3},{5,4},{6,5},{7,6},{8,7},{9,8},{10,9... | collective-permute-start | bytes 1572872 | tf_op jit(solution)/shard_map/ppermute | solution.py:213
  117.4 9.3 %collective-permute-done.10 = bf16[128,2048]{1,0:T(8,128)(2,1)S(1)} collective-permute-done((bf16[128,2048]{1,0:T(8,128)(2,1)S(1)}, bf16[128,2048]{1,0:T(8,128)(2,1)S(1)}, u32[]{:S(2)}, u32[]{:S(2)}) %collective-permute-start.10) | collective-permute-done | bytes 524320 | tf_op jit(solution)/shard_map/ppermute | solution.py:212
  126.7 1.9 collective-permute-start.12
  128.6 5.2 %collective-permute-start.13 = (bf16[128,2048]{1,0:T(8,128)(2,1)S(1)}, bf16[128,2048]{1,0:T(8,128)(2,1)S(1)}, u32[]{:S(2)}, u32[]{:S(2)}) collective-permute-start(bf16[128,2048]{1,0:T(8,128)(2,1)S(1)} %collective-permute-done.11), channel_id=1, source_target_pairs={{0,15},{1,0},{2,1},{3,2},{4,3},{5,4},{6,5},{7,6},{8,7},{9,8},{10,9... | collective-permute-start | bytes 1572872 | tf_op jit(solution)/shard_map/ppermute | solution.py:213
  133.9 9.4 %collective-permute-done.12 = bf16[128,2048]{1,0:T(8,128)(2,1)S(1)} collective-permute-done((bf16[128,2048]{1,0:T(8,128)(2,1)S(1)}, bf16[128,2048]{1,0:T(8,128)(2,1)S(1)}, u32[]{:S(2)}, u32[]{:S(2)}) %collective-permute-start.12) | collective-permute-done | bytes 524320 | tf_op jit(solution)/shard_map/ppermute | solution.py:212
  143.4 1.9 collective-permute-start.14
  145.4 5.2 %collective-permute-start.15 = (bf16[64,2048]{1,0:T(8,128)(2,1)S(1)}, bf16[64,2048]{1,0:T(8,128)(2,1)S(1)}, u32[]{:S(2)}, u32[]{:S(2)}) collective-permute-start(bf16[64,2048]{1,0:T(8,128)(2,1)S(1)} %slice.19), channel_id=1, source_target_pairs={{0,15},{1,0},{2,1},{3,2},{4,3},{5,4},{6,5},{7,6},{8,7},{9,8},{10,9... | collective-permute-start | bytes 786440 | tf_op jit(solution)/shard_map/ppermute | solution.py:218
  150.7 2.9 collective-permute-done.14
  153.7 2.0 collective-permute-done.15
  155.7 7.4 %rows.1.rows_ref = bf16[4,320,2048]{2,1,0:T(8,128)(2,1)S(1)} custom-call(s32[1]{0:T(128)} %bitcast.z_ref, bf16[2048,2048]{1,0:T(8,128)(2,1)S(1)} %constant_dynamic-update-slice_fusion.tokens_ref, f32[16,16,128]{2,1,0:T(8,128)S(1)} %bitcast.38), custom_call_target="tpu_custom_call" | custom-call | flops 3000000000 | bytes 14680064 | tf_op jit(solution)/shard_map/rows/pallas_call | solution.py:77
  163.1 2.3 copy-done
  165.4 2.5 copy-done.1
  167.9 1.2 copy-done.3
  169.1 3.8 left.1
  172.9 0.9 reshape.49
  173.8 20.7 %all-to-all-start.2 = ((f32[32,4,768]{2,1,0:T(4,128)}), f32[32,4,768]{2,1,0:T(4,128)S(1)}, u32[]{:S(2)}, u32[]{:S(2)}) async-start(f32[32,4,768]{2,1,0:T(4,128)} %reshape.49), calls=%async_computation.2 | async-start | bytes 786432 | tf_op jit(solution)/shard_map/all_to_all | solution.py:255
  194.5 10.3 %all-to-all-done.2 = f32[32,4,768]{2,1,0:T(4,128)S(1)} async-done(((f32[32,4,768]{2,1,0:T(4,128)}), f32[32,4,768]{2,1,0:T(4,128)S(1)}, u32[]{:S(2)}, u32[]{:S(2)}) %all-to-all-start.2) | async-done | bytes 393248 | tf_op jit(solution)/shard_map/all_to_all | solution.py:255
  204.8 22.8 %all-gather.3 = f32[32,4,768]{2,1,0:T(4,128)S(1)} all-gather(f32[1,4,768]{2,1,0:T(4,128)S(1)} %bitcast.44), channel_id=1, replica_groups=mesh['y'=4,'c'=2,'x'=4,'z'=16] {'x','y','c'}, dimensions={0}, use_global_device_ids=true | all-gather | bytes 405504 | tf_op jit(solution)/shard_map/all_gather | solution.py:258
  227.7 0.1 reshape.50
  227.8 0.5 fusion.20
  228.4 11.7 %custom-call.7 = f32[4,32,32]{2,1,0:T(8,128)S(1)} custom-call(f32[4,32,32]{2,1,0:T(8,128)S(1)} %fusion.3), custom_call_target="Cholesky" | custom-call | tf_op jit(solution)/shard_map/jit(cholesky)/cholesky | solution.py:236
  240.2 0.1 compare_reduce_fusion
  240.4 9.8 %custom-call.8 = f32[4,1,32,32]{2,3,1,0:T(8,128)S(1)} custom-call(f32[4,1,32,32]{3,2,1,0:T(8,128)S(1)} %select_bitcast_fusion), custom_call_target="InvertDiagBlocksLowerTriangular" | custom-call | tf_op jit(solution)/shard_map/triangular_solve | solution.py:237
  250.2 0.5 fusion.1.basis_ref
  250.8 2.5 copy-done.2
  253.3 3.2 right.1
  256.5 1.3 reshape.51
  257.8 4.5 %all-to-all-start.3 = ((f32[32,4,2048]{2,1,0:T(4,128)}), f32[32,4,2048]{2,1,0:T(4,128)S(1)}, u32[]{:S(2)}, u32[]{:S(2)}) async-start(f32[32,4,2048]{2,1,0:T(4,128)} %reshape.51), calls=%async_computation.3 | async-start | bytes 2097152 | tf_op jit(solution)/shard_map/all_to_all | solution.py:261
  262.3 11.0 %back.1 = bf16[16,80,768]{2,1,0:T(8,128)(2,1)} custom-call(bf16[4,320,2048]{2,1,0:T(8,128)(2,1)} %copy-done, bf16[4,768,2048]{2,1,0:T(8,128)(2,1)} %bitcast.39), custom_call_target="tpu_custom_call" | custom-call | flops 5000000000 | bytes 20971520 | tf_op jit(solution)/shard_map/back/pallas_call | solution.py:140
  273.3 5.8 %all-to-all-done.3 = f32[32,4,2048]{2,1,0:T(4,128)S(1)} async-done(((f32[32,4,2048]{2,1,0:T(4,128)}), f32[32,4,2048]{2,1,0:T(4,128)S(1)}, u32[]{:S(2)}, u32[]{:S(2)}) %all-to-all-start.3) | async-done | bytes 1048608 | tf_op jit(solution)/shard_map/all_to_all | solution.py:261
  279.2 8.7 %all-to-all-start = ((bf16[16,80,768]{2,1,0:T(8,128)(2,1)}), bf16[16,80,768]{2,1,0:T(8,128)(2,1)S(1)}, u32[]{:S(2)}, u32[]{:S(2)}) async-start(bf16[16,80,768]{2,1,0:T(8,128)(2,1)} %back.1), calls=%async_computation | async-start | bytes 3932160 | tf_op jit(solution)/shard_map/all_to_all | solution.py:254
  287.9 0.1 copy.26
  288.0 0.2 reshape.63.place_ref
  288.2 0.7 multiply_bitcast_fusion
  288.9 1.4 reduce_sum.29
  290.3 13.1 %all-gather.4 = f32[8,4,2048]{2,1,0:T(4,128)S(1)} all-gather(f32[1,4,2048]{2,1,0:T(4,128)S(1)} %bitcast.43), channel_id=1, replica_groups=mesh['y'=4,'c'=2,'x'=4,'z'=16] {'y','c'}, dimensions={0}, use_global_device_ids=true | all-gather | bytes 294912 | tf_op jit(solution)/shard_map/all_gather | solution.py:264
  303.4 0.8 reshape.61
  304.2 70.1 %all-to-all-done = bf16[16,80,768]{2,1,0:T(8,128)(2,1)S(1)} async-done(((bf16[16,80,768]{2,1,0:T(8,128)(2,1)}), bf16[16,80,768]{2,1,0:T(8,128)(2,1)S(1)}, u32[]{:S(2)}, u32[]{:S(2)}) %all-to-all-start) | async-done | bytes 1966112 | tf_op jit(solution)/shard_map/all_to_all | solution.py:254
  374.3 3.9 %spread.1 = bf16[128,8,768]{2,1,0:T(8,128)(2,1)} custom-call(s32[1024,1]{1,0:T(8,128)S(1)} %reshape.63.place_ref, bf16[1280,768]{1,0:T(8,128)(2,1)S(1)} %bitcast.36), custom_call_target="tpu_custom_call" | custom-call | flops 2000000000 | bytes 4194304 | tf_op jit(solution)/shard_map/spread/pallas_call | solution.py:189
  (49 shorter events, 1.4 us)
Async XLA Ops:
  7.2 76.4 %copy-start.5 = (bf16[128,2048]{1,0:T(8,128)(2,1)S(1)}, bf16[128,2048]{1,0:T(8,128)(2,1)}, u32[]{:S(2)}) copy-start(bf16[128,2048]{1,0:T(8,128)(2,1)} %param.6) | copy-start | bytes 1572868
  7.2 158.2 %all-gather.10.cloned.1.call-start = ((), (), s32[]{:S(2)}) async-start(), calls=%async_computation.5 | async-start | bytes 1310720 | tf_op jit(solution)/shard_map/all_gather | solution.py:247
  7.9 254.4 %all-gather.8.cloned.1.call-start = ((), (), s32[]{:S(2)}) async-start(), calls=%async_computation.4 | async-start | bytes 12976128 | tf_op jit(solution)/shard_map/all_gather | solution.py:244
  8.7 23.8 %collective-permute-start = (bf16[128,2048]{1,0:T(8,128)(2,1)}, bf16[128,2048]{1,0:T(8,128)(2,1)S(1)}, u32[]{:S(2)}, u32[]{:S(2)}) collective-permute-start(bf16[128,2048]{1,0:T(8,128)(2,1)} %param.6), channel_id=1, source_target_pairs={{0,1},{1,2},{2,3},{3,4},{4,5},{5,6},{6,7},{7,8},{8,9},{9,10},{10,1... | collective-permute-start | bytes 1572872 | tf_op jit(solution)/shard_map/ppermute | solution.py:212
  13.0 21.3 %collective-permute-start.1 = (bf16[128,2048]{1,0:T(8,128)(2,1)}, bf16[128,2048]{1,0:T(8,128)(2,1)S(1)}, u32[]{:S(2)}, u32[]{:S(2)}) collective-permute-start(bf16[128,2048]{1,0:T(8,128)(2,1)} %param.6), channel_id=1, source_target_pairs={{0,15},{1,0},{2,1},{3,2},{4,3},{5,4},{6,5},{7,6},{8,7},{9,8},{10,9... | collective-permute-start | bytes 1572872 | tf_op jit(solution)/shard_map/ppermute | solution.py:213
  22.5 142.8 %all-to-all-start.1 = ((bf16[4,320,768]{2,1,0:T(8,128)(2,1)}), bf16[4,320,768]{2,1,0:T(8,128)(2,1)S(1)}, u32[]{:S(2)}, u32[]{:S(2)}) async-start(bf16[4,320,768]{2,1,0:T(8,128)(2,1)} %bitcast.40), calls=%async_computation.1 | async-start | bytes 3932160 | tf_op jit(solution)/shard_map/all_to_all | solution.py:248
  32.5 15.4 %collective-permute-start.2 = (bf16[128,2048]{1,0:T(8,128)(2,1)S(1)}, bf16[128,2048]{1,0:T(8,128)(2,1)S(1)}, u32[]{:S(2)}, u32[]{:S(2)}) collective-permute-start(bf16[128,2048]{1,0:T(8,128)(2,1)S(1)} %collective-permute-done), channel_id=1, source_target_pairs={{0,1},{1,2},{2,3},{3,4},{4,5},{5,6},{6,7},{7,8},{8,9},{9,10},{10,1... | collective-permute-start | bytes 1572872 | tf_op jit(solution)/shard_map/ppermute | solution.py:212
  34.4 15.4 %collective-permute-start.3 = (bf16[128,2048]{1,0:T(8,128)(2,1)S(1)}, bf16[128,2048]{1,0:T(8,128)(2,1)S(1)}, u32[]{:S(2)}, u32[]{:S(2)}) collective-permute-start(bf16[128,2048]{1,0:T(8,128)(2,1)S(1)} %collective-permute-done.1), channel_id=1, source_target_pairs={{0,15},{1,0},{2,1},{3,2},{4,3},{5,4},{6,5},{7,6},{8,7},{9,8},{10,9... | collective-permute-start | bytes 1572872 | tf_op jit(solution)/shard_map/ppermute | solution.py:213
  47.8 35.8 %collective-permute-start.4 = (bf16[128,2048]{1,0:T(8,128)(2,1)S(1)}, bf16[128,2048]{1,0:T(8,128)(2,1)S(1)}, u32[]{:S(2)}, u32[]{:S(2)}) collective-permute-start(bf16[128,2048]{1,0:T(8,128)(2,1)S(1)} %collective-permute-done.2), channel_id=1, source_target_pairs={{0,1},{1,2},{2,3},{3,4},{4,5},{5,6},{6,7},{7,8},{8,9},{9,10},{10,1... | collective-permute-start | bytes 1572872 | tf_op jit(solution)/shard_map/ppermute | solution.py:212
  49.8 35.8 %collective-permute-start.5 = (bf16[128,2048]{1,0:T(8,128)(2,1)S(1)}, bf16[128,2048]{1,0:T(8,128)(2,1)S(1)}, u32[]{:S(2)}, u32[]{:S(2)}) collective-permute-start(bf16[128,2048]{1,0:T(8,128)(2,1)S(1)} %collective-permute-done.3), channel_id=1, source_target_pairs={{0,15},{1,0},{2,1},{3,2},{4,3},{5,4},{6,5},{7,6},{8,7},{9,8},{10,9... | collective-permute-start | bytes 1572872 | tf_op jit(solution)/shard_map/ppermute | solution.py:213
  83.6 11.2 %collective-permute-start.6 = (bf16[128,2048]{1,0:T(8,128)(2,1)S(1)}, bf16[128,2048]{1,0:T(8,128)(2,1)S(1)}, u32[]{:S(2)}, u32[]{:S(2)}) collective-permute-start(bf16[128,2048]{1,0:T(8,128)(2,1)S(1)} %collective-permute-done.4), channel_id=1, source_target_pairs={{0,1},{1,2},{2,3},{3,4},{4,5},{5,6},{6,7},{7,8},{8,9},{9,10},{10,1... | collective-permute-start | bytes 1572872 | tf_op jit(solution)/shard_map/ppermute | solution.py:212
  85.6 11.2 %collective-permute-start.7 = (bf16[128,2048]{1,0:T(8,128)(2,1)S(1)}, bf16[128,2048]{1,0:T(8,128)(2,1)S(1)}, u32[]{:S(2)}, u32[]{:S(2)}) collective-permute-start(bf16[128,2048]{1,0:T(8,128)(2,1)S(1)} %collective-permute-done.5), channel_id=1, source_target_pairs={{0,15},{1,0},{2,1},{3,2},{4,3},{5,4},{6,5},{7,6},{8,7},{9,8},{10,9... | collective-permute-start | bytes 1572872 | tf_op jit(solution)/shard_map/ppermute | solution.py:213
  94.9 15.2 %collective-permute-start.8 = (bf16[128,2048]{1,0:T(8,128)(2,1)S(1)}, bf16[128,2048]{1,0:T(8,128)(2,1)S(1)}, u32[]{:S(2)}, u32[]{:S(2)}) collective-permute-start(bf16[128,2048]{1,0:T(8,128)(2,1)S(1)} %collective-permute-done.6), channel_id=1, source_target_pairs={{0,1},{1,2},{2,3},{3,4},{4,5},{5,6},{6,7},{7,8},{8,9},{9,10},{10,1... | collective-permute-start | bytes 1572872 | tf_op jit(solution)/shard_map/ppermute | solution.py:212
  96.8 15.2 %collective-permute-start.9 = (bf16[128,2048]{1,0:T(8,128)(2,1)S(1)}, bf16[128,2048]{1,0:T(8,128)(2,1)S(1)}, u32[]{:S(2)}, u32[]{:S(2)}) collective-permute-start(bf16[128,2048]{1,0:T(8,128)(2,1)S(1)} %collective-permute-done.7), channel_id=1, source_target_pairs={{0,15},{1,0},{2,1},{3,2},{4,3},{5,4},{6,5},{7,6},{8,7},{9,8},{10,9... | collective-permute-start | bytes 1572872 | tf_op jit(solution)/shard_map/ppermute | solution.py:213
  110.0 16.6 %collective-permute-start.10 = (bf16[128,2048]{1,0:T(8,128)(2,1)S(1)}, bf16[128,2048]{1,0:T(8,128)(2,1)S(1)}, u32[]{:S(2)}, u32[]{:S(2)}) collective-permute-start(bf16[128,2048]{1,0:T(8,128)(2,1)S(1)} %collective-permute-done.8), channel_id=1, source_target_pairs={{0,1},{1,2},{2,3},{3,4},{4,5},{5,6},{6,7},{7,8},{8,9},{9,10},{10,1... | collective-permute-start | bytes 1572872 | tf_op jit(solution)/shard_map/ppermute | solution.py:212
  111.9 16.6 %collective-permute-start.11 = (bf16[128,2048]{1,0:T(8,128)(2,1)S(1)}, bf16[128,2048]{1,0:T(8,128)(2,1)S(1)}, u32[]{:S(2)}, u32[]{:S(2)}) collective-permute-start(bf16[128,2048]{1,0:T(8,128)(2,1)S(1)} %collective-permute-done.9), channel_id=1, source_target_pairs={{0,15},{1,0},{2,1},{3,2},{4,3},{5,4},{6,5},{7,6},{8,7},{9,8},{10,9... | collective-permute-start | bytes 1572872 | tf_op jit(solution)/shard_map/ppermute | solution.py:213
  126.7 16.7 %collective-permute-start.12 = (bf16[128,2048]{1,0:T(8,128)(2,1)S(1)}, bf16[128,2048]{1,0:T(8,128)(2,1)S(1)}, u32[]{:S(2)}, u32[]{:S(2)}) collective-permute-start(bf16[128,2048]{1,0:T(8,128)(2,1)S(1)} %collective-permute-done.10), channel_id=1, source_target_pairs={{0,1},{1,2},{2,3},{3,4},{4,5},{5,6},{6,7},{7,8},{8,9},{9,10},{10,1... | collective-permute-start | bytes 1572872 | tf_op jit(solution)/shard_map/ppermute | solution.py:212
  128.6 16.7 %collective-permute-start.13 = (bf16[128,2048]{1,0:T(8,128)(2,1)S(1)}, bf16[128,2048]{1,0:T(8,128)(2,1)S(1)}, u32[]{:S(2)}, u32[]{:S(2)}) collective-permute-start(bf16[128,2048]{1,0:T(8,128)(2,1)S(1)} %collective-permute-done.11), channel_id=1, source_target_pairs={{0,15},{1,0},{2,1},{3,2},{4,3},{5,4},{6,5},{7,6},{8,7},{9,8},{10,9... | collective-permute-start | bytes 1572872 | tf_op jit(solution)/shard_map/ppermute | solution.py:213
  143.4 10.3 %collective-permute-start.14 = (bf16[64,2048]{1,0:T(8,128)(2,1)S(1)}, bf16[64,2048]{1,0:T(8,128)(2,1)S(1)}, u32[]{:S(2)}, u32[]{:S(2)}) collective-permute-start(bf16[64,2048]{1,0:T(8,128)(2,1)S(1)} %slice.18), channel_id=1, source_target_pairs={{0,1},{1,2},{2,3},{3,4},{4,5},{5,6},{6,7},{7,8},{8,9},{9,10},{10,1... | collective-permute-start | bytes 786440 | tf_op jit(solution)/shard_map/ppermute | solution.py:217
  145.4 10.3 %collective-permute-start.15 = (bf16[64,2048]{1,0:T(8,128)(2,1)S(1)}, bf16[64,2048]{1,0:T(8,128)(2,1)S(1)}, u32[]{:S(2)}, u32[]{:S(2)}) collective-permute-start(bf16[64,2048]{1,0:T(8,128)(2,1)S(1)} %slice.19), channel_id=1, source_target_pairs={{0,15},{1,0},{2,1},{3,2},{4,3},{5,4},{6,5},{7,6},{8,7},{9,8},{10,9... | collective-permute-start | bytes 786440 | tf_op jit(solution)/shard_map/ppermute | solution.py:218
  163.1 2.3 copy-start
  165.4 2.5 copy-start.1
  167.9 1.2 copy-start.3
  173.8 31.0 %all-to-all-start.2 = ((f32[32,4,768]{2,1,0:T(4,128)}), f32[32,4,768]{2,1,0:T(4,128)S(1)}, u32[]{:S(2)}, u32[]{:S(2)}) async-start(f32[32,4,768]{2,1,0:T(4,128)} %reshape.49), calls=%async_computation.2 | async-start | bytes 786432 | tf_op jit(solution)/shard_map/all_to_all | solution.py:255
  250.8 2.5 copy-start.2
  257.8 21.4 %all-to-all-start.3 = ((f32[32,4,2048]{2,1,0:T(4,128)}), f32[32,4,2048]{2,1,0:T(4,128)S(1)}, u32[]{:S(2)}, u32[]{:S(2)}) async-start(f32[32,4,2048]{2,1,0:T(4,128)} %reshape.51), calls=%async_computation.3 | async-start | bytes 2097152 | tf_op jit(solution)/shard_map/all_to_all | solution.py:261
  279.2 8.7 %copy-start.4 = (f32[32,4,2048]{2,1,0:T(4,128)}, f32[32,4,2048]{2,1,0:T(4,128)S(1)}, u32[]{:S(2)}) copy-start(f32[32,4,2048]{2,1,0:T(4,128)S(1)} %all-to-all-done.3) | copy-start | bytes 3145732
  279.2 95.2 %all-to-all-start = ((bf16[16,80,768]{2,1,0:T(8,128)(2,1)}), bf16[16,80,768]{2,1,0:T(8,128)(2,1)S(1)}, u32[]{:S(2)}, u32[]{:S(2)}) async-start(bf16[16,80,768]{2,1,0:T(8,128)(2,1)} %back.1), calls=%async_computation | async-start | bytes 3932160 | tf_op jit(solution)/shard_map/all_to_all | solution.py:254
Sparse Core Ops, SparseCore 0:
  10.1 43.6 all-gather.9
  56.9 80.9 all-gather.7

commit v2 on v1

--- a/solution.py
+++ b/solution.py
@@ -9,6 +9,7 @@
 from jax.sharding import PartitionSpec as P
 
 N_X = 4
+N_Y = 4
 N_Z = 16
 N_REP = 8
 CAP = 20
@@ -16,6 +17,7 @@
 D = 2048
 FF = 768
 RANK = 32
+LIMIT = 56 << 20
 GROUP = 4
 BF = jnp.bfloat16
 F32 = jnp.float32
@@ -40,8 +42,15 @@
     return a[:n] + a[n : 2 * n] + a[2 * n :]
 
 
-def rows_kernel(z_ref, tokens_ref, meta_ref, rows_ref):
+def rows_kernel(z_ref, tokens_ref, meta_ref, warm_ref, hidden_ref, rows_ref, part_ref, warm3_ref):
     z = z_ref[0]
+
+    @pl.when(pl.program_id(0) == 0)
+    def _():
+        part_ref[...] = jnp.zeros_like(part_ref)
+        for x in range(N_X):
+            warm3_ref[x] = three(warm_ref[x])
+
     earlier = (
         lax.broadcasted_iota(jnp.int32, (TOK, TOK), 0) < lax.broadcasted_iota(jnp.int32, (TOK, TOK), 1)
     ).astype(F32).astype(BF)
@@ -71,9 +80,11 @@
         for c in range(0, D, 512):
             taken = dot(picks[x], tokens_ref[:, c : c + 512])
             rows_ref[x, :, c : c + 512] = (taken * factors[x]).astype(BF)
-
-
-def make_rows(z, tokens, meta):
+        projected = fold(dot(warm3_ref[x], rows_ref[x], NT))
+        part_ref[x] += fold(dot(three(projected), hidden_ref[x]))
+
+
+def make_rows(z, tokens, meta, warm, hidden):
     return pl.pallas_call(
         rows_kernel,
         grid_spec=pltpu.PrefetchScalarGridSpec(
@@ -82,37 +93,23 @@
             in_specs=[
                 pl.BlockSpec((GROUP * TOK, D), lambda g, s: (g, 0)),
                 pl.BlockSpec((GROUP, 16, TOK), lambda g, s: (g, 0, 0)),
+                pl.BlockSpec((N_X, RANK, D), lambda g, s: (0, 0, 0)),
+                pl.BlockSpec((N_X, GROUP * CAP, FF), lambda g, s: (0, g, 0)),
             ],
-            out_specs=pl.BlockSpec((N_X, GROUP * CAP, D), lambda g, s: (0, g, 0)),
+            out_specs=[
+                pl.BlockSpec((N_X, GROUP * CAP, D), lambda g, s: (0, g, 0)),
+                pl.BlockSpec((N_X, RANK, FF), lambda g, s: (0, 0, 0)),
+            ],
+            scratch_shapes=[pltpu.VMEM((N_X, 3 * RANK, D), BF)],
         ),
-        out_shape=jax.ShapeDtypeStruct((N_X, N_Z * CAP, D), BF),
-        compiler_params=pltpu.CompilerParams(vmem_limit_bytes=40 << 20),
+        out_shape=[
+            jax.ShapeDtypeStruct((N_X, N_Z * CAP, D), BF),
+            jax.ShapeDtypeStruct((N_X, RANK, FF), F32),
+        ],
+        compiler_params=pltpu.CompilerParams(vmem_limit_bytes=LIMIT),
         cost_estimate=pl.CostEstimate(flops=3 * 10**9, bytes_accessed=14 << 20, transcendentals=0),
         name="rows",
-    )(z, tokens, meta)
-
-
-def left_kernel(rows_ref, warm_ref, hidden_ref, part_ref):
-    projected = fold(dot(three(warm_ref[0]), rows_ref[0], NT))
-    part_ref[0] = fold(dot(three(projected), hidden_ref[0]))
-
-
-def left_part(rows, warm, hidden):
-    slots = N_Z * CAP
-    return pl.pallas_call(
-        left_kernel,
-        grid=(N_X,),
-        in_specs=[
-            pl.BlockSpec((1, slots, D), lambda x: (x, 0, 0)),
-            pl.BlockSpec((1, RANK, D), lambda x: (x, 0, 0)),
-            pl.BlockSpec((1, slots, FF), lambda x: (x, 0, 0)),
-        ],
-        out_specs=pl.BlockSpec((1, RANK, FF), lambda x: (x, 0, 0)),
-        out_shape=jax.ShapeDtypeStruct((N_X, RANK, FF), F32),
-        compiler_params=pltpu.CompilerParams(vmem_limit_bytes=40 << 20),
-        cost_estimate=pl.CostEstimate(flops=10**9, bytes_accessed=9 << 20, transcendentals=0),
-        name="left",
-    )(rows, warm, hidden)
+    )(z, tokens, meta, warm, hidden)
 
 
 def back_kernel(rows_ref, weight_ref, back_ref, held_ref):
@@ -147,7 +144,7 @@
         out_specs=pl.BlockSpec((N_Z, N_X * CAP, FF), lambda x: (0, 0, 0)),
         out_shape=jax.ShapeDtypeStruct((N_Z, N_X * CAP, FF), BF),
         scratch_shapes=[pltpu.VMEM((N_X, slots, FF), BF)],
-        compiler_params=pltpu.CompilerParams(vmem_limit_bytes=48 << 20),
+        compiler_params=pltpu.CompilerParams(vmem_limit_bytes=LIMIT),
         cost_estimate=pl.CostEstimate(flops=5 * 10**9, bytes_accessed=20 << 20, transcendentals=0),
         name="back",
     )(rows, weights)
@@ -170,7 +167,7 @@
         ],
         out_specs=pl.BlockSpec((1, RANK, D), lambda x: (x, 0, 0)),
         out_shape=jax.ShapeDtypeStruct((N_X, RANK, D), F32),
-        compiler_params=pltpu.CompilerParams(vmem_limit_bytes=40 << 20),
+        compiler_params=pltpu.CompilerParams(vmem_limit_bytes=LIMIT),
         cost_estimate=pl.CostEstimate(flops=10**9, bytes_accessed=9 << 20, transcendentals=0),
         name="right",
     )(basis, hidden, rows)
@@ -195,7 +192,7 @@
         ],
         out_specs=pl.BlockSpec((pairs // 8, 8, FF), lambda i: (i, 0, 0)),
         out_shape=jax.ShapeDtypeStruct((TOK, 8, FF), BF),
-        compiler_params=pltpu.CompilerParams(vmem_limit_bytes=40 << 20),
+        compiler_params=pltpu.CompilerParams(vmem_limit_bytes=LIMIT),
         cost_estimate=pl.CostEstimate(flops=2 * 10**9, bytes_accessed=4 << 20, transcendentals=0),
         name="spread",
     )(place, rows)
@@ -229,12 +226,44 @@
     return place.reshape(TOK * 8, 1)
 
 
-def orthonormal(p_sum_t):
-    gram = lax.dot_general(
-        p_sum_t, p_sum_t, (((2,), (2,)), ((0,), (0,))), precision=lax.Precision.HIGHEST
+def basis_kernel(sum_ref, basis_ref):
+    sums = [sum_ref[x] for x in range(N_X)]
+    exact = lax.Precision.HIGHEST
+    gram = jnp.stack(
+        [lax.dot_general(p, p, NT, precision=exact, preferred_element_type=F32) for p in sums]
     )
-    factor = jnp.linalg.cholesky(gram)
-    return lax.linalg.triangular_solve(factor, p_sum_t, left_side=True, lower=True)
+    shape = (N_X, RANK, RANK)
+    row = lax.broadcasted_iota(jnp.int32, shape, 1)
+    column = lax.broadcasted_iota(jnp.int32, shape, 2)
+    done = jnp.where(row == column, 1.0, 0.0)
+    for j in range(RANK):
+        pivot = gram[:, j : j + 1, j : j + 1]
+        below = jnp.where(row[:, :, :1] > j, gram[:, :, j : j + 1] / pivot, 0.0)
+        scale = jnp.where(row[:, :, :1] == j, lax.rsqrt(pivot), 1.0)
+        done = (done - below * done[:, j : j + 1, :]) * scale
+        gram = gram - below * gram[:, j : j + 1, :]
+    for x in range(N_X):
+        basis_ref[x] = lax.dot_general(done[x], sums[x], NN, precision=exact, preferred_element_type=F32)
+
+
+def orthonormal(p_sum):
+    return pl.pallas_call(
+        basis_kernel,
+        out_shape=jax.ShapeDtypeStruct((N_X, RANK, FF), F32),
+        compiler_params=pltpu.CompilerParams(vmem_limit_bytes=LIMIT),
+        cost_estimate=pl.CostEstimate(flops=10**7, bytes_accessed=1 << 20, transcendentals=0),
+        name="basis",
+    )(p_sum)
+
+
+def sum_right(parts, x):
+    total = lax.dynamic_index_in_dim(parts, x, 0, keepdims=False)
+    for d in (2, 1, 3):
+        piece = lax.dynamic_index_in_dim(parts, lax.rem(x + d, N_X), 0, keepdims=False)
+        total = total + lax.ppermute(piece, "x", [(i, (i + d) % N_X) for i in range(N_X)])
+    total = total + lax.ppermute(total, "c", [(0, 1), (1, 0)])
+    moved = [lax.ppermute(total, "y", [(i, (i + d) % N_Y) for i in range(N_Y)]) for d in (2, 1, 3)]
+    return total + moved[0] + (moved[1] + moved[2])
 
 
 def shards(grad_out, expert_ids, gates, hidden, w_down, q_start):
@@ -243,13 +272,14 @@
     plane = ("x", "y", "c")
     weights = lax.all_gather(w_down[0], plane, axis=0, tiled=True).reshape(N_X, FF, D)
     meta = jnp.concatenate([expert_ids.T.astype(F32), gates.T], axis=0)
-    meta = lax.all_gather(meta, "z", axis=0)
+    meta = lax.all_to_all(
+        jnp.broadcast_to(meta[None], (N_Z,) + meta.shape), "z", split_axis=0, concat_axis=0, tiled=True
+    )
     warm = lax.all_gather(q_start[0].T, "x", axis=0)
     stored = lax.all_to_all(hidden.reshape(N_X, N_Z * CAP, FF), "x", split_axis=0, concat_axis=0, tiled=True)
     place = places(expert_ids)
     tokens = gather_tokens(grad_out, z)
-    rows = make_rows(z.reshape(1), tokens, meta)
-    p_part = left_part(rows, warm, stored)
+    rows, p_part = make_rows(z.reshape(1), tokens, meta, warm, stored)
     back = back_rows(rows, weights)
     returned = lax.all_to_all(back, "z", split_axis=0, concat_axis=0, tiled=True)
     shares = lax.all_to_all(
@@ -257,18 +287,14 @@
     )
     p_sum = lax.all_gather(jnp.sum(shares, axis=0), plane, axis=0, tiled=True).reshape(N_X, RANK, FF)
     basis = orthonormal(p_sum)
-    q_part = right_part(basis, stored, rows)
-    shares = lax.all_to_all(
-        q_part.reshape(N_X * N_REP, RANK // N_REP, D), plane, split_axis=0, concat_axis=0, tiled=True
-    )
-    q_sum = lax.all_gather(jnp.sum(shares, axis=0), ("y", "c"), axis=0, tiled=True)
+    q_sum = sum_right(right_part(basis, stored, rows), x)
     p_basis = lax.dynamic_index_in_dim(basis, x, 0, keepdims=False).T * math.sqrt(FF)
     grad_hidden = spread(place, returned.reshape(N_Z * N_X * CAP, FF))
     return (grad_hidden, p_basis[None], (q_sum.T / N_REP)[None])
 
 
 def solution(mesh):
-    fine = Mesh(mesh.devices.reshape(4, 2, N_X, N_Z), ("y", "c", "x", "z"))
+    fine = Mesh(mesh.devices.reshape(N_Y, 2, N_X, N_Z), ("y", "c", "x", "z"))
     rep, exp = ("y", "c"), ("x", "z")
     in_specs = (
         P(rep + exp, None),

time: 388 us -> 302 us (0.78)
  waiting for transfers between devices: 137 us -> 56.7 us
  blocking collectives: 62.6 us -> 25.7 us
  other arithmetic: 27 us -> 6.36 us
  local copies, waits for them, and re-layouts: 13.8 us -> 31.9 us
  starting transfers between devices: 99.2 us -> 116 us
  Pallas kernels: 29.3 us -> 44.8 us
    all_to_all x1, waiting for transfers between devices: 70.1 us -> 7.05 us  [shards(): lax.all_to_all(back, 'z', split_axis=0, concat_axis=0, tiled=True)]
    all_gather x2 -> x0, blocking collectives: 39.8 us -> none  [the longest x1 26.7 us: shards(): meta = lax.all_gather(meta, 'z', axis=0)]
    ppermute x0 -> x7, starting transfers between devices: none -> 23.7 us  [the longest x3 10.7 us: sum_right(): lax.ppermute(total, 'y', [(i, (i + d) % N_Y) for i in range(N_Y)])]
    another operation x7 -> x0, other arithmetic: 21.8 us -> none  [the longest x4 11.9 us: orthonormal(): factor = jnp.linalg.cholesky(gram)]
    ppermute x7, waiting for transfers between devices: 44.8 us -> 28.2 us  [gather_tokens(): right = lax.ppermute(right, 'z', ahead)]
    ppermute x0 -> x7, waiting for transfers between devices: none -> 11.6 us  [the longest x3 6.61 us: sum_right(): lax.ppermute(piece, 'x', [(i, (i + d) % N_X) for i in range(N_X)])]
    all_to_all x1, starting transfers between devices: 20.7 us -> 9.64 us  [shards(): lax.all_to_all(p_part.reshape(N_X * N_REP, RANK // N_REP, FF), plane, spl...]
    all_to_all x1, waiting for transfers between devices: 10.3 us -> 0.01 us  [shards(): lax.all_to_all(p_part.reshape(N_X * N_REP, RANK // N_REP, FF), plane, spl...]
  transfers between devices with their start and end apart: 22 -> 29, of which waited for: 11 -> 13; matrix products, arithmetic and copies ran while one was open for 9% -> 12% of each run, Pallas kernels for 7% -> 13%
where the time goes in v2:
time: 302 us; the launch traced here: 297 us
  starting transfers between devices  116 us (38%)
  waiting for transfers between devices  56.7 us (19%)
  Pallas kernels  44.8 us (15%)
  local copies, waits for them, and re-layouts  31.9 us (11%)
  blocking collectives  25.7 us (9%)
  between operations  14.5 us (5%)
  other arithmetic  6.36 us (2%)
    ppermute x7, starting transfers between devices, gather_tokens(): left = lax.ppermute(left, 'z', behind)  35.8 us
    ppermute x7, waiting for transfers between devices, gather_tokens(): right = lax.ppermute(right, 'z', ahead)  28.2 us
    all_gather x1, blocking collectives, shards(): lax.all_gather(jnp.sum(shares, axis=0), plane, axis=0, tiled=True)  25.7 us
    ppermute x7, starting transfers between devices, gather_tokens(): right = lax.ppermute(right, 'z', ahead)  17 us
    pallas_call x1, Pallas kernels, make_rows(): pl.pallas_call(rows_kernel, grid_spec=pltpu.PrefetchScalarGridSpec(num_sc...  16.3 us
    all_to_all x1, starting transfers between devices, shards(): lax.all_to_all(back, 'z', split_axis=0, concat_axis=0, tiled=True)  12 us
    pallas_call x1, Pallas kernels, back_rows(): pl.pallas_call(back_kernel, grid=(N_X,), in_specs=[pl.BlockSpec((1, slots...  11 us
    ppermute x3, starting transfers between devices, sum_right(): lax.ppermute(total, 'y', [(i, (i + d) % N_Y) for i in range(N_Y)])  10.7 us
  transfers between devices with their start and end apart: 29, of which 13 were waited for; matrix products, arithmetic and copies ran while one was open for 12% of the time, Pallas kernels for 13%

profile of v2, /device:TPU:1, one launch (start us, length us, event | category | flops | bytes accessed | tf_op | source)
XLA Modules:
  0.0 296.6 jit_solution(604429696994115828)
XLA Ops:
  8.7 4.4 %collective-permute-start = (bf16[128,2048]{1,0:T(8,128)(2,1)}, bf16[128,2048]{1,0:T(8,128)(2,1)S(1)}, u32[]{:S(2)}, u32[]{:S(2)}) collective-permute-start(bf16[128,2048]{1,0:T(8,128)(2,1)} %param.6), channel_id=1, source_target_pairs={{0,1},{1,2},{2,3},{3,4},{4,5},{5,6},{6,7},{7,8},{8,9},{9,10},{10,1... | collective-permute-start | bytes 1572872 | tf_op jit(solution)/shard_map/ppermute | solution.py:209
  13.0 9.5 %collective-permute-start.1 = (bf16[128,2048]{1,0:T(8,128)(2,1)}, bf16[128,2048]{1,0:T(8,128)(2,1)S(1)}, u32[]{:S(2)}, u32[]{:S(2)}) collective-permute-start(bf16[128,2048]{1,0:T(8,128)(2,1)} %param.6), channel_id=1, source_target_pairs={{0,15},{1,0},{2,1},{3,2},{4,3},{5,4},{6,5},{7,6},{8,7},{9,8},{10,9... | collective-permute-start | bytes 1572872 | tf_op jit(solution)/shard_map/ppermute | solution.py:210
  22.5 9.9 %collective-permute-done = bf16[128,2048]{1,0:T(8,128)(2,1)S(1)} collective-permute-done((bf16[128,2048]{1,0:T(8,128)(2,1)}, bf16[128,2048]{1,0:T(8,128)(2,1)S(1)}, u32[]{:S(2)}, u32[]{:S(2)}) %collective-permute-start) | collective-permute-done | bytes 524320 | tf_op jit(solution)/shard_map/ppermute | solution.py:209
  32.5 1.9 collective-permute-start.2
  34.4 4.6 %collective-permute-start.3 = (bf16[128,2048]{1,0:T(8,128)(2,1)S(1)}, bf16[128,2048]{1,0:T(8,128)(2,1)S(1)}, u32[]{:S(2)}, u32[]{:S(2)}) collective-permute-start(bf16[128,2048]{1,0:T(8,128)(2,1)S(1)} %collective-permute-done.1), channel_id=1, source_target_pairs={{0,15},{1,0},{2,1},{3,2},{4,3},{5,4},{6,5},{7,6},{8,7},{9,8},{10,9... | collective-permute-start | bytes 1572872 | tf_op jit(solution)/shard_map/ppermute | solution.py:210
  40.7 7.2 %collective-permute-done.2 = bf16[128,2048]{1,0:T(8,128)(2,1)} collective-permute-done((bf16[128,2048]{1,0:T(8,128)(2,1)S(1)}, bf16[128,2048]{1,0:T(8,128)(2,1)}, u32[]{:S(2)}, u32[]{:S(2)}) %collective-permute-start.2) | collective-permute-done | bytes 524320 | tf_op jit(solution)/shard_map/ppermute | solution.py:209
  47.8 1.9 collective-permute-start.4
  49.8 4.6 %collective-permute-start.5 = (bf16[128,2048]{1,0:T(8,128)(2,1)S(1)}, bf16[128,2048]{1,0:T(8,128)(2,1)}, u32[]{:S(2)}, u32[]{:S(2)}) collective-permute-start(bf16[128,2048]{1,0:T(8,128)(2,1)S(1)} %collective-permute-done.3), channel_id=1, source_target_pairs={{0,15},{1,0},{2,1},{3,2},{4,3},{5,4},{6,5},{7,6},{8,7},{9,8},{10,9... | collective-permute-start | bytes 1572872 | tf_op jit(solution)/shard_map/ppermute | solution.py:210
  56.5 7.7 %all-to-all-start = ((f32[16,16,128]{2,1,0:T(8,128)}), f32[16,16,128]{2,1,0:T(8,128)S(1)}, u32[]{:S(2)}, u32[]{:S(2)}) async-start(f32[16,16,128]{2,1,0:T(8,128)} %broadcast_in_dim.42), calls=%async_computation | async-start | bytes 262144 | tf_op jit(solution)/shard_map/all_to_all | solution.py:275
  64.3 4.3 %broadcast_in_dim.41 = bf16[2048,2048]{1,0:T(8,128)(2,1)} broadcast(bf16[]{:T(256)} %constant.127.clone.1), dimensions={} | broadcast | bytes 8388610 | tf_op jit(solution)/shard_map/broadcast_in_dim | solution.py:204
  68.6 0.9 constant_dynamic-update-slice_fusion.16
  69.5 3.1 %collective-permute-start.6 = (bf16[128,2048]{1,0:T(8,128)(2,1)S(1)}, bf16[128,2048]{1,0:T(8,128)(2,1)S(1)}, u32[]{:S(2)}, u32[]{:S(2)}) collective-permute-start(bf16[128,2048]{1,0:T(8,128)(2,1)S(1)} %collective-permute-done.4), channel_id=1, source_target_pairs={{0,1},{1,2},{2,3},{3,4},{4,5},{5,6},{6,7},{7,8},{8,9},{9,10},{10,1... | collective-permute-start | bytes 1572872 | tf_op jit(solution)/shard_map/ppermute | solution.py:209
  72.6 3.4 %collective-permute-start.7 = (bf16[128,2048]{1,0:T(8,128)(2,1)}, bf16[128,2048]{1,0:T(8,128)(2,1)S(1)}, u32[]{:S(2)}, u32[]{:S(2)}) collective-permute-start(bf16[128,2048]{1,0:T(8,128)(2,1)} %collective-permute-done.5), channel_id=1, source_target_pairs={{0,15},{1,0},{2,1},{3,2},{4,3},{5,4},{6,5},{7,6},{8,7},{9,8},{10,9... | collective-permute-start | bytes 1572872 | tf_op jit(solution)/shard_map/ppermute | solution.py:210
  76.0 0.9 constant_dynamic-update-slice_fusion.15
  77.7 1.9 constant_dynamic-update-slice_fusion.13
  79.6 5.0 %collective-permute-done.6 = bf16[128,2048]{1,0:T(8,128)(2,1)S(1)} collective-permute-done((bf16[128,2048]{1,0:T(8,128)(2,1)S(1)}, bf16[128,2048]{1,0:T(8,128)(2,1)S(1)}, u32[]{:S(2)}, u32[]{:S(2)}) %collective-permute-start.6) | collective-permute-done | bytes 524320 | tf_op jit(solution)/shard_map/ppermute | solution.py:209
  84.6 1.9 collective-permute-start.8
  86.5 4.6 %collective-permute-start.9 = (bf16[128,2048]{1,0:T(8,128)(2,1)S(1)}, bf16[128,2048]{1,0:T(8,128)(2,1)S(1)}, u32[]{:S(2)}, u32[]{:S(2)}) collective-permute-start(bf16[128,2048]{1,0:T(8,128)(2,1)S(1)} %collective-permute-done.7), channel_id=1, source_target_pairs={{0,15},{1,0},{2,1},{3,2},{4,3},{5,4},{6,5},{7,6},{8,7},{9,8},{10,9... | collective-permute-start | bytes 1572872 | tf_op jit(solution)/shard_map/ppermute | solution.py:210
  91.1 0.8 constant_dynamic-update-slice_fusion.12
  92.7 1.9 constant_dynamic-update-slice_fusion.10
  94.6 3.0 %collective-permute-done.8 = bf16[128,2048]{1,0:T(8,128)(2,1)S(1)} collective-permute-done((bf16[128,2048]{1,0:T(8,128)(2,1)S(1)}, bf16[128,2048]{1,0:T(8,128)(2,1)S(1)}, u32[]{:S(2)}, u32[]{:S(2)}) %collective-permute-start.8) | collective-permute-done | bytes 524320 | tf_op jit(solution)/shard_map/ppermute | solution.py:209
  97.6 1.9 collective-permute-start.10
  99.6 4.6 %collective-permute-start.11 = (bf16[128,2048]{1,0:T(8,128)(2,1)S(1)}, bf16[128,2048]{1,0:T(8,128)(2,1)}, u32[]{:S(2)}, u32[]{:S(2)}) collective-permute-start(bf16[128,2048]{1,0:T(8,128)(2,1)S(1)} %collective-permute-done.9), channel_id=1, source_target_pairs={{0,15},{1,0},{2,1},{3,2},{4,3},{5,4},{6,5},{7,6},{8,7},{9,8},{10,9... | collective-permute-start | bytes 1572872 | tf_op jit(solution)/shard_map/ppermute | solution.py:210
  104.1 0.9 constant_dynamic-update-slice_fusion.9
  105.0 0.8 constant_dynamic-update-slice_fusion.8
  105.9 0.8 constant_dynamic-update-slice_fusion.7
  106.7 3.2 %collective-permute-done.10 = bf16[128,2048]{1,0:T(8,128)(2,1)} collective-permute-done((bf16[128,2048]{1,0:T(8,128)(2,1)S(1)}, bf16[128,2048]{1,0:T(8,128)(2,1)}, u32[]{:S(2)}, u32[]{:S(2)}) %collective-permute-start.10) | collective-permute-done | bytes 524320 | tf_op jit(solution)/shard_map/ppermute | solution.py:209
  109.9 1.9 collective-permute-start.12
  111.8 4.6 %collective-permute-start.13 = (bf16[128,2048]{1,0:T(8,128)(2,1)}, bf16[128,2048]{1,0:T(8,128)(2,1)S(1)}, u32[]{:S(2)}, u32[]{:S(2)}) collective-permute-start(bf16[128,2048]{1,0:T(8,128)(2,1)} %collective-permute-done.11), channel_id=1, source_target_pairs={{0,15},{1,0},{2,1},{3,2},{4,3},{5,4},{6,5},{7,6},{8,7},{9,8},{10,9... | collective-permute-start | bytes 1572872 | tf_op jit(solution)/shard_map/ppermute | solution.py:210
  116.4 4.0 %all-to-all-start.1 = ((bf16[4,320,768]{2,1,0:T(8,128)(2,1)}), bf16[4,320,768]{2,1,0:T(8,128)(2,1)S(1)}, u32[]{:S(2)}, u32[]{:S(2)}) async-start(bf16[4,320,768]{2,1,0:T(8,128)(2,1)} %bitcast.36), calls=%async_computation.1 | async-start | bytes 3932160 | tf_op jit(solution)/shard_map/all_to_all | solution.py:279
  120.4 1.9 constant_dynamic-update-slice_fusion.6
  122.3 1.9 constant_dynamic-update-slice_fusion.5
  124.2 1.9 constant_dynamic-update-slice_fusion.4
  126.1 1.9 collective-permute-start.14
  128.1 4.6 %collective-permute-start.15 = (bf16[64,2048]{1,0:T(8,128)(2,1)S(1)}, bf16[64,2048]{1,0:T(8,128)(2,1)S(1)}, u32[]{:S(2)}, u32[]{:S(2)}) collective-permute-start(bf16[64,2048]{1,0:T(8,128)(2,1)S(1)} %slice.9), channel_id=1, source_target_pairs={{0,15},{1,0},{2,1},{3,2},{4,3},{5,4},{6,5},{7,6},{8,7},{9,8},{10,9... | collective-permute-start | bytes 786440 | tf_op jit(solution)/shard_map/ppermute | solution.py:215
  132.7 0.9 constant_dynamic-update-slice_fusion.3
  136.7 7.5 %all-to-all-done.1.hidden_ref = bf16[4,320,768]{2,1,0:T(8,128)(2,1)S(1)} async-done(((bf16[4,320,768]{2,1,0:T(8,128)(2,1)}), bf16[4,320,768]{2,1,0:T(8,128)(2,1)S(1)}, u32[]{:S(2)}, u32[]{:S(2)}) %all-to-all-start.1) | async-done | bytes 1966112 | tf_op jit(solution)/shard_map/all_to_all | solution.py:279
  144.2 1.3 copy-done
  145.5 16.3 %rows.1 = (bf16[4,320,2048]{2,1,0:T(8,128)(2,1)}, f32[4,32,768]{2,1,0:T(8,128)}) custom-call(s32[1]{0:T(128)} %bitcast.z_ref, bf16[2048,2048]{1,0:T(8,128)(2,1)} %constant_dynamic-update-slice_fusion.tokens_ref, f32[16,16,128]{2,1,0:T(8,128)} %copy-done.2, f32[4,32,2048]{2,1,0:T(8,128)} %bitcast.38, bf16[4,320,768]{2,1,0:T(8,128)(2,1)} %copy-done), custom_call_target="tpu_custom_call" | custom-call | flops 3000000000 | bytes 14680064 | tf_op jit(solution)/shard_map/rows/pallas_call | solution.py:88
  161.8 1.9 reshape.37
  163.7 9.6 %all-to-all-start.3 = ((f32[32,4,768]{2,1,0:T(4,128)}), f32[32,4,768]{2,1,0:T(4,128)S(1)}, u32[]{:S(2)}, u32[]{:S(2)}) async-start(f32[32,4,768]{2,1,0:T(4,128)} %reshape.37), calls=%async_computation.3 | async-start | bytes 786432 | tf_op jit(solution)/shard_map/all_to_all | solution.py:285
  173.3 11.0 %back.1 = bf16[16,80,768]{2,1,0:T(8,128)(2,1)} custom-call(bf16[4,320,2048]{2,1,0:T(8,128)(2,1)} %get-tuple-element.5.rows_ref, bf16[4,768,2048]{2,1,0:T(8,128)(2,1)} %bitcast.35), custom_call_target="tpu_custom_call" | custom-call | flops 5000000000 | bytes 20971520 | tf_op jit(solution)/shard_map/back/pallas_call | solution.py:137
  184.4 12.0 %all-to-all-start.2 = ((bf16[16,80,768]{2,1,0:T(8,128)(2,1)}), bf16[16,80,768]{2,1,0:T(8,128)(2,1)S(1)}, u32[]{:S(2)}, u32[]{:S(2)}) async-start(bf16[16,80,768]{2,1,0:T(8,128)(2,1)} %back.1), calls=%async_computation.2 | async-start | bytes 3932160 | tf_op jit(solution)/shard_map/all_to_all | solution.py:284
  196.5 25.7 %all-gather.2 = f32[32,4,768]{2,1,0:T(4,128)S(1)} all-gather(f32[1,4,768]{2,1,0:T(4,128)S(1)} %bitcast.40), channel_id=1, replica_groups=mesh['y'=4,'c'=2,'x'=4,'z'=16] {'x','y','c'}, dimensions={0}, use_global_device_ids=true | all-gather | bytes 405504 | tf_op jit(solution)/shard_map/all_gather | solution.py:288
  222.2 0.9 reshape.38.sum_ref
  223.1 5.3 %basis.1.basis_ref = f32[4,32,768]{2,1,0:T(8,128)} custom-call(f32[4,32,768]{2,1,0:T(8,128)} %reshape.38.sum_ref), custom_call_target="tpu_custom_call" | custom-call | flops 10000000 | bytes 1048576 | tf_op jit(solution)/shard_map/basis/pallas_call | solution.py:250
  228.3 6.4 %right.1 = f32[4,32,2048]{2,1,0:T(8,128)} custom-call(f32[4,32,768]{2,1,0:T(8,128)} %basis.1.basis_ref, bf16[4,320,768]{2,1,0:T(8,128)(2,1)} %copy-done, bf16[4,320,2048]{2,1,0:T(8,128)(2,1)} %get-tuple-element.5.rows_ref), custom_call_target="tpu_custom_call" | custom-call | flops 1000000000 | bytes 9437184 | tf_op jit(solution)/shard_map/right/pallas_call | solution.py:160
  234.7 1.2 dynamic-slice_bitcast_fusion.2
  235.9 4.1 %collective-permute-start.16 = (f32[32,2048]{1,0:T(8,128)S(1)}, f32[32,2048]{1,0:T(8,128)S(1)}, u32[]{:S(2)}, u32[]{:S(2)}) collective-permute-start(f32[32,2048]{1,0:T(8,128)S(1)} %get-tuple-element.7), channel_id=1, source_target_pairs={{0,32},{16,48},{32,0},{48,16},{1,33},{17,49},{33,1},{49,17},{2,34}... | collective-permute-start | bytes 786440 | tf_op jit(solution)/shard_map/ppermute | solution.py:263
  240.0 2.4 collective-permute-start.17
  242.4 4.1 %collective-permute-start.18 = (f32[32,2048]{1,0:T(8,128)S(1)}, f32[32,2048]{1,0:T(8,128)S(1)}, u32[]{:S(2)}, u32[]{:S(2)}) collective-permute-start(f32[32,2048]{1,0:T(8,128)S(1)} %get-tuple-element.8), channel_id=1, source_target_pairs={{0,48},{16,0},{32,16},{48,32},{1,49},{17,1},{33,17},{49,33},{2,50}... | collective-permute-start | bytes 786440 | tf_op jit(solution)/shard_map/ppermute | solution.py:263
  247.0 6.1 %collective-permute-done.17 = f32[32,2048]{1,0:T(8,128)S(1)} collective-permute-done((f32[32,2048]{1,0:T(8,128)S(1)}, f32[32,2048]{1,0:T(8,128)S(1)}, u32[]{:S(2)}, u32[]{:S(2)}) %collective-permute-start.17) | collective-permute-done | bytes 262176 | tf_op jit(solution)/shard_map/ppermute | solution.py:263
  253.1 1.0 fusion.1
  254.1 2.4 collective-permute-start.19
  256.5 1.1 collective-permute-done.19
  257.7 4.2 %collective-permute-start.20 = (f32[32,2048]{1,0:T(8,128)S(1)}, f32[32,2048]{1,0:T(8,128)S(1)}, u32[]{:S(2)}, u32[]{:S(2)}) collective-permute-start(f32[32,2048]{1,0:T(8,128)S(1)} %add.237), channel_id=1, source_target_pairs={{0,256},{128,384},{256,0},{384,128},{1,257},{129,385},{257,1},{385... | collective-permute-start | bytes 786440 | tf_op jit(solution)/shard_map/ppermute | solution.py:265
  261.9 2.3 collective-permute-start.21
  264.2 4.2 %collective-permute-start.22 = (f32[32,2048]{1,0:T(8,128)S(1)}, f32[32,2048]{1,0:T(8,128)S(1)}, u32[]{:S(2)}, u32[]{:S(2)}) collective-permute-start(f32[32,2048]{1,0:T(8,128)S(1)} %add.237), channel_id=1, source_target_pairs={{0,384},{128,0},{256,128},{384,256},{1,385},{129,1},{257,129},{385... | collective-permute-start | bytes 786440 | tf_op jit(solution)/shard_map/ppermute | solution.py:265
  268.6 1.0 reshape.45.place_ref
  269.6 1.5 multiply_bitcast_fusion.1
  271.1 3.8 %collective-permute-done.21 = f32[32,2048]{1,0:T(8,128)S(1)} collective-permute-done((f32[32,2048]{1,0:T(8,128)S(1)}, f32[32,2048]{1,0:T(8,128)S(1)}, u32[]{:S(2)}, u32[]{:S(2)}) %collective-permute-start.21) | collective-permute-done | bytes 262176 | tf_op jit(solution)/shard_map/ppermute | solution.py:265
  275.7 7.1 %all-to-all-done.2 = bf16[16,80,768]{2,1,0:T(8,128)(2,1)S(1)} async-done(((bf16[16,80,768]{2,1,0:T(8,128)(2,1)}), bf16[16,80,768]{2,1,0:T(8,128)(2,1)S(1)}, u32[]{:S(2)}, u32[]{:S(2)}) %all-to-all-start.2) | async-done | bytes 1966112 | tf_op jit(solution)/shard_map/all_to_all | solution.py:284
  282.7 1.3 copy-done.1
  284.0 5.8 %spread.1 = bf16[128,8,768]{2,1,0:T(8,128)(2,1)} custom-call(s32[1024,1]{1,0:T(8,128)} %reshape.45.place_ref, bf16[1280,768]{1,0:T(8,128)(2,1)} %bitcast.37), custom_call_target="tpu_custom_call" | custom-call | flops 2000000000 | bytes 4194304 | tf_op jit(solution)/shard_map/spread/pallas_call | solution.py:186
  (49 shorter events, 11.7 us)
Async XLA Ops:
  7.2 61.5 %copy-start.3 = (bf16[128,2048]{1,0:T(8,128)(2,1)S(1)}, bf16[128,2048]{1,0:T(8,128)(2,1)}, u32[]{:S(2)}) copy-start(bf16[128,2048]{1,0:T(8,128)(2,1)} %param.6) | copy-start | bytes 1572868
  7.2 137.0 %all-gather.6.cloned.1.call-start = ((), (), s32[]{:S(2)}) async-start(), calls=%async_computation.4 | async-start | bytes 1310720 | tf_op jit(solution)/shard_map/all_gather | solution.py:278
  7.9 165.4 %all-gather.8.cloned.1.call-start = ((), (), s32[]{:S(2)}) async-start(), calls=%async_computation.5 | async-start | bytes 12976128 | tf_op jit(solution)/shard_map/all_gather | solution.py:273
  8.7 23.8 %collective-permute-start = (bf16[128,2048]{1,0:T(8,128)(2,1)}, bf16[128,2048]{1,0:T(8,128)(2,1)S(1)}, u32[]{:S(2)}, u32[]{:S(2)}) collective-permute-start(bf16[128,2048]{1,0:T(8,128)(2,1)} %param.6), channel_id=1, source_target_pairs={{0,1},{1,2},{2,3},{3,4},{4,5},{5,6},{6,7},{7,8},{8,9},{9,10},{10,1... | collective-permute-start | bytes 1572872 | tf_op jit(solution)/shard_map/ppermute | solution.py:209
  13.0 21.3 %collective-permute-start.1 = (bf16[128,2048]{1,0:T(8,128)(2,1)}, bf16[128,2048]{1,0:T(8,128)(2,1)S(1)}, u32[]{:S(2)}, u32[]{:S(2)}) collective-permute-start(bf16[128,2048]{1,0:T(8,128)(2,1)} %param.6), channel_id=1, source_target_pairs={{0,15},{1,0},{2,1},{3,2},{4,3},{5,4},{6,5},{7,6},{8,7},{9,8},{10,9... | collective-permute-start | bytes 1572872 | tf_op jit(solution)/shard_map/ppermute | solution.py:210
  32.5 15.4 %collective-permute-start.2 = (bf16[128,2048]{1,0:T(8,128)(2,1)S(1)}, bf16[128,2048]{1,0:T(8,128)(2,1)}, u32[]{:S(2)}, u32[]{:S(2)}) collective-permute-start(bf16[128,2048]{1,0:T(8,128)(2,1)S(1)} %collective-permute-done), channel_id=1, source_target_pairs={{0,1},{1,2},{2,3},{3,4},{4,5},{5,6},{6,7},{7,8},{8,9},{9,10},{10,1... | collective-permute-start | bytes 1572872 | tf_op jit(solution)/shard_map/ppermute | solution.py:209
  34.4 15.4 %collective-permute-start.3 = (bf16[128,2048]{1,0:T(8,128)(2,1)S(1)}, bf16[128,2048]{1,0:T(8,128)(2,1)S(1)}, u32[]{:S(2)}, u32[]{:S(2)}) collective-permute-start(bf16[128,2048]{1,0:T(8,128)(2,1)S(1)} %collective-permute-done.1), channel_id=1, source_target_pairs={{0,15},{1,0},{2,1},{3,2},{4,3},{5,4},{6,5},{7,6},{8,7},{9,8},{10,9... | collective-permute-start | bytes 1572872 | tf_op jit(solution)/shard_map/ppermute | solution.py:210
  47.8 21.7 %collective-permute-start.4 = (bf16[128,2048]{1,0:T(8,128)(2,1)}, bf16[128,2048]{1,0:T(8,128)(2,1)S(1)}, u32[]{:S(2)}, u32[]{:S(2)}) collective-permute-start(bf16[128,2048]{1,0:T(8,128)(2,1)} %collective-permute-done.2), channel_id=1, source_target_pairs={{0,1},{1,2},{2,3},{3,4},{4,5},{5,6},{6,7},{7,8},{8,9},{9,10},{10,1... | collective-permute-start | bytes 1572872 | tf_op jit(solution)/shard_map/ppermute | solution.py:209
  49.8 22.8 %collective-permute-start.5 = (bf16[128,2048]{1,0:T(8,128)(2,1)S(1)}, bf16[128,2048]{1,0:T(8,128)(2,1)}, u32[]{:S(2)}, u32[]{:S(2)}) collective-permute-start(bf16[128,2048]{1,0:T(8,128)(2,1)S(1)} %collective-permute-done.3), channel_id=1, source_target_pairs={{0,15},{1,0},{2,1},{3,2},{4,3},{5,4},{6,5},{7,6},{8,7},{9,8},{10,9... | collective-permute-start | bytes 1572872 | tf_op jit(solution)/shard_map/ppermute | solution.py:210
  56.5 59.9 %all-to-all-start = ((f32[16,16,128]{2,1,0:T(8,128)}), f32[16,16,128]{2,1,0:T(8,128)S(1)}, u32[]{:S(2)}, u32[]{:S(2)}) async-start(f32[16,16,128]{2,1,0:T(8,128)} %broadcast_in_dim.42), calls=%async_computation | async-start | bytes 262144 | tf_op jit(solution)/shard_map/all_to_all | solution.py:275
  69.5 15.0 %collective-permute-start.6 = (bf16[128,2048]{1,0:T(8,128)(2,1)S(1)}, bf16[128,2048]{1,0:T(8,128)(2,1)S(1)}, u32[]{:S(2)}, u32[]{:S(2)}) collective-permute-start(bf16[128,2048]{1,0:T(8,128)(2,1)S(1)} %collective-permute-done.4), channel_id=1, source_target_pairs={{0,1},{1,2},{2,3},{3,4},{4,5},{5,6},{6,7},{7,8},{8,9},{9,10},{10,1... | collective-permute-start | bytes 1572872 | tf_op jit(solution)/shard_map/ppermute | solution.py:209
  72.6 13.9 %collective-permute-start.7 = (bf16[128,2048]{1,0:T(8,128)(2,1)}, bf16[128,2048]{1,0:T(8,128)(2,1)S(1)}, u32[]{:S(2)}, u32[]{:S(2)}) collective-permute-start(bf16[128,2048]{1,0:T(8,128)(2,1)} %collective-permute-done.5), channel_id=1, source_target_pairs={{0,15},{1,0},{2,1},{3,2},{4,3},{5,4},{6,5},{7,6},{8,7},{9,8},{10,9... | collective-permute-start | bytes 1572872 | tf_op jit(solution)/shard_map/ppermute | solution.py:210
  84.6 13.1 %collective-permute-start.8 = (bf16[128,2048]{1,0:T(8,128)(2,1)S(1)}, bf16[128,2048]{1,0:T(8,128)(2,1)S(1)}, u32[]{:S(2)}, u32[]{:S(2)}) collective-permute-start(bf16[128,2048]{1,0:T(8,128)(2,1)S(1)} %collective-permute-done.6), channel_id=1, source_target_pairs={{0,1},{1,2},{2,3},{3,4},{4,5},{5,6},{6,7},{7,8},{8,9},{9,10},{10,1... | collective-permute-start | bytes 1572872 | tf_op jit(solution)/shard_map/ppermute | solution.py:209
  86.5 13.1 %collective-permute-start.9 = (bf16[128,2048]{1,0:T(8,128)(2,1)S(1)}, bf16[128,2048]{1,0:T(8,128)(2,1)S(1)}, u32[]{:S(2)}, u32[]{:S(2)}) collective-permute-start(bf16[128,2048]{1,0:T(8,128)(2,1)S(1)} %collective-permute-done.7), channel_id=1, source_target_pairs={{0,15},{1,0},{2,1},{3,2},{4,3},{5,4},{6,5},{7,6},{8,7},{9,8},{10,9... | collective-permute-start | bytes 1572872 | tf_op jit(solution)/shard_map/ppermute | solution.py:210
  97.6 12.3 %collective-permute-start.10 = (bf16[128,2048]{1,0:T(8,128)(2,1)S(1)}, bf16[128,2048]{1,0:T(8,128)(2,1)}, u32[]{:S(2)}, u32[]{:S(2)}) collective-permute-start(bf16[128,2048]{1,0:T(8,128)(2,1)S(1)} %collective-permute-done.8), channel_id=1, source_target_pairs={{0,1},{1,2},{2,3},{3,4},{4,5},{5,6},{6,7},{7,8},{8,9},{9,10},{10,1... | collective-permute-start | bytes 1572872 | tf_op jit(solution)/shard_map/ppermute | solution.py:209
  99.6 16.9 %copy-start.4 = (bf16[128,2048]{1,0:T(8,128)(2,1)}, bf16[128,2048]{1,0:T(8,128)(2,1)S(1)}, u32[]{:S(2)}) copy-start(bf16[128,2048]{1,0:T(8,128)(2,1)S(1)} %collective-permute-done.9) | copy-start | bytes 1572868
  99.6 12.2 %collective-permute-start.11 = (bf16[128,2048]{1,0:T(8,128)(2,1)S(1)}, bf16[128,2048]{1,0:T(8,128)(2,1)}, u32[]{:S(2)}, u32[]{:S(2)}) collective-permute-start(bf16[128,2048]{1,0:T(8,128)(2,1)S(1)} %collective-permute-done.9), channel_id=1, source_target_pairs={{0,15},{1,0},{2,1},{3,2},{4,3},{5,4},{6,5},{7,6},{8,7},{9,8},{10,9... | collective-permute-start | bytes 1572872 | tf_op jit(solution)/shard_map/ppermute | solution.py:210
  109.9 16.2 %collective-permute-start.12 = (bf16[128,2048]{1,0:T(8,128)(2,1)}, bf16[128,2048]{1,0:T(8,128)(2,1)S(1)}, u32[]{:S(2)}, u32[]{:S(2)}) collective-permute-start(bf16[128,2048]{1,0:T(8,128)(2,1)} %collective-permute-done.10), channel_id=1, source_target_pairs={{0,1},{1,2},{2,3},{3,4},{4,5},{5,6},{6,7},{7,8},{8,9},{9,10},{10,1... | collective-permute-start | bytes 1572872 | tf_op jit(solution)/shard_map/ppermute | solution.py:209
  111.8 16.3 %collective-permute-start.13 = (bf16[128,2048]{1,0:T(8,128)(2,1)}, bf16[128,2048]{1,0:T(8,128)(2,1)S(1)}, u32[]{:S(2)}, u32[]{:S(2)}) collective-permute-start(bf16[128,2048]{1,0:T(8,128)(2,1)} %collective-permute-done.11), channel_id=1, source_target_pairs={{0,15},{1,0},{2,1},{3,2},{4,3},{5,4},{6,5},{7,6},{8,7},{9,8},{10,9... | collective-permute-start | bytes 1572872 | tf_op jit(solution)/shard_map/ppermute | solution.py:210
  116.4 27.8 %copy-start.2 = (f32[16,16,128]{2,1,0:T(8,128)}, f32[16,16,128]{2,1,0:T(8,128)S(1)}, u32[]{:S(2)}) copy-start(f32[16,16,128]{2,1,0:T(8,128)S(1)} %all-to-all-done.meta_ref) | copy-start | bytes 393220
  116.4 27.8 %all-to-all-start.1 = ((bf16[4,320,768]{2,1,0:T(8,128)(2,1)}), bf16[4,320,768]{2,1,0:T(8,128)(2,1)S(1)}, u32[]{:S(2)}, u32[]{:S(2)}) async-start(bf16[4,320,768]{2,1,0:T(8,128)(2,1)} %bitcast.36), calls=%async_computation.1 | async-start | bytes 3932160 | tf_op jit(solution)/shard_map/all_to_all | solution.py:279
  126.1 8.6 %collective-permute-start.14 = (bf16[64,2048]{1,0:T(8,128)(2,1)S(1)}, bf16[64,2048]{1,0:T(8,128)(2,1)S(1)}, u32[]{:S(2)}, u32[]{:S(2)}) collective-permute-start(bf16[64,2048]{1,0:T(8,128)(2,1)S(1)} %slice.8), channel_id=1, source_target_pairs={{0,1},{1,2},{2,3},{3,4},{4,5},{5,6},{6,7},{7,8},{8,9},{9,10},{10,1... | collective-permute-start | bytes 786440 | tf_op jit(solution)/shard_map/ppermute | solution.py:214
  128.1 7.9 %collective-permute-start.15 = (bf16[64,2048]{1,0:T(8,128)(2,1)S(1)}, bf16[64,2048]{1,0:T(8,128)(2,1)S(1)}, u32[]{:S(2)}, u32[]{:S(2)}) collective-permute-start(bf16[64,2048]{1,0:T(8,128)(2,1)S(1)} %slice.9), channel_id=1, source_target_pairs={{0,15},{1,0},{2,1},{3,2},{4,3},{5,4},{6,5},{7,6},{8,7},{9,8},{10,9... | collective-permute-start | bytes 786440 | tf_op jit(solution)/shard_map/ppermute | solution.py:215
  144.2 1.3 copy-start
  163.7 20.7 %all-to-all-start.3 = ((f32[32,4,768]{2,1,0:T(4,128)}), f32[32,4,768]{2,1,0:T(4,128)S(1)}, u32[]{:S(2)}, u32[]{:S(2)}) async-start(f32[32,4,768]{2,1,0:T(4,128)} %reshape.37), calls=%async_computation.3 | async-start | bytes 786432 | tf_op jit(solution)/shard_map/all_to_all | solution.py:285
  184.4 98.4 %all-to-all-start.2 = ((bf16[16,80,768]{2,1,0:T(8,128)(2,1)}), bf16[16,80,768]{2,1,0:T(8,128)(2,1)S(1)}, u32[]{:S(2)}, u32[]{:S(2)}) async-start(bf16[16,80,768]{2,1,0:T(8,128)(2,1)} %back.1), calls=%async_computation.2 | async-start | bytes 3932160 | tf_op jit(solution)/shard_map/all_to_all | solution.py:284
  235.9 11.2 %collective-permute-start.16 = (f32[32,2048]{1,0:T(8,128)S(1)}, f32[32,2048]{1,0:T(8,128)S(1)}, u32[]{:S(2)}, u32[]{:S(2)}) collective-permute-start(f32[32,2048]{1,0:T(8,128)S(1)} %get-tuple-element.7), channel_id=1, source_target_pairs={{0,32},{16,48},{32,0},{48,16},{1,33},{17,49},{33,1},{49,17},{2,34}... | collective-permute-start | bytes 786440 | tf_op jit(solution)/shard_map/ppermute | solution.py:263
  240.0 13.1 %collective-permute-start.17 = (f32[32,2048]{1,0:T(8,128)S(1)}, f32[32,2048]{1,0:T(8,128)S(1)}, u32[]{:S(2)}, u32[]{:S(2)}) collective-permute-start(f32[32,2048]{1,0:T(8,128)S(1)} %get-tuple-element.9), channel_id=1, source_target_pairs={{0,16},{16,32},{32,48},{48,0},{1,17},{17,33},{33,49},{49,1},{2,18}... | collective-permute-start | bytes 786440 | tf_op jit(solution)/shard_map/ppermute | solution.py:263
  242.4 10.7 %collective-permute-start.18 = (f32[32,2048]{1,0:T(8,128)S(1)}, f32[32,2048]{1,0:T(8,128)S(1)}, u32[]{:S(2)}, u32[]{:S(2)}) collective-permute-start(f32[32,2048]{1,0:T(8,128)S(1)} %get-tuple-element.8), channel_id=1, source_target_pairs={{0,48},{16,0},{32,16},{48,32},{1,49},{17,1},{33,17},{49,33},{2,50}... | collective-permute-start | bytes 786440 | tf_op jit(solution)/shard_map/ppermute | solution.py:263
  254.1 3.5 %collective-permute-start.19 = (f32[32,2048]{1,0:T(8,128)S(1)}, f32[32,2048]{1,0:T(8,128)S(1)}, u32[]{:S(2)}, u32[]{:S(2)}) collective-permute-start(f32[32,2048]{1,0:T(8,128)S(1)} %fusion.1), channel_id=1, source_target_pairs={{0,64},{64,0},{1,65},{65,1},{2,66},{66,2},{3,67},{67,3},{4,68},{68... | collective-permute-start | bytes 786440 | tf_op jit(solution)/shard_map/ppermute | solution.py:264
  257.7 13.4 %collective-permute-start.20 = (f32[32,2048]{1,0:T(8,128)S(1)}, f32[32,2048]{1,0:T(8,128)S(1)}, u32[]{:S(2)}, u32[]{:S(2)}) collective-permute-start(f32[32,2048]{1,0:T(8,128)S(1)} %add.237), channel_id=1, source_target_pairs={{0,256},{128,384},{256,0},{384,128},{1,257},{129,385},{257,1},{385... | collective-permute-start | bytes 786440 | tf_op jit(solution)/shard_map/ppermute | solution.py:265
  261.9 13.0 %collective-permute-start.21 = (f32[32,2048]{1,0:T(8,128)S(1)}, f32[32,2048]{1,0:T(8,128)S(1)}, u32[]{:S(2)}, u32[]{:S(2)}) collective-permute-start(f32[32,2048]{1,0:T(8,128)S(1)} %add.237), channel_id=1, source_target_pairs={{0,128},{128,256},{256,384},{384,0},{1,129},{129,257},{257,385},{3... | collective-permute-start | bytes 786440 | tf_op jit(solution)/shard_map/ppermute | solution.py:265
  264.2 10.7 %collective-permute-start.22 = (f32[32,2048]{1,0:T(8,128)S(1)}, f32[32,2048]{1,0:T(8,128)S(1)}, u32[]{:S(2)}, u32[]{:S(2)}) collective-permute-start(f32[32,2048]{1,0:T(8,128)S(1)} %add.237), channel_id=1, source_target_pairs={{0,384},{128,0},{256,128},{384,256},{1,385},{129,1},{257,129},{385... | collective-permute-start | bytes 786440 | tf_op jit(solution)/shard_map/ppermute | solution.py:265
  282.7 1.3 copy-start.1
Sparse Core Ops, SparseCore 0:
  10.1 36.0 all-gather.5
  49.3 80.9 all-gather.7

commit v3 on v2

v3 whole, which is shorter than its diff:
```python
import math

import jax
import jax.numpy as jnp
from jax import lax
from jax.experimental import pallas as pl
from jax.experimental.pallas import tpu as pltpu
from jax.sharding import Mesh
from jax.sharding import PartitionSpec as P

N_X = 4
N_Y = 4
N_Z = 16
N_REP = 8
CAP = 20
TOK = 128
D = 2048
FF = 768
RANK = 32
LIMIT = 56 << 20
GROUP = 4
GROUPS = N_Z // GROUP
SPAN = GROUP * CAP
SLOTS = N_Z * CAP
SHARE = FF // N_REP
PAD = 16
OFFSETS = [-((j + 1) // 2) if j % 2 else j // 2 for j in range(N_Z)]
BF = jnp.bfloat16
F32 = jnp.float32
NT = (((1,), (1,)), ((), ()))
NN = (((1,), (0,)), ((), ()))


def dot(a, b, dims=NN):
    return lax.dot_general(a, b, dims, preferred_element_type=F32)


def three(a):
    high = a.astype(BF)
    rest = a - high.astype(F32)
    mid = rest.astype(BF)
    low = (rest - mid.astype(F32)).astype(BF)
    return jnp.concatenate([high, mid, low], axis=0)


def fold(a):
    n = a.shape[0] // 3
    return a[:n] + a[n : 2 * n] + a[2 * n :]


def offset(j):
    return jnp.where(j % 2 == 1, -((j + 1) // 2), j // 2)


def picks_kernel(z_ref, meta_ref, picks_ref, scale_ref, order_ref, move_ref):
    z = z_ref[0]
    earlier = (
        lax.broadcasted_iota(jnp.int32, (TOK, TOK), 0) < lax.broadcasted_iota(jnp.int32, (TOK, TOK), 1)
    ).astype(F32).astype(BF)
    slot_of = lax.broadcasted_iota(jnp.int32, (SPAN, TOK), 0).astype(F32)
    for g in range(GROUPS):
        named, gate = [], []
        for x in range(N_X):
            expert = (x * N_Z + z).astype(F32)
            for b in range(GROUP):
                at = lax.rem(z + OFFSETS[g * GROUP + b] + N_Z, N_Z)
                hit = meta_ref[at, 0:8, :] == expert
                named.append(jnp.sum(jnp.where(hit, 1.0, 0.0), axis=0, keepdims=True))
                gate.append(jnp.sum(jnp.where(hit, meta_ref[at, 8:16, :], 0.0), axis=0, keepdims=True))
        rank = dot(jnp.concatenate(named, axis=0).astype(BF), earlier)
        for x in range(N_X):
            scale = jnp.zeros((SPAN, 1), F32)
            for b in range(GROUP):
                i = x * GROUP + b
                target = jnp.where(named[i] > 0.5, rank[i : i + 1, :] + float(b * CAP), -1.0)
                hit = slot_of == target
                picks_ref[g, x * SPAN : (x + 1) * SPAN, b * TOK : (b + 1) * TOK] = jnp.where(hit, 1.0, 0.0).astype(BF)
                scale += jnp.sum(jnp.where(hit, gate[i], 0.0), axis=1, keepdims=True)
            scale_ref[g, x * SPAN : (x + 1) * SPAN, :] = jnp.broadcast_to(scale, (SPAN, 128))
    came = lax.broadcasted_iota(jnp.int32, (SLOTS, SLOTS), 0)
    own = lax.broadcasted_iota(jnp.int32, (SLOTS, SLOTS), 1)
    block = lax.rem(z + offset(came // CAP) + N_Z, N_Z)
    order_ref[...] = jnp.where(own == block * CAP + came % CAP, 1.0, 0.0).astype(BF)
    x, b, k = own // SPAN, (own % SPAN) // CAP, own % CAP
    move_ref[...] = jnp.where(came == b * (N_X * CAP) + x * CAP + k, 1.0, 0.0).astype(BF)


def make_picks(z, meta):
    slots = N_X * SPAN
    return pl.pallas_call(
        picks_kernel,
        in_specs=[pl.BlockSpec(memory_space=pltpu.SMEM), pl.BlockSpec(memory_space=pltpu.VMEM)],
        out_specs=[pl.BlockSpec(memory_space=pltpu.VMEM)] * 4,
        out_shape=[
            jax.ShapeDtypeStruct((GROUPS, slots, GROUP * TOK), BF),
            jax.ShapeDtypeStruct((GROUPS, slots, 128), F32),
            jax.ShapeDtypeStruct((SLOTS, SLOTS), BF),
            jax.ShapeDtypeStruct((SLOTS, SLOTS), BF),
        ],
        compiler_params=pltpu.CompilerParams(vmem_limit_bytes=LIMIT),
        cost_estimate=pl.CostEstimate(flops=10**7, bytes_accessed=4 << 20, transcendentals=0),
        name="picks",
    )(z, meta)


def rows_kernel(picks_ref, scale_ref, *refs):
    rows_ref = refs[-1]
    tokens = jnp.concatenate([ref[...] for ref in refs[:-1]], axis=0)
    for c in range(0, tokens.shape[1], 512):
        taken = dot(picks_ref[0], tokens[:, c : c + 512])
        for x in range(N_X):
            scale = scale_ref[0, x * SPAN : (x + 1) * SPAN, :1]
            rows_ref[x, :, c : c + 512] = (taken[x * SPAN : (x + 1) * SPAN] * scale).astype(BF)


def make_rows(group, picks, scale, blocks):
    slots = N_X * SPAN
    wide = D // 2
    return pl.pallas_call(
        rows_kernel,
        grid=(D // wide,),
        in_specs=[
            pl.BlockSpec((1, slots, GROUP * TOK), lambda i: (group, 0, 0)),
            pl.BlockSpec((1, slots, 128), lambda i: (group, 0, 0)),
        ]
        + [pl.BlockSpec((block.shape[0], wide), lambda i: (0, i)) for block in blocks],
        out_specs=pl.BlockSpec((N_X, SPAN, wide), lambda i: (0, 0, i)),
        out_shape=jax.ShapeDtypeStruct((N_X, SPAN, D), BF),
        compiler_params=pltpu.CompilerParams(vmem_limit_bytes=LIMIT),
        cost_estimate=pl.CostEstimate(flops=7 * 10**8, bytes_accessed=4 << 20, transcendentals=0),
        name="rows",
    )(picks, scale, *blocks)


def all_rows(refs):
    return jnp.concatenate([ref[0] for ref in refs], axis=0)


def unfold(a):
    a = a.reshape(N_REP, PAD, a.shape[1])
    k = RANK // N_REP
    return (a[:, :k] + a[:, k : 2 * k] + a[:, 2 * k : 3 * k]).reshape(RANK, a.shape[2])


def project_kernel(gathered_ref, order_ref, *refs):
    projected = unfold(dot(gathered_ref[0].reshape(N_REP * PAD, D), all_rows(refs[:-1]), NT))
    refs[-1][0] = dot(three(projected), order_ref[...]).astype(BF)


def project(gathered, order, rows):
    slots = len(rows) * SPAN
    return pl.pallas_call(
        project_kernel,
        grid=(N_X,),
        in_specs=[
            pl.BlockSpec((1, N_REP, PAD, D), lambda x: (x, 0, SHARE // PAD, 0)),
            pl.BlockSpec((slots, SLOTS), lambda x: (0, 0)),
        ]
        + [pl.BlockSpec((1, SPAN, D), lambda x: (x, 0, 0))] * len(rows),
        out_specs=pl.BlockSpec((1, 3 * RANK, SLOTS), lambda x: (x, 0, 0)),
        out_shape=jax.ShapeDtypeStruct((N_X, 3 * RANK, SLOTS), BF),
        compiler_params=pltpu.CompilerParams(vmem_limit_bytes=LIMIT),
        cost_estimate=pl.CostEstimate(flops=10**9, bytes_accessed=6 << 20, transcendentals=0),
        name="project",
    )(gathered, order, *rows)


def left_kernel(near_ref, gathered_ref, rows_ref, hidden_ref, order_ref, part_ref):
    projected = unfold(dot(gathered_ref[0].reshape(N_REP * PAD, D), rows_ref[0], NT))
    ordered = near_ref[0] + dot(three(projected), order_ref[...]).astype(BF)
    part_ref[...] = fold(dot(ordered, hidden_ref[0])).reshape(part_ref.shape)


def left_part(near, gathered, rows, hidden, order):
    last = GROUPS - 1
    return pl.pallas_call(
        left_kernel,
        grid=(N_X,),
        in_specs=[
            pl.BlockSpec((1, 3 * RANK, SLOTS), lambda x: (x, 0, 0)),
            pl.BlockSpec((1, N_REP, PAD, D), lambda x: (x, 0, SHARE // PAD, 0)),
            pl.BlockSpec((1, SPAN, D), lambda x: (x, 0, 0)),
            pl.BlockSpec((1, SLOTS, FF), lambda x: (x, 0, 0)),
            pl.BlockSpec((SPAN, SLOTS), lambda x: (last, 0)),
        ],
        out_specs=pl.BlockSpec((N_REP, RANK // N_REP, FF), lambda x: (x, 0, 0)),
        out_shape=jax.ShapeDtypeStruct((N_X * N_REP, RANK // N_REP, FF), F32),
        compiler_params=pltpu.CompilerParams(vmem_limit_bytes=LIMIT),
        cost_estimate=pl.CostEstimate(flops=10**9, bytes_accessed=6 << 20, transcendentals=0),
        name="left",
    )(near, gathered, rows, hidden, order)


def back_kernel(z_ref, gathered_ref, move_ref, *refs):
    back_ref, held_ref = refs[-2:]
    x = pl.program_id(0)
    z = z_ref[0]
    weight = gathered_ref[0, :, :SHARE, :].reshape(FF, D)
    rows = all_rows(refs[:-2])
    for c in range(0, FF, 256):
        held_ref[pl.ds(x, 1), :, c : c + 256] = dot(rows, weight[c : c + 256], NT).astype(BF)[None]

    @pl.when(x == N_X - 1)
    def _():
        for g in range(GROUPS):
            source = jnp.concatenate([held_ref[i, g * SPAN : (g + 1) * SPAN, :] for i in range(N_X)], axis=0)
            moved = dot(move_ref[...], source).astype(BF)
            for b in range(GROUP):
                at = lax.rem(z + OFFSETS[g * GROUP + b] + N_Z, N_Z)
                back_ref[pl.ds(at, 1)] = moved[b * N_X * CAP : (b + 1) * N_X * CAP][None]


def back_rows(z, gathered, move, rows):
    return pl.pallas_call(
        back_kernel,
        grid_spec=pltpu.PrefetchScalarGridSpec(
            num_scalar_prefetch=1,
            grid=(N_X,),
            in_specs=[
                pl.BlockSpec((1, N_REP, SHARE + PAD, D), lambda x, s: (x, 0, 0, 0)),
                pl.BlockSpec((SLOTS, SLOTS), lambda x, s: (0, 0)),
            ]
            + [pl.BlockSpec((1, SPAN, D), lambda x, s: (x, 0, 0))] * GROUPS,
            out_specs=pl.BlockSpec((N_Z, N_X * CAP, FF), lambda x, s: (0, 0, 0)),
            scratch_shapes=[pltpu.VMEM((N_X, SLOTS, FF), BF)],
        ),
        out_shape=jax.ShapeDtypeStruct((N_Z, N_X * CAP, FF), BF),
        compiler_params=pltpu.CompilerParams(vmem_limit_bytes=LIMIT),
        cost_estimate=pl.CostEstimate(flops=4 * 10**9, bytes_accessed=20 << 20, transcendentals=0),
        name="back",
    )(z, gathered, move, *rows)


def right_kernel(basis_ref, hidden_ref, order_ref, *refs):
    part_ref = refs[-1]
    mapped = fold(dot(three(basis_ref[0]), hidden_ref[0], NT))
    ordered = dot(three(mapped), order_ref[...], NT).astype(BF)
    part_ref[0] = fold(dot(ordered, all_rows(refs[:-1])))


def right_part(basis, hidden, order, rows):
    return pl.pallas_call(
        right_kernel,
        grid=(N_X,),
        in_specs=[
            pl.BlockSpec((1, RANK, FF), lambda x: (x, 0, 0)),
            pl.BlockSpec((1, SLOTS, FF), lambda x: (x, 0, 0)),
            pl.BlockSpec((SLOTS, SLOTS), lambda x: (0, 0)),
        ]
        + [pl.BlockSpec((1, SPAN, D), lambda x: (x, 0, 0))] * GROUPS,
        out_specs=pl.BlockSpec((1, RANK, D), lambda x: (x, 0, 0)),
        out_shape=jax.ShapeDtypeStruct((N_X, RANK, D), F32),
        compiler_params=pltpu.CompilerParams(vmem_limit_bytes=LIMIT),
        cost_estimate=pl.CostEstimate(flops=10**9, bytes_accessed=9 << 20, transcendentals=0),
        name="right",
    )(basis, hidden, order, *rows)


def spread_kernel(place_ref, rows_ref, out_ref):
    count = rows_ref.shape[0]
    pairs = place_ref.shape[0]
    pick = jnp.where(lax.broadcasted_iota(jnp.int32, (pairs, count), 1) == place_ref[...], 1.0, 0.0).astype(BF)
    out_ref[...] = dot(pick, rows_ref[...]).astype(BF).reshape(out_ref.shape)


def spread(place, rows):
    count = rows.shape[0]
    pairs = 256
    return pl.pallas_call(
        spread_kernel,
        grid=(TOK * 8 // pairs,),
        in_specs=[
            pl.BlockSpec((pairs, 1), lambda i: (i, 0)),
            pl.BlockSpec((count, FF), lambda i: (0, 0)),
        ],
        out_specs=pl.BlockSpec((pairs // 8, 8, FF), lambda i: (i, 0, 0)),
        out_shape=jax.ShapeDtypeStruct((TOK, 8, FF), BF),
        compiler_params=pltpu.CompilerParams(vmem_limit_bytes=LIMIT),
        cost_estimate=pl.CostEstimate(flops=2 * 10**9, bytes_accessed=4 << 20, transcendentals=0),
        name="spread",
    )(place, rows)


def turn(n, d):
    return [(i, (i + d) % n) for i in range(n)]


def places(expert_ids):
    ids = expert_ids
    hit = ids[:, :, None] == jnp.arange(N_X * N_Z, dtype=jnp.int32)[None, None, :]
    named = jnp.any(hit, axis=1)
    earlier = jnp.tril(jnp.ones((TOK, TOK), BF), -1)
    rank = dot(earlier, named.astype(BF))
    slot = jnp.sum(jnp.where(hit, rank[:, None, :], 0.0), axis=2).astype(jnp.int32)
    place = (ids % N_Z) * (N_X * CAP) + (ids // N_Z) * CAP + slot
    return place.reshape(TOK * 8, 1)


def basis_kernel(sum_ref, basis_ref):
    sums = [sum_ref[x * RANK : (x + 1) * RANK, :] for x in range(N_X)]
    exact = lax.Precision.HIGHEST
    gram = jnp.stack(
        [lax.dot_general(p, p, NT, precision=exact, preferred_element_type=F32) for p in sums]
    )
    shape = (N_X, RANK, RANK)
    row = lax.broadcasted_iota(jnp.int32, shape, 1)
    column = lax.broadcasted_iota(jnp.int32, shape, 2)
    done = jnp.where(row == column, 1.0, 0.0)
    for j in range(RANK):
        pivot = gram[:, j : j + 1, j : j + 1]
        below = jnp.where(row[:, :, :1] > j, gram[:, :, j : j + 1] / pivot, 0.0)
        scale = jnp.where(row[:, :, :1] == j, lax.rsqrt(pivot), 1.0)
        done = (done - below * done[:, j : j + 1, :]) * scale
        gram = gram - below * gram[:, j : j + 1, :]
    for x in range(N_X):
        basis_ref[x] = lax.dot_general(done[x], sums[x], NN, precision=exact, preferred_element_type=F32)


def orthonormal(p_sum):
    return pl.pallas_call(
        basis_kernel,
        out_shape=jax.ShapeDtypeStruct((N_X, RANK, FF), F32),
        compiler_params=pltpu.CompilerParams(vmem_limit_bytes=LIMIT),
        cost_estimate=pl.CostEstimate(flops=10**7, bytes_accessed=1 << 20, transcendentals=0),
        name="basis",
    )(p_sum)


def sum_right(parts, x):
    total = lax.dynamic_index_in_dim(parts, x, 0, keepdims=False)
    for d in (2, 1, 3):
        piece = lax.dynamic_index_in_dim(parts, lax.rem(x + d, N_X), 0, keepdims=False)
        total = total + lax.ppermute(piece, "x", turn(N_X, d))
    total = total + lax.ppermute(total, "c", turn(2, 1))
    moved = [lax.ppermute(total, "y", turn(N_Y, d)) for d in (2, 1, 3)]
    return total + moved[0] + (moved[1] + moved[2])


def shards(grad_out, expert_ids, gates, hidden, w_down, q_start):
    x, z = lax.axis_index("x"), lax.axis_index("z")
    plane = ("x", "y", "c")
    at = z.reshape(1)
    k = RANK // N_REP
    rep = lax.axis_index("y") * 2 + lax.axis_index("c")
    warm = three(lax.dynamic_slice(q_start[0].T, (rep * k, 0), (k, D)))
    warm = jnp.pad(warm, ((0, PAD - 3 * k), (0, 0)))
    gathered = lax.all_gather(jnp.concatenate([w_down[0], warm], axis=0), plane, axis=0, tiled=True)
    gathered = gathered.reshape(N_X, N_REP, SHARE + PAD, D)
    meta = jnp.concatenate([expert_ids.T.astype(F32), gates.T], axis=0)
    meta = lax.all_to_all(
        jnp.broadcast_to(meta[None], (N_Z,) + meta.shape), "z", split_axis=0, concat_axis=0, tiled=True
    )
    stored = lax.all_to_all(hidden.reshape(N_X, SLOTS, FF), "x", split_axis=0, concat_axis=0, tiled=True)

    blocks = [grad_out]
    right = left = grad_out
    rows = []
    for step in range(1, N_Z // 2):
        before = (right, left)
        right = lax.ppermute(right, "z", turn(N_Z, 1))
        left = lax.ppermute(left, "z", turn(N_Z, -1))
        beside = []
        if step == 1:
            beside = [meta]
        elif step == 2:
            picks, scale, order, move = make_picks(at, meta)
            beside = [picks]
        elif step == 3 or step == 5 or step == 7:
            g = len(rows)
            rows.append(make_rows(g, picks, scale, blocks[g * GROUP : (g + 1) * GROUP]))
            beside = [rows[g]]
        now = (right, left)
        right, _, *beside = lax.optimization_barrier((right, before[1], *beside))
        left, _ = lax.optimization_barrier((left, before[0]))
        if step == 1:
            meta = beside[0]
        blocks += [*now]
    half = TOK // 2
    last = blocks[12:] + [
        lax.ppermute(right[:half], "z", turn(N_Z, 1)),
        lax.ppermute(left[half:], "z", turn(N_Z, -1)),
    ]
    near = project(gathered, order, rows)
    last, near = lax.optimization_barrier((last, near))
    rows.append(make_rows(3, picks, scale, last))
    p_part = left_part(near, gathered, rows[-1], stored, order)
    back = back_rows(at, gathered, move, rows)
    returned = lax.all_to_all(back, "z", split_axis=0, concat_axis=0, tiled=True)
    shares = lax.all_to_all(p_part, plane, split_axis=0, concat_axis=0, tiled=True)
    basis = orthonormal(lax.all_gather(jnp.sum(shares, axis=0), plane, axis=0, tiled=True))
    q_sum = sum_right(right_part(basis, stored, order, rows), x)
    p_basis = lax.dynamic_index_in_dim(basis, x, 0, keepdims=False).T * math.sqrt(FF)
    place = places(expert_ids)
    grad_hidden = spread(place, returned.reshape(N_Z * N_X * CAP, FF))
    return (grad_hidden, p_basis[None], (q_sum.T / N_REP)[None])


def solution(mesh):
    fine = Mesh(mesh.devices.reshape(N_Y, 2, N_X, N_Z), ("y", "c", "x", "z"))
    rep, exp = ("y", "c"), ("x", "z")
    in_specs = (
        P(rep + exp, None),
        P(rep + exp, None),
        P(rep + exp, None),
        P(rep, exp, None, None),
        P(exp, rep, None),
        P(exp, None, None),
    )
    out_specs = (P(rep + exp, None, None), P(exp, None, None), P(exp, None, None))
    return jax.shard_map(shards, mesh=fine, in_specs=in_specs, out_specs=out_specs, check_vma=False)
```

time: 302 us -> 290 us (0.960)
  local copies, waits for them, and re-layouts: 31.9 us -> 6.53 us
  Pallas kernels: 44.8 us -> 57.6 us
  starting transfers between devices: 116 us -> 121 us
  waiting for transfers between devices: 56.7 us -> 53 us
    dynamic_update_slice x17 -> x0, local copies, waits for them, and re-layouts: 19.3 us -> none  [the longest x7 9.02 us: gather_tokens(): lax.dynamic_update_slice(tokens, left, (lax.rem(z + step, N_Z) * TOK, 0))]
    pallas_call x2 -> x8, Pallas kernels: 27.4 us -> 39.6 us  [the longest x4 13.7 us: make_rows(): pl.pallas_call(rows_kernel, grid=(D // wide,), in_specs=[pl.BlockSpec((1,...]
    all_to_all x2, waiting for transfers between devices: 7.5 us -> 0.01 us  [the longest x1 0.01 us: shards(): lax.all_to_all(hidden.reshape(N_X, SLOTS, FF), 'x', split_axis=0, concat_...]
    all_to_all x1, waiting for transfers between devices: 0.01 us -> 5.51 us  [shards(): lax.all_to_all(jnp.broadcast_to(meta[None], (N_Z,) + meta.shape), 'z', sp...]
    broadcast_in_dim x1 -> x0, local copies, waits for them, and re-layouts: 4.28 us -> none  [gather_tokens(): tokens = jnp.zeros((N_Z * TOK, D), BF)]
    all_to_all x1, starting transfers between devices: 12 us -> 15.2 us  [shards(): lax.all_to_all(back, 'z', split_axis=0, concat_axis=0, tiled=True)]
    all_to_all x2, starting transfers between devices: 13.7 us -> 16.8 us  [the longest x1 12.7 us: shards(): lax.all_to_all(p_part, plane, split_axis=0, concat_axis=0, tiled=True)]
  transfers between devices with their start and end apart: 29 -> 28, of which waited for: 13 -> 18; matrix products, arithmetic and copies ran while one was open for 12% -> 3% of each run, Pallas kernels for 13% -> 16%
where the time goes in v3:
time: 290 us; the launch traced here: 285 us
  starting transfers between devices  121 us (42%)
  Pallas kernels  57.6 us (20%)
  waiting for transfers between devices  53 us (18%)
  blocking collectives  25.7 us (9%)
  between operations  14.5 us (5%)
  local copies, waits for them, and re-layouts  6.53 us (2%)
  other arithmetic  6.33 us (2%)
    ppermute x7, starting transfers between devices, shards(): right = lax.ppermute(right, 'z', turn(N_Z, 1))  26 us
    all_gather x1, blocking collectives, shards(): lax.all_gather(jnp.sum(shares, axis=0), plane, axis=0, tiled=True)  25.7 us
    ppermute x7, starting transfers between devices, shards(): left = lax.ppermute(left, 'z', turn(N_Z, -1))  25.4 us
    ppermute x7, waiting for transfers between devices, shards(): left = lax.ppermute(left, 'z', turn(N_Z, -1))  20.6 us
    all_to_all x1, starting transfers between devices, shards(): lax.all_to_all(back, 'z', split_axis=0, concat_axis=0, tiled=True)  15.2 us
    pallas_call x4, Pallas kernels, make_rows(): pl.pallas_call(rows_kernel, grid=(D // wide,), in_specs=[pl.BlockSpec((1,...  13.7 us
    all_to_all x1, starting transfers between devices, shards(): lax.all_to_all(p_part, plane, split_axis=0, concat_axis=0, tiled=True)  12.7 us
    pallas_call x1, Pallas kernels, back_rows(): pl.pallas_call(back_kernel, grid_spec=pltpu.PrefetchScalarGridSpec(num_sc...  11.6 us
  transfers between devices with their start and end apart: 28, of which 18 were waited for; matrix products, arithmetic and copies ran while one was open for 3% of the time, Pallas kernels for 16%

profile of v3, /device:TPU:1, one launch (start us, length us, event | category | flops | bytes accessed | tf_op | source)
XLA Modules:
  0.0 284.9 jit_solution(5758845067549304416)
XLA Ops:
  7.2 0.9 subtract_convert_fusion
  8.2 1.8 pad_maximum_fusion
  10.1 4.4 %collective-permute-start = (bf16[128,2048]{1,0:T(8,128)(2,1)S(1)}, bf16[128,2048]{1,0:T(8,128)(2,1)S(1)}, u32[]{:S(2)}, u32[]{:S(2)}) collective-permute-start(bf16[128,2048]{1,0:T(8,128)(2,1)S(1)} %copy-done.5), channel_id=1, source_target_pairs={{0,1},{1,2},{2,3},{3,4},{4,5},{5,6},{6,7},{7,8},{8,9},{9,10},{10,1... | collective-permute-start | bytes 1572872 | tf_op jit(solution)/shard_map/ppermute | solution.py:360
  14.5 9.5 %collective-permute-start.1 = (bf16[128,2048]{1,0:T(8,128)(2,1)S(1)}, bf16[128,2048]{1,0:T(8,128)(2,1)S(1)}, u32[]{:S(2)}, u32[]{:S(2)}) collective-permute-start(bf16[128,2048]{1,0:T(8,128)(2,1)S(1)} %copy-done.5), channel_id=1, source_target_pairs={{0,15},{1,0},{2,1},{3,2},{4,3},{5,4},{6,5},{7,6},{8,7},{9,8},{10,9... | collective-permute-start | bytes 1572872 | tf_op jit(solution)/shard_map/ppermute | solution.py:361
  24.4 0.7 broadcast_in_dim.38
  25.0 8.4 %all-to-all-start = ((f32[16,16,128]{2,1,0:T(8,128)}), f32[16,16,128]{2,1,0:T(8,128)S(1)}, u32[]{:S(2)}, u32[]{:S(2)}) async-start(f32[16,16,128]{2,1,0:T(8,128)} %broadcast_in_dim.38), calls=%async_computation | async-start | bytes 262144 | tf_op jit(solution)/shard_map/all_to_all | solution.py:350
  33.4 1.2 collective-permute-done.1.refs_2_
  34.6 5.3 %collective-permute-start.3 = (bf16[128,2048]{1,0:T(8,128)(2,1)S(1)}, bf16[128,2048]{1,0:T(8,128)(2,1)S(1)}, u32[]{:S(2)}, u32[]{:S(2)}) collective-permute-start(bf16[128,2048]{1,0:T(8,128)(2,1)S(1)} %collective-permute-done.1.refs_2_), channel_id=1, source_target_pairs={{0,15},{1,0},{2,1},{3,2},{4,3},{5,4},{6,5},{7,6},{8,7},{9,8},{10,9... | collective-permute-start | bytes 1572872 | tf_op jit(solution)/shard_map/ppermute | solution.py:361
  39.9 5.5 %all-to-all-done.meta_ref = f32[16,16,128]{2,1,0:T(8,128)S(1)} async-done(((f32[16,16,128]{2,1,0:T(8,128)}), f32[16,16,128]{2,1,0:T(8,128)S(1)}, u32[]{:S(2)}, u32[]{:S(2)}) %all-to-all-start) | async-done | bytes 131104 | tf_op jit(solution)/shard_map/all_to_all | solution.py:350
  45.4 3.5 %collective-permute-start.2 = (bf16[128,2048]{1,0:T(8,128)(2,1)S(1)}, bf16[128,2048]{1,0:T(8,128)(2,1)S(1)}, u32[]{:S(2)}, u32[]{:S(2)}) collective-permute-start(bf16[128,2048]{1,0:T(8,128)(2,1)S(1)} %collective-permute-done.refs_1_), channel_id=1, source_target_pairs={{0,1},{1,2},{2,3},{3,4},{4,5},{5,6},{6,7},{7,8},{8,9},{9,10},{10,1... | collective-permute-start | bytes 1572872 | tf_op jit(solution)/shard_map/ppermute | solution.py:360
  48.9 2.5 collective-permute-done.3.refs_0_
  51.4 2.9 %collective-permute-start.5 = (bf16[128,2048]{1,0:T(8,128)(2,1)S(1)}, bf16[128,2048]{1,0:T(8,128)(2,1)S(1)}, u32[]{:S(2)}, u32[]{:S(2)}) collective-permute-start(bf16[128,2048]{1,0:T(8,128)(2,1)S(1)} %collective-permute-done.3.refs_0_), channel_id=1, source_target_pairs={{0,15},{1,0},{2,1},{3,2},{4,3},{5,4},{6,5},{7,6},{8,7},{9,8},{10,9... | collective-permute-start | bytes 1572872 | tf_op jit(solution)/shard_map/ppermute | solution.py:361
  54.3 3.3 %picks.1 = (bf16[4,320,512]{2,1,0:T(8,128)(2,1)}, f32[4,320,128]{2,1,0:T(8,128)}, bf16[320,320]{1,0:T(8,128)(2,1)}, bf16[320,320]{1,0:T(8,128)(2,1)}) custom-call(s32[1]{0:T(128)} %bitcast.z_ref, f32[16,16,128]{2,1,0:T(8,128)} %copy-done.4), custom_call_target="tpu_custom_call" | custom-call | flops 10000000 | bytes 4194304 | tf_op jit(solution)/shard_map/picks/pallas_call | solution.py:90
  58.3 3.1 %collective-permute-start.4 = (bf16[128,2048]{1,0:T(8,128)(2,1)S(1)}, bf16[128,2048]{1,0:T(8,128)(2,1)S(1)}, u32[]{:S(2)}, u32[]{:S(2)}) collective-permute-start(bf16[128,2048]{1,0:T(8,128)(2,1)S(1)} %collective-permute-done.2.refs_3_), channel_id=1, source_target_pairs={{0,1},{1,2},{2,3},{3,4},{4,5},{5,6},{6,7},{7,8},{8,9},{9,10},{10,1... | collective-permute-start | bytes 1572872 | tf_op jit(solution)/shard_map/ppermute | solution.py:360
  61.4 5.5 %collective-permute-done.5.refs_2_ = bf16[128,2048]{1,0:T(8,128)(2,1)S(1)} collective-permute-done((bf16[128,2048]{1,0:T(8,128)(2,1)S(1)}, bf16[128,2048]{1,0:T(8,128)(2,1)S(1)}, u32[]{:S(2)}, u32[]{:S(2)}) %collective-permute-start.5) | collective-permute-done | bytes 524320 | tf_op jit(solution)/shard_map/ppermute | solution.py:361
  66.9 1.9 collective-permute-start.7
  68.8 3.4 %rows.4.refs_0_ = bf16[4,80,2048]{2,1,0:T(8,128)(2,1)} custom-call(bf16[4,320,512]{2,1,0:T(8,128)(2,1)} %get-tuple-element.30.picks_ref, f32[4,320,128]{2,1,0:T(8,128)} %get-tuple-element.31.scale_ref, bf16[128,2048]{1,0:T(8,128)(2,1)} %refs_0_.1, bf16[128,2048]{1,0:T(8,128)(2,1)} %copy-done.7, bf16[128,2048]{1,0:T(8,128)(2,1)} %copy-done.8, ...), custom_call_target="tpu_custom_call" | custom-call | flops 700000000 | bytes 4194304 | tf_op jit(solution)/shard_map/rows/pallas_call | solution.py:119
  72.2 4.2 %collective-permute-start.6 = (bf16[128,2048]{1,0:T(8,128)(2,1)S(1)}, bf16[128,2048]{1,0:T(8,128)(2,1)}, u32[]{:S(2)}, u32[]{:S(2)}) collective-permute-start(bf16[128,2048]{1,0:T(8,128)(2,1)S(1)} %collective-permute-done.4.refs_1_), channel_id=1, source_target_pairs={{0,1},{1,2},{2,3},{3,4},{4,5},{5,6},{6,7},{7,8},{8,9},{9,10},{10,1... | collective-permute-start | bytes 1572872 | tf_op jit(solution)/shard_map/ppermute | solution.py:360
  76.4 5.4 %collective-permute-done.7.refs_0_ = bf16[128,2048]{1,0:T(8,128)(2,1)S(1)} collective-permute-done((bf16[128,2048]{1,0:T(8,128)(2,1)S(1)}, bf16[128,2048]{1,0:T(8,128)(2,1)S(1)}, u32[]{:S(2)}, u32[]{:S(2)}) %collective-permute-start.7) | collective-permute-done | bytes 524320 | tf_op jit(solution)/shard_map/ppermute | solution.py:361
  81.8 1.9 collective-permute-start.9
  83.7 2.1 collective-permute-done.6.refs_3_
  85.8 4.3 %collective-permute-start.8 = (bf16[128,2048]{1,0:T(8,128)(2,1)}, bf16[128,2048]{1,0:T(8,128)(2,1)S(1)}, u32[]{:S(2)}, u32[]{:S(2)}) collective-permute-start(bf16[128,2048]{1,0:T(8,128)(2,1)} %collective-permute-done.6.refs_3_), channel_id=1, source_target_pairs={{0,1},{1,2},{2,3},{3,4},{4,5},{5,6},{6,7},{7,8},{8,9},{9,10},{10,1... | collective-permute-start | bytes 1572872 | tf_op jit(solution)/shard_map/ppermute | solution.py:360
  90.1 4.1 %all-to-all-start.2 = ((bf16[4,320,768]{2,1,0:T(8,128)(2,1)}), bf16[4,320,768]{2,1,0:T(8,128)(2,1)S(1)}, u32[]{:S(2)}, u32[]{:S(2)}) async-start(bf16[4,320,768]{2,1,0:T(8,128)(2,1)} %bitcast.46), calls=%async_computation.2 | async-start | bytes 3932160 | tf_op jit(solution)/shard_map/all_to_all | solution.py:353
  94.2 1.7 collective-permute-done.9.refs_2_
  95.9 1.9 collective-permute-start.11
  97.8 3.5 %rows.5.refs_1_ = bf16[4,80,2048]{2,1,0:T(8,128)(2,1)} custom-call(bf16[4,320,512]{2,1,0:T(8,128)(2,1)} %get-tuple-element.30.picks_ref, f32[4,320,128]{2,1,0:T(8,128)} %get-tuple-element.31.scale_ref, bf16[128,2048]{1,0:T(8,128)(2,1)} %copy-done.6, bf16[128,2048]{1,0:T(8,128)(2,1)} %copy-done.12, bf16[128,2048]{1,0:T(8,128)(2,1)} %copy-done.10, ...), custom_call_target="tpu_custom_call" | custom-call | flops 700000000 | bytes 4194304 | tf_op jit(solution)/shard_map/rows/pallas_call | solution.py:119
  101.3 3.6 %collective-permute-start.10 = (bf16[128,2048]{1,0:T(8,128)(2,1)S(1)}, bf16[128,2048]{1,0:T(8,128)(2,1)S(1)}, u32[]{:S(2)}, u32[]{:S(2)}) collective-permute-start(bf16[128,2048]{1,0:T(8,128)(2,1)S(1)} %collective-permute-done.8.refs_1_), channel_id=1, source_target_pairs={{0,1},{1,2},{2,3},{3,4},{4,5},{5,6},{6,7},{7,8},{8,9},{9,10},{10,1... | collective-permute-start | bytes 1572872 | tf_op jit(solution)/shard_map/ppermute | solution.py:360
  104.9 4.0 %collective-permute-done.11.refs_0_ = bf16[128,2048]{1,0:T(8,128)(2,1)S(1)} collective-permute-done((bf16[128,2048]{1,0:T(8,128)(2,1)S(1)}, bf16[128,2048]{1,0:T(8,128)(2,1)S(1)}, u32[]{:S(2)}, u32[]{:S(2)}) %collective-permute-start.11) | collective-permute-done | bytes 524320 | tf_op jit(solution)/shard_map/ppermute | solution.py:361
  109.0 2.0 collective-permute-start.13
  111.0 3.4 %collective-permute-done.10.refs_3_ = bf16[128,2048]{1,0:T(8,128)(2,1)S(1)} collective-permute-done((bf16[128,2048]{1,0:T(8,128)(2,1)S(1)}, bf16[128,2048]{1,0:T(8,128)(2,1)S(1)}, u32[]{:S(2)}, u32[]{:S(2)}) %collective-permute-start.10) | collective-permute-done | bytes 524320 | tf_op jit(solution)/shard_map/ppermute | solution.py:360
  114.4 3.0 %collective-permute-start.12 = (bf16[128,2048]{1,0:T(8,128)(2,1)S(1)}, bf16[128,2048]{1,0:T(8,128)(2,1)S(1)}, u32[]{:S(2)}, u32[]{:S(2)}) collective-permute-start(bf16[128,2048]{1,0:T(8,128)(2,1)S(1)} %collective-permute-done.10.refs_3_), channel_id=1, source_target_pairs={{0,1},{1,2},{2,3},{3,4},{4,5},{5,6},{6,7},{7,8},{8,9},{9,10},{10,1... | collective-permute-start | bytes 1572872 | tf_op jit(solution)/shard_map/ppermute | solution.py:360
  117.4 3.4 %rows.6.refs_2_ = bf16[4,80,2048]{2,1,0:T(8,128)(2,1)} custom-call(bf16[4,320,512]{2,1,0:T(8,128)(2,1)} %get-tuple-element.30.picks_ref, f32[4,320,128]{2,1,0:T(8,128)} %get-tuple-element.31.scale_ref, bf16[128,2048]{1,0:T(8,128)(2,1)} %copy-done.9, bf16[128,2048]{1,0:T(8,128)(2,1)} %copy-done.14, bf16[128,2048]{1,0:T(8,128)(2,1)} %copy-done.13, ...), custom_call_target="tpu_custom_call" | custom-call | flops 700000000 | bytes 4194304 | tf_op jit(solution)/shard_map/rows/pallas_call | solution.py:119
  121.1 3.2 %collective-permute-start.15 = (bf16[64,2048]{1,0:T(8,128)(2,1)S(1)}, bf16[64,2048]{1,0:T(8,128)(2,1)}, u32[]{:S(2)}, u32[]{:S(2)}) collective-permute-start(bf16[64,2048]{1,0:T(8,128)(2,1)S(1)} %slice.7), channel_id=1, source_target_pairs={{0,15},{1,0},{2,1},{3,2},{4,3},{5,4},{6,5},{7,6},{8,7},{9,8},{10,9... | collective-permute-start | bytes 786440 | tf_op jit(solution)/shard_map/ppermute | solution.py:381
  124.3 2.2 collective-permute-done.12.refs_1_
  126.5 2.4 collective-permute-start.14
  128.9 5.6 %project.1.near_ref = bf16[4,96,320]{2,1,0:T(8,128)(2,1)} custom-call(bf16[4,8,112,2048]{3,2,1,0:T(8,128)(2,1)} %bitcast.43, bf16[320,320]{1,0:T(8,128)(2,1)} %get-tuple-element.46.order_ref, bf16[4,80,2048]{2,1,0:T(8,128)(2,1)} %rows.4.refs_0_, bf16[4,80,2048]{2,1,0:T(8,128)(2,1)} %rows.5.refs_1_, bf16[4,80,2048]{2,1,0:T(8,128)(2,1)} %rows.6.refs_2_), custom_call_target="tpu_custom_call" | custom-call | flops 1000000000 | bytes 6291456 | tf_op jit(solution)/shard_map/project/pallas_call | solution.py:152
  135.0 3.4 %rows.7.refs_3_.rows_ref = bf16[4,80,2048]{2,1,0:T(8,128)(2,1)} custom-call(bf16[4,320,512]{2,1,0:T(8,128)(2,1)} %get-tuple-element.30.picks_ref, f32[4,320,128]{2,1,0:T(8,128)} %get-tuple-element.31.scale_ref, bf16[128,2048]{1,0:T(8,128)(2,1)} %copy-done.11, bf16[128,2048]{1,0:T(8,128)(2,1)} %copy-done.3, bf16[128,2048]{1,0:T(8,128)(2,1)} %copy-done.2, ...), custom_call_target="tpu_custom_call" | custom-call | flops 700000000 | bytes 4194304 | tf_op jit(solution)/shard_map/rows/pallas_call | solution.py:119
  138.4 1.3 copy-done
  139.7 5.4 %left.1 = f32[32,4,768]{2,1,0:T(4,128)} custom-call(bf16[4,96,320]{2,1,0:T(8,128)(2,1)} %project.1.near_ref, bf16[4,8,112,2048]{3,2,1,0:T(8,128)(2,1)} %bitcast.44, bf16[4,80,2048]{2,1,0:T(8,128)(2,1)} %rows.7.refs_3_.rows_ref, bf16[4,320,768]{2,1,0:T(8,128)(2,1)} %copy-done, bf16[320,320]{1,0:T(8,128)(2,1)} %get-tuple-element.46.order_ref), custom_call_target="tpu_custom_call" | custom-call | flops 1000000000 | bytes 6291456 | tf_op jit(solution)/shard_map/left/pallas_call | solution.py:176
  145.1 12.7 %all-to-all-start.3 = ((f32[32,4,768]{2,1,0:T(4,128)}), f32[32,4,768]{2,1,0:T(4,128)S(1)}, u32[]{:S(2)}, u32[]{:S(2)}) async-start(f32[32,4,768]{2,1,0:T(4,128)} %left.1), calls=%async_computation.3 | async-start | bytes 786432 | tf_op jit(solution)/shard_map/all_to_all | solution.py:389
  157.8 11.6 %back.1 = bf16[16,80,768]{2,1,0:T(8,128)(2,1)} custom-call(s32[1]{0:T(128)} %bitcast.z_ref, bf16[4,8,112,2048]{3,2,1,0:T(8,128)(2,1)} %bitcast.45, bf16[320,320]{1,0:T(8,128)(2,1)} %get-tuple-element.29.move_ref, bf16[4,80,2048]{2,1,0:T(8,128)(2,1)} %rows.4.refs_0_, bf16[4,80,2048]{2,1,0:T(8,128)(2,1)} %rows.5.refs_1_, bf16[4,80,2048]{2,1,0:T(8,128)(2,1)} %rows.6.refs_2_, ...), custom_call_target="tpu_custom_call" | custom-call | flops 4000000000 | bytes 20971520 | tf_op jit(solution)/shard_map/back/pallas_call | solution.py:214
  169.4 15.2 %all-to-all-start.1 = ((bf16[16,80,768]{2,1,0:T(8,128)(2,1)}), bf16[16,80,768]{2,1,0:T(8,128)(2,1)S(1)}, u32[]{:S(2)}, u32[]{:S(2)}) async-start(bf16[16,80,768]{2,1,0:T(8,128)(2,1)} %back.1), calls=%async_computation.1 | async-start | bytes 3932160 | tf_op jit(solution)/shard_map/all_to_all | solution.py:388
  184.7 25.7 %all-gather = f32[32,4,768]{2,1,0:T(4,128)S(1)} all-gather(f32[1,4,768]{2,1,0:T(4,128)S(1)} %bitcast.49), channel_id=1, replica_groups=mesh['y'=4,'c'=2,'x'=4,'z'=16] {'x','y','c'}, dimensions={0}, use_global_device_ids=true | all-gather | bytes 405504 | tf_op jit(solution)/shard_map/all_gather | solution.py:390
  210.4 0.9 reshape.36.sum_ref
  211.3 5.3 %basis.1.basis_ref = f32[4,32,768]{2,1,0:T(8,128)} custom-call(f32[128,768]{1,0:T(8,128)} %reshape.36.sum_ref), custom_call_target="tpu_custom_call" | custom-call | flops 10000000 | bytes 1048576 | tf_op jit(solution)/shard_map/basis/pallas_call | solution.py:320
  216.6 7.0 %right.1 = f32[4,32,2048]{2,1,0:T(8,128)} custom-call(f32[4,32,768]{2,1,0:T(8,128)} %basis.1.basis_ref, bf16[4,320,768]{2,1,0:T(8,128)(2,1)} %copy-done, bf16[320,320]{1,0:T(8,128)(2,1)} %get-tuple-element.46.order_ref, bf16[4,80,2048]{2,1,0:T(8,128)(2,1)} %rows.4.refs_0_, bf16[4,80,2048]{2,1,0:T(8,128)(2,1)} %rows.5.refs_1_, ...), custom_call_target="tpu_custom_call" | custom-call | flops 1000000000 | bytes 9437184 | tf_op jit(solution)/shard_map/right/pallas_call | solution.py:242
  223.5 1.2 dynamic-slice_bitcast_fusion.2
  224.7 4.1 %collective-permute-start.16 = (f32[32,2048]{1,0:T(8,128)S(1)}, f32[32,2048]{1,0:T(8,128)S(1)}, u32[]{:S(2)}, u32[]{:S(2)}) collective-permute-start(f32[32,2048]{1,0:T(8,128)S(1)} %get-tuple-element.56), channel_id=1, source_target_pairs={{0,32},{16,48},{32,0},{48,16},{1,33},{17,49},{33,1},{49,17},{2,34}... | collective-permute-start | bytes 786440 | tf_op jit(solution)/shard_map/ppermute | solution.py:333
  228.8 2.4 collective-permute-start.17
  231.2 4.1 %collective-permute-start.18 = (f32[32,2048]{1,0:T(8,128)S(1)}, f32[32,2048]{1,0:T(8,128)S(1)}, u32[]{:S(2)}, u32[]{:S(2)}) collective-permute-start(f32[32,2048]{1,0:T(8,128)S(1)} %get-tuple-element.57), channel_id=1, source_target_pairs={{0,48},{16,0},{32,16},{48,32},{1,49},{17,1},{33,17},{49,33},{2,50}... | collective-permute-start | bytes 786440 | tf_op jit(solution)/shard_map/ppermute | solution.py:333
  235.8 6.1 %collective-permute-done.17 = f32[32,2048]{1,0:T(8,128)S(1)} collective-permute-done((f32[32,2048]{1,0:T(8,128)S(1)}, f32[32,2048]{1,0:T(8,128)S(1)}, u32[]{:S(2)}, u32[]{:S(2)}) %collective-permute-start.17) | collective-permute-done | bytes 262176 | tf_op jit(solution)/shard_map/ppermute | solution.py:333
  241.9 1.0 fusion.1
  243.0 2.4 collective-permute-start.19
  245.4 1.1 collective-permute-done.19
  246.5 4.2 %collective-permute-start.20 = (f32[32,2048]{1,0:T(8,128)S(1)}, f32[32,2048]{1,0:T(8,128)S(1)}, u32[]{:S(2)}, u32[]{:S(2)}) collective-permute-start(f32[32,2048]{1,0:T(8,128)S(1)} %add.92), channel_id=1, source_target_pairs={{0,256},{128,384},{256,0},{384,128},{1,257},{129,385},{257,1},{385... | collective-permute-start | bytes 786440 | tf_op jit(solution)/shard_map/ppermute | solution.py:335
  250.8 2.3 collective-permute-start.21
  253.0 4.2 %collective-permute-start.22 = (f32[32,2048]{1,0:T(8,128)S(1)}, f32[32,2048]{1,0:T(8,128)S(1)}, u32[]{:S(2)}, u32[]{:S(2)}) collective-permute-start(f32[32,2048]{1,0:T(8,128)S(1)} %add.92), channel_id=1, source_target_pairs={{0,384},{128,0},{256,128},{384,256},{1,385},{129,1},{257,129},{385... | collective-permute-start | bytes 786440 | tf_op jit(solution)/shard_map/ppermute | solution.py:335
  257.4 1.0 reshape.37.place_ref
  258.4 1.5 multiply_bitcast_fusion.1
  259.9 3.8 %collective-permute-done.21 = f32[32,2048]{1,0:T(8,128)S(1)} collective-permute-done((f32[32,2048]{1,0:T(8,128)S(1)}, f32[32,2048]{1,0:T(8,128)S(1)}, u32[]{:S(2)}, u32[]{:S(2)}) %collective-permute-start.21) | collective-permute-done | bytes 262176 | tf_op jit(solution)/shard_map/ppermute | solution.py:335
  263.8 0.8 multiply_bitcast_fusion
  264.5 6.5 %all-to-all-done.1 = bf16[16,80,768]{2,1,0:T(8,128)(2,1)S(1)} async-done(((bf16[16,80,768]{2,1,0:T(8,128)(2,1)}), bf16[16,80,768]{2,1,0:T(8,128)(2,1)S(1)}, u32[]{:S(2)}, u32[]{:S(2)}) %all-to-all-start.1) | async-done | bytes 1966112 | tf_op jit(solution)/shard_map/all_to_all | solution.py:388
  271.0 1.3 copy-done.1
  272.3 5.8 %spread.1 = bf16[128,8,768]{2,1,0:T(8,128)(2,1)} custom-call(s32[1024,1]{1,0:T(8,128)} %reshape.37.place_ref, bf16[1280,768]{1,0:T(8,128)(2,1)} %bitcast.47), custom_call_target="tpu_custom_call" | custom-call | flops 2000000000 | bytes 4194304 | tf_op jit(solution)/shard_map/spread/pallas_call | solution.py:269
  (64 shorter events, 2.7 us)
Async XLA Ops:
  7.2 2.9 %copy-start.5 = (bf16[128,2048]{1,0:T(8,128)(2,1)S(1)}, bf16[128,2048]{1,0:T(8,128)(2,1)}, u32[]{:S(2)}) copy-start(bf16[128,2048]{1,0:T(8,128)(2,1)} %refs_0_.1) | copy-start | bytes 1572868
  7.2 16.8 %copy-start.17 = (s32[128,8]{0,1:T(8,128)S(1)}, s32[128,8]{0,1:T(8,128)}, u32[]{:S(2)}) copy-start(s32[128,8]{0,1:T(8,128)} %param.7) | copy-start | bytes 12292
  7.2 17.1 %copy-start.18 = (f32[128,8]{0,1:T(8,128)S(1)}, f32[128,8]{0,1:T(8,128)}, u32[]{:S(2)}) copy-start(f32[128,8]{0,1:T(8,128)} %param.8) | copy-start | bytes 12292
  7.2 121.7 %all-gather.3.cloned.1.call-start = ((), (), s32[]{:S(2)}) async-start(), calls=%async_computation.4 | async-start | bytes 15138816 | tf_op jit(solution)/shard_map/all_gather | solution.py:347
  10.1 35.3 %collective-permute-start = (bf16[128,2048]{1,0:T(8,128)(2,1)S(1)}, bf16[128,2048]{1,0:T(8,128)(2,1)S(1)}, u32[]{:S(2)}, u32[]{:S(2)}) collective-permute-start(bf16[128,2048]{1,0:T(8,128)(2,1)S(1)} %copy-done.5), channel_id=1, source_target_pairs={{0,1},{1,2},{2,3},{3,4},{4,5},{5,6},{6,7},{7,8},{8,9},{9,10},{10,1... | collective-permute-start | bytes 1572872 | tf_op jit(solution)/shard_map/ppermute | solution.py:360
  14.5 20.1 %collective-permute-start.1 = (bf16[128,2048]{1,0:T(8,128)(2,1)S(1)}, bf16[128,2048]{1,0:T(8,128)(2,1)S(1)}, u32[]{:S(2)}, u32[]{:S(2)}) collective-permute-start(bf16[128,2048]{1,0:T(8,128)(2,1)S(1)} %copy-done.5), channel_id=1, source_target_pairs={{0,15},{1,0},{2,1},{3,2},{4,3},{5,4},{6,5},{7,6},{8,7},{9,8},{10,9... | collective-permute-start | bytes 1572872 | tf_op jit(solution)/shard_map/ppermute | solution.py:361
  25.0 20.4 %all-to-all-start = ((f32[16,16,128]{2,1,0:T(8,128)}), f32[16,16,128]{2,1,0:T(8,128)S(1)}, u32[]{:S(2)}, u32[]{:S(2)}) async-start(f32[16,16,128]{2,1,0:T(8,128)} %broadcast_in_dim.38), calls=%async_computation | async-start | bytes 262144 | tf_op jit(solution)/shard_map/all_to_all | solution.py:350
  34.5 34.3 %copy-start.8 = (bf16[128,2048]{1,0:T(8,128)(2,1)}, bf16[128,2048]{1,0:T(8,128)(2,1)S(1)}, u32[]{:S(2)}) copy-start(bf16[128,2048]{1,0:T(8,128)(2,1)S(1)} %collective-permute-done.1.refs_2_) | copy-start | bytes 1572868
  34.6 16.9 %collective-permute-start.3 = (bf16[128,2048]{1,0:T(8,128)(2,1)S(1)}, bf16[128,2048]{1,0:T(8,128)(2,1)S(1)}, u32[]{:S(2)}, u32[]{:S(2)}) collective-permute-start(bf16[128,2048]{1,0:T(8,128)(2,1)S(1)} %collective-permute-done.1.refs_2_), channel_id=1, source_target_pairs={{0,15},{1,0},{2,1},{3,2},{4,3},{5,4},{6,5},{7,6},{8,7},{9,8},{10,9... | collective-permute-start | bytes 1572872 | tf_op jit(solution)/shard_map/ppermute | solution.py:361
  45.4 8.9 %copy-start.4 = (f32[16,16,128]{2,1,0:T(8,128)}, f32[16,16,128]{2,1,0:T(8,128)S(1)}, u32[]{:S(2)}) copy-start(f32[16,16,128]{2,1,0:T(8,128)S(1)} %all-to-all-done.meta_ref) | copy-start | bytes 393220
  45.4 23.4 %copy-start.7 = (bf16[128,2048]{1,0:T(8,128)(2,1)}, bf16[128,2048]{1,0:T(8,128)(2,1)S(1)}, u32[]{:S(2)}) copy-start(bf16[128,2048]{1,0:T(8,128)(2,1)S(1)} %collective-permute-done.refs_1_) | copy-start | bytes 1572868
  45.4 12.9 %collective-permute-start.2 = (bf16[128,2048]{1,0:T(8,128)(2,1)S(1)}, bf16[128,2048]{1,0:T(8,128)(2,1)S(1)}, u32[]{:S(2)}, u32[]{:S(2)}) collective-permute-start(bf16[128,2048]{1,0:T(8,128)(2,1)S(1)} %collective-permute-done.refs_1_), channel_id=1, source_target_pairs={{0,1},{1,2},{2,3},{3,4},{4,5},{5,6},{6,7},{7,8},{8,9},{9,10},{10,1... | collective-permute-start | bytes 1572872 | tf_op jit(solution)/shard_map/ppermute | solution.py:360
  51.4 20.8 %copy-start.6 = (bf16[128,2048]{1,0:T(8,128)(2,1)}, bf16[128,2048]{1,0:T(8,128)(2,1)S(1)}, u32[]{:S(2)}) copy-start(bf16[128,2048]{1,0:T(8,128)(2,1)S(1)} %collective-permute-done.3.refs_0_) | copy-start | bytes 1572868
  51.4 15.5 %collective-permute-start.5 = (bf16[128,2048]{1,0:T(8,128)(2,1)S(1)}, bf16[128,2048]{1,0:T(8,128)(2,1)S(1)}, u32[]{:S(2)}, u32[]{:S(2)}) collective-permute-start(bf16[128,2048]{1,0:T(8,128)(2,1)S(1)} %collective-permute-done.3.refs_0_), channel_id=1, source_target_pairs={{0,15},{1,0},{2,1},{3,2},{4,3},{5,4},{6,5},{7,6},{8,7},{9,8},{10,9... | collective-permute-start | bytes 1572872 | tf_op jit(solution)/shard_map/ppermute | solution.py:361
  58.3 10.6 %copy-start.15 = (bf16[128,2048]{1,0:T(8,128)(2,1)}, bf16[128,2048]{1,0:T(8,128)(2,1)S(1)}, u32[]{:S(2)}) copy-start(bf16[128,2048]{1,0:T(8,128)(2,1)S(1)} %collective-permute-done.2.refs_3_) | copy-start | bytes 1572868
  58.3 13.9 %collective-permute-start.4 = (bf16[128,2048]{1,0:T(8,128)(2,1)S(1)}, bf16[128,2048]{1,0:T(8,128)(2,1)S(1)}, u32[]{:S(2)}, u32[]{:S(2)}) collective-permute-start(bf16[128,2048]{1,0:T(8,128)(2,1)S(1)} %collective-permute-done.2.refs_3_), channel_id=1, source_target_pairs={{0,1},{1,2},{2,3},{3,4},{4,5},{5,6},{6,7},{7,8},{8,9},{9,10},{10,1... | collective-permute-start | bytes 1572872 | tf_op jit(solution)/shard_map/ppermute | solution.py:360
  66.9 5.3 %copy-start.10 = (bf16[128,2048]{1,0:T(8,128)(2,1)}, bf16[128,2048]{1,0:T(8,128)(2,1)S(1)}, u32[]{:S(2)}) copy-start(bf16[128,2048]{1,0:T(8,128)(2,1)S(1)} %collective-permute-done.5.refs_2_) | copy-start | bytes 1572868
  66.9 14.9 %collective-permute-start.7 = (bf16[128,2048]{1,0:T(8,128)(2,1)S(1)}, bf16[128,2048]{1,0:T(8,128)(2,1)S(1)}, u32[]{:S(2)}, u32[]{:S(2)}) collective-permute-start(bf16[128,2048]{1,0:T(8,128)(2,1)S(1)} %collective-permute-done.5.refs_2_), channel_id=1, source_target_pairs={{0,15},{1,0},{2,1},{3,2},{4,3},{5,4},{6,5},{7,6},{8,7},{9,8},{10,9... | collective-permute-start | bytes 1572872 | tf_op jit(solution)/shard_map/ppermute | solution.py:361
  72.2 9.5 %copy-start.12 = (bf16[128,2048]{1,0:T(8,128)(2,1)}, bf16[128,2048]{1,0:T(8,128)(2,1)S(1)}, u32[]{:S(2)}) copy-start(bf16[128,2048]{1,0:T(8,128)(2,1)S(1)} %collective-permute-done.4.refs_1_) | copy-start | bytes 1572868
  72.2 13.5 %collective-permute-start.6 = (bf16[128,2048]{1,0:T(8,128)(2,1)S(1)}, bf16[128,2048]{1,0:T(8,128)(2,1)}, u32[]{:S(2)}, u32[]{:S(2)}) collective-permute-start(bf16[128,2048]{1,0:T(8,128)(2,1)S(1)} %collective-permute-done.4.refs_1_), channel_id=1, source_target_pairs={{0,1},{1,2},{2,3},{3,4},{4,5},{5,6},{6,7},{7,8},{8,9},{9,10},{10,1... | collective-permute-start | bytes 1572872 | tf_op jit(solution)/shard_map/ppermute | solution.py:360
  81.8 8.3 %copy-start.9 = (bf16[128,2048]{1,0:T(8,128)(2,1)}, bf16[128,2048]{1,0:T(8,128)(2,1)S(1)}, u32[]{:S(2)}) copy-start(bf16[128,2048]{1,0:T(8,128)(2,1)S(1)} %collective-permute-done.7.refs_0_) | copy-start | bytes 1572868
  81.8 14.1 %collective-permute-start.9 = (bf16[128,2048]{1,0:T(8,128)(2,1)S(1)}, bf16[128,2048]{1,0:T(8,128)(2,1)S(1)}, u32[]{:S(2)}, u32[]{:S(2)}) collective-permute-start(bf16[128,2048]{1,0:T(8,128)(2,1)S(1)} %collective-permute-done.7.refs_0_), channel_id=1, source_target_pairs={{0,15},{1,0},{2,1},{3,2},{4,3},{5,4},{6,5},{7,6},{8,7},{9,8},{10,9... | collective-permute-start | bytes 1572872 | tf_op jit(solution)/shard_map/ppermute | solution.py:361
  85.8 15.6 %collective-permute-start.8 = (bf16[128,2048]{1,0:T(8,128)(2,1)}, bf16[128,2048]{1,0:T(8,128)(2,1)S(1)}, u32[]{:S(2)}, u32[]{:S(2)}) collective-permute-start(bf16[128,2048]{1,0:T(8,128)(2,1)} %collective-permute-done.6.refs_3_), channel_id=1, source_target_pairs={{0,1},{1,2},{2,3},{3,4},{4,5},{5,6},{6,7},{7,8},{8,9},{9,10},{10,1... | collective-permute-start | bytes 1572872 | tf_op jit(solution)/shard_map/ppermute | solution.py:360
  90.1 48.3 %all-to-all-start.2 = ((bf16[4,320,768]{2,1,0:T(8,128)(2,1)}), bf16[4,320,768]{2,1,0:T(8,128)(2,1)S(1)}, u32[]{:S(2)}, u32[]{:S(2)}) async-start(bf16[4,320,768]{2,1,0:T(8,128)(2,1)} %bitcast.46), calls=%async_computation.2 | async-start | bytes 3932160 | tf_op jit(solution)/shard_map/all_to_all | solution.py:353
  95.9 5.4 %copy-start.13 = (bf16[128,2048]{1,0:T(8,128)(2,1)}, bf16[128,2048]{1,0:T(8,128)(2,1)S(1)}, u32[]{:S(2)}) copy-start(bf16[128,2048]{1,0:T(8,128)(2,1)S(1)} %collective-permute-done.9.refs_2_) | copy-start | bytes 1572868
  95.9 13.1 %collective-permute-start.11 = (bf16[128,2048]{1,0:T(8,128)(2,1)S(1)}, bf16[128,2048]{1,0:T(8,128)(2,1)S(1)}, u32[]{:S(2)}, u32[]{:S(2)}) collective-permute-start(bf16[128,2048]{1,0:T(8,128)(2,1)S(1)} %collective-permute-done.9.refs_2_), channel_id=1, source_target_pairs={{0,15},{1,0},{2,1},{3,2},{4,3},{5,4},{6,5},{7,6},{8,7},{9,8},{10,9... | collective-permute-start | bytes 1572872 | tf_op jit(solution)/shard_map/ppermute | solution.py:361
  101.3 9.6 %copy-start.14 = (bf16[128,2048]{1,0:T(8,128)(2,1)}, bf16[128,2048]{1,0:T(8,128)(2,1)S(1)}, u32[]{:S(2)}) copy-start(bf16[128,2048]{1,0:T(8,128)(2,1)S(1)} %collective-permute-done.8.refs_1_) | copy-start | bytes 1572868
  101.3 13.1 %collective-permute-start.10 = (bf16[128,2048]{1,0:T(8,128)(2,1)S(1)}, bf16[128,2048]{1,0:T(8,128)(2,1)S(1)}, u32[]{:S(2)}, u32[]{:S(2)}) collective-permute-start(bf16[128,2048]{1,0:T(8,128)(2,1)S(1)} %collective-permute-done.8.refs_1_), channel_id=1, source_target_pairs={{0,1},{1,2},{2,3},{3,4},{4,5},{5,6},{6,7},{7,8},{8,9},{9,10},{10,1... | collective-permute-start | bytes 1572872 | tf_op jit(solution)/shard_map/ppermute | solution.py:360
  109.0 11.8 %copy-start.11 = (bf16[128,2048]{1,0:T(8,128)(2,1)}, bf16[128,2048]{1,0:T(8,128)(2,1)S(1)}, u32[]{:S(2)}) copy-start(bf16[128,2048]{1,0:T(8,128)(2,1)S(1)} %collective-permute-done.11.refs_0_) | copy-start | bytes 1572868
  109.0 12.1 %collective-permute-start.13 = (bf16[128,2048]{1,0:T(8,128)(2,1)S(1)}, bf16[128,2048]{1,0:T(8,128)(2,1)S(1)}, u32[]{:S(2)}, u32[]{:S(2)}) collective-permute-start(bf16[128,2048]{1,0:T(8,128)(2,1)S(1)} %collective-permute-done.11.refs_0_), channel_id=1, source_target_pairs={{0,15},{1,0},{2,1},{3,2},{4,3},{5,4},{6,5},{7,6},{8,7},{9,8},{10,9... | collective-permute-start | bytes 1572872 | tf_op jit(solution)/shard_map/ppermute | solution.py:361
  114.4 3.0 %copy-start.16 = (bf16[128,2048]{1,0:T(8,128)(2,1)}, bf16[128,2048]{1,0:T(8,128)(2,1)S(1)}, u32[]{:S(2)}) copy-start(bf16[128,2048]{1,0:T(8,128)(2,1)S(1)} %collective-permute-done.10.refs_3_) | copy-start | bytes 1572868
  114.4 12.1 %collective-permute-start.12 = (bf16[128,2048]{1,0:T(8,128)(2,1)S(1)}, bf16[128,2048]{1,0:T(8,128)(2,1)S(1)}, u32[]{:S(2)}, u32[]{:S(2)}) collective-permute-start(bf16[128,2048]{1,0:T(8,128)(2,1)S(1)} %collective-permute-done.10.refs_3_), channel_id=1, source_target_pairs={{0,1},{1,2},{2,3},{3,4},{4,5},{5,6},{6,7},{7,8},{8,9},{9,10},{10,1... | collective-permute-start | bytes 1572872 | tf_op jit(solution)/shard_map/ppermute | solution.py:360
  121.1 13.4 %copy-start.2 = (bf16[128,2048]{1,0:T(8,128)(2,1)}, bf16[128,2048]{1,0:T(8,128)(2,1)S(1)}, u32[]{:S(2)}) copy-start(bf16[128,2048]{1,0:T(8,128)(2,1)S(1)} %collective-permute-done.13.refs_2_) | copy-start | bytes 1572868
  121.1 13.4 %collective-permute-start.15 = (bf16[64,2048]{1,0:T(8,128)(2,1)S(1)}, bf16[64,2048]{1,0:T(8,128)(2,1)}, u32[]{:S(2)}, u32[]{:S(2)}) collective-permute-start(bf16[64,2048]{1,0:T(8,128)(2,1)S(1)} %slice.7), channel_id=1, source_target_pairs={{0,15},{1,0},{2,1},{3,2},{4,3},{5,4},{6,5},{7,6},{8,7},{9,8},{10,9... | collective-permute-start | bytes 786440 | tf_op jit(solution)/shard_map/ppermute | solution.py:381
  126.5 8.0 %copy-start.3 = (bf16[128,2048]{1,0:T(8,128)(2,1)}, bf16[128,2048]{1,0:T(8,128)(2,1)S(1)}, u32[]{:S(2)}) copy-start(bf16[128,2048]{1,0:T(8,128)(2,1)S(1)} %collective-permute-done.12.refs_1_) | copy-start | bytes 1572868
  126.5 8.4 %collective-permute-start.14 = (bf16[64,2048]{1,0:T(8,128)(2,1)S(1)}, bf16[64,2048]{1,0:T(8,128)(2,1)}, u32[]{:S(2)}, u32[]{:S(2)}) collective-permute-start(bf16[64,2048]{1,0:T(8,128)(2,1)S(1)} %slice.6), channel_id=1, source_target_pairs={{0,1},{1,2},{2,3},{3,4},{4,5},{5,6},{6,7},{7,8},{8,9},{9,10},{10,1... | collective-permute-start | bytes 786440 | tf_op jit(solution)/shard_map/ppermute | solution.py:380
  138.4 1.3 copy-start
  145.1 24.3 %all-to-all-start.3 = ((f32[32,4,768]{2,1,0:T(4,128)}), f32[32,4,768]{2,1,0:T(4,128)S(1)}, u32[]{:S(2)}, u32[]{:S(2)}) async-start(f32[32,4,768]{2,1,0:T(4,128)} %left.1), calls=%async_computation.3 | async-start | bytes 786432 | tf_op jit(solution)/shard_map/all_to_all | solution.py:389
  169.4 101.5 %all-to-all-start.1 = ((bf16[16,80,768]{2,1,0:T(8,128)(2,1)}), bf16[16,80,768]{2,1,0:T(8,128)(2,1)S(1)}, u32[]{:S(2)}, u32[]{:S(2)}) async-start(bf16[16,80,768]{2,1,0:T(8,128)(2,1)} %back.1), calls=%async_computation.1 | async-start | bytes 3932160 | tf_op jit(solution)/shard_map/all_to_all | solution.py:388
  224.7 11.2 %collective-permute-start.16 = (f32[32,2048]{1,0:T(8,128)S(1)}, f32[32,2048]{1,0:T(8,128)S(1)}, u32[]{:S(2)}, u32[]{:S(2)}) collective-permute-start(f32[32,2048]{1,0:T(8,128)S(1)} %get-tuple-element.56), channel_id=1, source_target_pairs={{0,32},{16,48},{32,0},{48,16},{1,33},{17,49},{33,1},{49,17},{2,34}... | collective-permute-start | bytes 786440 | tf_op jit(solution)/shard_map/ppermute | solution.py:333
  228.8 13.1 %collective-permute-start.17 = (f32[32,2048]{1,0:T(8,128)S(1)}, f32[32,2048]{1,0:T(8,128)S(1)}, u32[]{:S(2)}, u32[]{:S(2)}) collective-permute-start(f32[32,2048]{1,0:T(8,128)S(1)} %get-tuple-element.58), channel_id=1, source_target_pairs={{0,16},{16,32},{32,48},{48,0},{1,17},{17,33},{33,49},{49,1},{2,18}... | collective-permute-start | bytes 786440 | tf_op jit(solution)/shard_map/ppermute | solution.py:333
  231.2 10.7 %collective-permute-start.18 = (f32[32,2048]{1,0:T(8,128)S(1)}, f32[32,2048]{1,0:T(8,128)S(1)}, u32[]{:S(2)}, u32[]{:S(2)}) collective-permute-start(f32[32,2048]{1,0:T(8,128)S(1)} %get-tuple-element.57), channel_id=1, source_target_pairs={{0,48},{16,0},{32,16},{48,32},{1,49},{17,1},{33,17},{49,33},{2,50}... | collective-permute-start | bytes 786440 | tf_op jit(solution)/shard_map/ppermute | solution.py:333
  243.0 3.5 %collective-permute-start.19 = (f32[32,2048]{1,0:T(8,128)S(1)}, f32[32,2048]{1,0:T(8,128)S(1)}, u32[]{:S(2)}, u32[]{:S(2)}) collective-permute-start(f32[32,2048]{1,0:T(8,128)S(1)} %fusion.1), channel_id=1, source_target_pairs={{0,64},{64,0},{1,65},{65,1},{2,66},{66,2},{3,67},{67,3},{4,68},{68... | collective-permute-start | bytes 786440 | tf_op jit(solution)/shard_map/ppermute | solution.py:334
  246.5 13.4 %collective-permute-start.20 = (f32[32,2048]{1,0:T(8,128)S(1)}, f32[32,2048]{1,0:T(8,128)S(1)}, u32[]{:S(2)}, u32[]{:S(2)}) collective-permute-start(f32[32,2048]{1,0:T(8,128)S(1)} %add.92), channel_id=1, source_target_pairs={{0,256},{128,384},{256,0},{384,128},{1,257},{129,385},{257,1},{385... | collective-permute-start | bytes 786440 | tf_op jit(solution)/shard_map/ppermute | solution.py:335
  250.8 13.0 %collective-permute-start.21 = (f32[32,2048]{1,0:T(8,128)S(1)}, f32[32,2048]{1,0:T(8,128)S(1)}, u32[]{:S(2)}, u32[]{:S(2)}) collective-permute-start(f32[32,2048]{1,0:T(8,128)S(1)} %add.92), channel_id=1, source_target_pairs={{0,128},{128,256},{256,384},{384,0},{1,129},{129,257},{257,385},{3... | collective-permute-start | bytes 786440 | tf_op jit(solution)/shard_map/ppermute | solution.py:335
  253.0 10.7 %collective-permute-start.22 = (f32[32,2048]{1,0:T(8,128)S(1)}, f32[32,2048]{1,0:T(8,128)S(1)}, u32[]{:S(2)}, u32[]{:S(2)}) collective-permute-start(f32[32,2048]{1,0:T(8,128)S(1)} %add.92), channel_id=1, source_target_pairs={{0,384},{128,0},{256,128},{384,256},{1,385},{129,1},{257,129},{385... | collective-permute-start | bytes 786440 | tf_op jit(solution)/shard_map/ppermute | solution.py:335
  271.0 1.3 copy-start.1
Sparse Core Ops, SparseCore 0:
  11.2 88.8 all-gather.2

commit v4 on v3

--- a/solution.py
+++ b/solution.py
@@ -41,6 +41,12 @@
     mid = rest.astype(BF)
     low = (rest - mid.astype(F32)).astype(BF)
     return jnp.concatenate([high, mid, low], axis=0)
+
+
+def three_outside(a):
+    high = lax.reduce_precision(a, 8, 7)
+    mid = lax.reduce_precision(a - high, 8, 7)
+    return jnp.concatenate([high, mid, a - high - mid], axis=0).astype(BF)
 
 
 def fold(a):
@@ -168,7 +174,7 @@
 def left_kernel(near_ref, gathered_ref, rows_ref, hidden_ref, order_ref, part_ref):
     projected = unfold(dot(gathered_ref[0].reshape(N_REP * PAD, D), rows_ref[0], NT))
     ordered = near_ref[0] + dot(three(projected), order_ref[...]).astype(BF)
-    part_ref[...] = fold(dot(ordered, hidden_ref[0])).reshape(part_ref.shape)
+    part_ref[0] = fold(dot(ordered, hidden_ref[0]))
 
 
 def left_part(near, gathered, rows, hidden, order):
@@ -183,8 +189,8 @@
             pl.BlockSpec((1, SLOTS, FF), lambda x: (x, 0, 0)),
             pl.BlockSpec((SPAN, SLOTS), lambda x: (last, 0)),
         ],
-        out_specs=pl.BlockSpec((N_REP, RANK // N_REP, FF), lambda x: (x, 0, 0)),
-        out_shape=jax.ShapeDtypeStruct((N_X * N_REP, RANK // N_REP, FF), F32),
+        out_specs=pl.BlockSpec((1, RANK, FF), lambda x: (x, 0, 0)),
+        out_shape=jax.ShapeDtypeStruct((N_X, RANK, FF), F32),
         compiler_params=pltpu.CompilerParams(vmem_limit_bytes=LIMIT),
         cost_estimate=pl.CostEstimate(flops=10**9, bytes_accessed=6 << 20, transcendentals=0),
         name="left",
@@ -250,7 +256,7 @@
         + [pl.BlockSpec((1, SPAN, D), lambda x: (x, 0, 0))] * GROUPS,
         out_specs=pl.BlockSpec((1, RANK, D), lambda x: (x, 0, 0)),
         out_shape=jax.ShapeDtypeStruct((N_X, RANK, D), F32),
-        compiler_params=pltpu.CompilerParams(vmem_limit_bytes=LIMIT),
+        compiler_params=pltpu.CompilerParams(vmem_limit_bytes=12 << 20),
         cost_estimate=pl.CostEstimate(flops=10**9, bytes_accessed=9 << 20, transcendentals=0),
         name="right",
     )(basis, hidden, order, *rows)
@@ -275,7 +281,7 @@
         ],
         out_specs=pl.BlockSpec((pairs // 8, 8, FF), lambda i: (i, 0, 0)),
         out_shape=jax.ShapeDtypeStruct((TOK, 8, FF), BF),
-        compiler_params=pltpu.CompilerParams(vmem_limit_bytes=LIMIT),
+        compiler_params=pltpu.CompilerParams(vmem_limit_bytes=16 << 20),
         cost_estimate=pl.CostEstimate(flops=2 * 10**9, bytes_accessed=4 << 20, transcendentals=0),
         name="spread",
     )(place, rows)
@@ -296,8 +302,12 @@
     return place.reshape(TOK * 8, 1)
 
 
-def basis_kernel(sum_ref, basis_ref):
-    sums = [sum_ref[x * RANK : (x + 1) * RANK, :] for x in range(N_X)]
+def basis_kernel(c_ref, mine_ref, other_ref, basis_ref):
+    first = c_ref[0] == 0
+    sums = []
+    for x in range(N_X):
+        mine, other = mine_ref[x], other_ref[x]
+        sums.append(jnp.concatenate([jnp.where(first, mine, other), jnp.where(first, other, mine)], axis=0))
     exact = lax.Precision.HIGHEST
     gram = jnp.stack(
         [lax.dot_general(p, p, NT, precision=exact, preferred_element_type=F32) for p in sums]
@@ -316,33 +326,47 @@
         basis_ref[x] = lax.dot_general(done[x], sums[x], NN, precision=exact, preferred_element_type=F32)
 
 
-def orthonormal(p_sum):
+def orthonormal(c, mine, other):
     return pl.pallas_call(
         basis_kernel,
+        in_specs=[pl.BlockSpec(memory_space=pltpu.SMEM)] + [pl.BlockSpec(memory_space=pltpu.VMEM)] * 2,
         out_shape=jax.ShapeDtypeStruct((N_X, RANK, FF), F32),
-        compiler_params=pltpu.CompilerParams(vmem_limit_bytes=LIMIT),
+        compiler_params=pltpu.CompilerParams(vmem_limit_bytes=12 << 20),
         cost_estimate=pl.CostEstimate(flops=10**7, bytes_accessed=1 << 20, transcendentals=0),
         name="basis",
-    )(p_sum)
-
-
-def sum_right(parts, x):
-    total = lax.dynamic_index_in_dim(parts, x, 0, keepdims=False)
+    )(c, mine, other)
+
+
+def half_sum(parts, c):
+    k = RANK // 2
+    keep = lax.dynamic_slice_in_dim(parts, c * k, k, 1)
+    send = lax.dynamic_slice_in_dim(parts, (1 - c) * k, k, 1)
+    return keep + lax.ppermute(send, "c", turn(2, 1))
+
+
+def ring_sum(a, axis):
+    moved = [lax.ppermute(a, axis, turn(4, d)) for d in (2, 1, 3)]
+    return a + moved[0] + (moved[1] + moved[2])
+
+
+def sum_right(parts, x, c):
+    half = half_sum(parts, c)
+    total = lax.dynamic_index_in_dim(half, x, 0, keepdims=False)
     for d in (2, 1, 3):
-        piece = lax.dynamic_index_in_dim(parts, lax.rem(x + d, N_X), 0, keepdims=False)
+        piece = lax.dynamic_index_in_dim(half, lax.rem(x + d, N_X), 0, keepdims=False)
         total = total + lax.ppermute(piece, "x", turn(N_X, d))
-    total = total + lax.ppermute(total, "c", turn(2, 1))
-    moved = [lax.ppermute(total, "y", turn(N_Y, d)) for d in (2, 1, 3)]
-    return total + moved[0] + (moved[1] + moved[2])
+    total = ring_sum(total, "y")
+    other = lax.ppermute(total, "c", turn(2, 1))
+    return jnp.where(c == 0, jnp.concatenate([total, other]), jnp.concatenate([other, total]))
 
 
 def shards(grad_out, expert_ids, gates, hidden, w_down, q_start):
-    x, z = lax.axis_index("x"), lax.axis_index("z")
+    x, y, c, z = (lax.axis_index(name) for name in ("x", "y", "c", "z"))
     plane = ("x", "y", "c")
     at = z.reshape(1)
     k = RANK // N_REP
-    rep = lax.axis_index("y") * 2 + lax.axis_index("c")
-    warm = three(lax.dynamic_slice(q_start[0].T, (rep * k, 0), (k, D)))
+    rep = y * 2 + c
+    warm = three_outside(lax.dynamic_slice(q_start[0].T, (rep * k, 0), (k, D)))
     warm = jnp.pad(warm, ((0, PAD - 3 * k), (0, 0)))
     gathered = lax.all_gather(jnp.concatenate([w_down[0], warm], axis=0), plane, axis=0, tiled=True)
     gathered = gathered.reshape(N_X, N_REP, SHARE + PAD, D)
@@ -383,12 +407,13 @@
     near = project(gathered, order, rows)
     last, near = lax.optimization_barrier((last, near))
     rows.append(make_rows(3, picks, scale, last))
-    p_part = left_part(near, gathered, rows[-1], stored, order)
     back = back_rows(at, gathered, move, rows)
     returned = lax.all_to_all(back, "z", split_axis=0, concat_axis=0, tiled=True)
-    shares = lax.all_to_all(p_part, plane, split_axis=0, concat_axis=0, tiled=True)
-    basis = orthonormal(lax.all_gather(jnp.sum(shares, axis=0), plane, axis=0, tiled=True))
-    q_sum = sum_right(right_part(basis, stored, order, rows), x)
+    last_rows, _ = lax.optimization_barrier((rows[-1], back))
+    p_half = half_sum(left_part(near, gathered, last_rows, stored, order), c)
+    p_half = ring_sum(ring_sum(p_half, "y"), "x")
+    basis = orthonormal(c.reshape(1), p_half, lax.ppermute(p_half, "c", turn(2, 1)))
+    q_sum = sum_right(right_part(basis, stored, order, rows), x, c)
     p_basis = lax.dynamic_index_in_dim(basis, x, 0, keepdims=False).T * math.sqrt(FF)
     place = places(expert_ids)
     grad_hidden = spread(place, returned.reshape(N_Z * N_X * CAP, FF))

time: 290 us -> 281 us (0.969); the launches traced: 285 us -> 279 us
  starting transfers between devices: 121 us -> 148 us
  blocking collectives: 25.7 us -> 0 us
  Pallas kernels: 57.6 us -> 52.4 us
    ppermute x4 -> x13, starting transfers between devices: 13.1 us -> 53.7 us  [the longest x9 32.3 us: ring_sum(): moved = [lax.ppermute(a, axis, turn(4, d)) for d in (2, 1, 3)]]
    all_gather x1 -> x0, blocking collectives: 25.7 us -> none  [shards(): lax.all_gather(jnp.sum(shares, axis=0), plane, axis=0, tiled=True)]
    all_to_all x1 -> x0, starting transfers between devices: 12.7 us -> none  [shards(): lax.all_to_all(p_part, plane, split_axis=0, concat_axis=0, tiled=True)]
    ppermute x4 -> x13, waiting for transfers between devices: 4.99 us -> 12.4 us  [the longest x9 8.99 us: ring_sum(): moved = [lax.ppermute(a, axis, turn(4, d)) for d in (2, 1, 3)]]
    all_to_all x1, waiting for transfers between devices: 6.48 us -> 0.01 us  [shards(): lax.all_to_all(back, 'z', split_axis=0, concat_axis=0, tiled=True)]
    pallas_call x1, Pallas kernels: 6.95 us -> 3.71 us  [right_part(): pl.pallas_call(right_kernel, grid=(N_X,), in_specs=[pl.BlockSpec((1, RANK...]
  transfers between devices with their start and end apart: 28 -> 36, of which waited for: 18 -> 23; matrix products, arithmetic and copies ran while one was open for 3% -> 2% of each run, Pallas kernels for 16% -> 17%
where the time goes in v4:
time: 281 us; the launch traced here: 279 us
  starting transfers between devices  148 us (53%)
  Pallas kernels  52.4 us (19%)
  waiting for transfers between devices  51 us (18%)
  between operations  14.7 us (5%)
  other arithmetic  6.43 us (2%)
  local copies, waits for them, and re-layouts  5.88 us (2%)
    ppermute x9, starting transfers between devices, ring_sum(): moved = [lax.ppermute(a, axis, turn(4, d)) for d in (2, 1, 3)]  32.3 us
    ppermute x7, starting transfers between devices, shards(): left = lax.ppermute(left, 'z', turn(N_Z, -1))  26.3 us
    ppermute x7, starting transfers between devices, shards(): right = lax.ppermute(right, 'z', turn(N_Z, 1))  25.9 us
    ppermute x7, waiting for transfers between devices, shards(): left = lax.ppermute(left, 'z', turn(N_Z, -1))  20.8 us
    all_to_all x1, starting transfers between devices, shards(): lax.all_to_all(back, 'z', split_axis=0, concat_axis=0, tiled=True)  14.6 us
    pallas_call x4, Pallas kernels, make_rows(): pl.pallas_call(rows_kernel, grid=(D // wide,), in_specs=[pl.BlockSpec((1,...  13.8 us
    pallas_call x1, Pallas kernels, back_rows(): pl.pallas_call(back_kernel, grid_spec=pltpu.PrefetchScalarGridSpec(num_sc...  11.6 us
    ppermute x2, starting transfers between devices, half_sum(): return keep + lax.ppermute(send, 'c', turn(2, 1))  11 us
  transfers between devices with their start and end apart: 36, of which 23 were waited for; matrix products, arithmetic and copies ran while one was open for 2% of the time, Pallas kernels for 17%

profile of v4, /device:TPU:1, one launch (start us, length us, event | category | flops | bytes accessed | tf_op | source)
XLA Modules:
  0.0 279.2 jit_solution(4200820141936421651)
XLA Ops:
  8.2 1.8 pad_maximum_fusion
  10.0 4.4 %collective-permute-start = (bf16[128,2048]{1,0:T(8,128)(2,1)S(1)}, bf16[128,2048]{1,0:T(8,128)(2,1)S(1)}, u32[]{:S(2)}, u32[]{:S(2)}) collective-permute-start(bf16[128,2048]{1,0:T(8,128)(2,1)S(1)} %copy-done.11), channel_id=1, source_target_pairs={{0,1},{1,2},{2,3},{3,4},{4,5},{5,6},{6,7},{7,8},{8,9},{9,10},{10,1... | collective-permute-start | bytes 1572872 | tf_op jit(solution)/shard_map/ppermute | solution.py:384
  14.4 9.5 %collective-permute-start.1 = (bf16[128,2048]{1,0:T(8,128)(2,1)S(1)}, bf16[128,2048]{1,0:T(8,128)(2,1)S(1)}, u32[]{:S(2)}, u32[]{:S(2)}) collective-permute-start(bf16[128,2048]{1,0:T(8,128)(2,1)S(1)} %copy-done.11), channel_id=1, source_target_pairs={{0,15},{1,0},{2,1},{3,2},{4,3},{5,4},{6,5},{7,6},{8,7},{9,8},{10,9... | collective-permute-start | bytes 1572872 | tf_op jit(solution)/shard_map/ppermute | solution.py:385
  25.0 8.4 %all-to-all-start = ((f32[16,16,128]{2,1,0:T(8,128)}), f32[16,16,128]{2,1,0:T(8,128)S(1)}, u32[]{:S(2)}, u32[]{:S(2)}) async-start(f32[16,16,128]{2,1,0:T(8,128)} %broadcast_in_dim.38), calls=%async_computation | async-start | bytes 262144 | tf_op jit(solution)/shard_map/all_to_all | solution.py:374
  33.3 1.2 collective-permute-done.1.refs_2_
  34.5 5.3 %collective-permute-start.3 = (bf16[128,2048]{1,0:T(8,128)(2,1)S(1)}, bf16[128,2048]{1,0:T(8,128)(2,1)S(1)}, u32[]{:S(2)}, u32[]{:S(2)}) collective-permute-start(bf16[128,2048]{1,0:T(8,128)(2,1)S(1)} %collective-permute-done.1.refs_2_), channel_id=1, source_target_pairs={{0,15},{1,0},{2,1},{3,2},{4,3},{5,4},{6,5},{7,6},{8,7},{9,8},{10,9... | collective-permute-start | bytes 1572872 | tf_op jit(solution)/shard_map/ppermute | solution.py:385
  39.8 5.5 %all-to-all-done.meta_ref = f32[16,16,128]{2,1,0:T(8,128)S(1)} async-done(((f32[16,16,128]{2,1,0:T(8,128)}), f32[16,16,128]{2,1,0:T(8,128)S(1)}, u32[]{:S(2)}, u32[]{:S(2)}) %all-to-all-start) | async-done | bytes 131104 | tf_op jit(solution)/shard_map/all_to_all | solution.py:374
  45.3 3.5 %collective-permute-start.2 = (bf16[128,2048]{1,0:T(8,128)(2,1)S(1)}, bf16[128,2048]{1,0:T(8,128)(2,1)S(1)}, u32[]{:S(2)}, u32[]{:S(2)}) collective-permute-start(bf16[128,2048]{1,0:T(8,128)(2,1)S(1)} %collective-permute-done.refs_1_), channel_id=1, source_target_pairs={{0,1},{1,2},{2,3},{3,4},{4,5},{5,6},{6,7},{7,8},{8,9},{9,10},{10,1... | collective-permute-start | bytes 1572872 | tf_op jit(solution)/shard_map/ppermute | solution.py:384
  48.8 2.5 collective-permute-done.3.refs_0_
  51.4 2.9 %collective-permute-start.5 = (bf16[128,2048]{1,0:T(8,128)(2,1)S(1)}, bf16[128,2048]{1,0:T(8,128)(2,1)S(1)}, u32[]{:S(2)}, u32[]{:S(2)}) collective-permute-start(bf16[128,2048]{1,0:T(8,128)(2,1)S(1)} %collective-permute-done.3.refs_0_), channel_id=1, source_target_pairs={{0,15},{1,0},{2,1},{3,2},{4,3},{5,4},{6,5},{7,6},{8,7},{9,8},{10,9... | collective-permute-start | bytes 1572872 | tf_op jit(solution)/shard_map/ppermute | solution.py:385
  54.3 3.3 %picks.1 = (bf16[4,320,512]{2,1,0:T(8,128)(2,1)}, f32[4,320,128]{2,1,0:T(8,128)}, bf16[320,320]{1,0:T(8,128)(2,1)}, bf16[320,320]{1,0:T(8,128)(2,1)}) custom-call(s32[1]{0:T(128)} %bitcast.z_ref, f32[16,16,128]{2,1,0:T(8,128)} %copy-done.10), custom_call_target="tpu_custom_call" | custom-call | flops 10000000 | bytes 4194304 | tf_op jit(solution)/shard_map/picks/pallas_call | solution.py:96
  58.2 3.1 %collective-permute-start.4 = (bf16[128,2048]{1,0:T(8,128)(2,1)S(1)}, bf16[128,2048]{1,0:T(8,128)(2,1)S(1)}, u32[]{:S(2)}, u32[]{:S(2)}) collective-permute-start(bf16[128,2048]{1,0:T(8,128)(2,1)S(1)} %collective-permute-done.2.refs_3_), channel_id=1, source_target_pairs={{0,1},{1,2},{2,3},{3,4},{4,5},{5,6},{6,7},{7,8},{8,9},{9,10},{10,1... | collective-permute-start | bytes 1572872 | tf_op jit(solution)/shard_map/ppermute | solution.py:384
  61.4 5.5 %collective-permute-done.5.refs_2_ = bf16[128,2048]{1,0:T(8,128)(2,1)S(1)} collective-permute-done((bf16[128,2048]{1,0:T(8,128)(2,1)S(1)}, bf16[128,2048]{1,0:T(8,128)(2,1)S(1)}, u32[]{:S(2)}, u32[]{:S(2)}) %collective-permute-start.5) | collective-permute-done | bytes 524320 | tf_op jit(solution)/shard_map/ppermute | solution.py:385
  66.9 1.9 collective-permute-start.7
  68.8 3.4 %rows.4.refs_0_ = bf16[4,80,2048]{2,1,0:T(8,128)(2,1)} custom-call(bf16[4,320,512]{2,1,0:T(8,128)(2,1)} %get-tuple-element.31.picks_ref, f32[4,320,128]{2,1,0:T(8,128)} %get-tuple-element.32.scale_ref, bf16[128,2048]{1,0:T(8,128)(2,1)} %refs_0_.1, bf16[128,2048]{1,0:T(8,128)(2,1)} %copy-done.13, bf16[128,2048]{1,0:T(8,128)(2,1)} %copy-done.14, ...), custom_call_target="tpu_custom_call" | custom-call | flops 700000000 | bytes 4194304 | tf_op jit(solution)/shard_map/rows/pallas_call | solution.py:125
  72.2 4.2 %collective-permute-start.6 = (bf16[128,2048]{1,0:T(8,128)(2,1)S(1)}, bf16[128,2048]{1,0:T(8,128)(2,1)S(1)}, u32[]{:S(2)}, u32[]{:S(2)}) collective-permute-start(bf16[128,2048]{1,0:T(8,128)(2,1)S(1)} %collective-permute-done.4.refs_1_), channel_id=1, source_target_pairs={{0,1},{1,2},{2,3},{3,4},{4,5},{5,6},{6,7},{7,8},{8,9},{9,10},{10,1... | collective-permute-start | bytes 1572872 | tf_op jit(solution)/shard_map/ppermute | solution.py:384
  76.4 5.3 %collective-permute-done.7.refs_0_ = bf16[128,2048]{1,0:T(8,128)(2,1)S(1)} collective-permute-done((bf16[128,2048]{1,0:T(8,128)(2,1)S(1)}, bf16[128,2048]{1,0:T(8,128)(2,1)S(1)}, u32[]{:S(2)}, u32[]{:S(2)}) %collective-permute-start.7) | collective-permute-done | bytes 524320 | tf_op jit(solution)/shard_map/ppermute | solution.py:385
  81.7 1.9 collective-permute-start.9
  83.6 2.1 collective-permute-done.6.refs_3_
  85.8 4.2 %collective-permute-start.8 = (bf16[128,2048]{1,0:T(8,128)(2,1)S(1)}, bf16[128,2048]{1,0:T(8,128)(2,1)}, u32[]{:S(2)}, u32[]{:S(2)}) collective-permute-start(bf16[128,2048]{1,0:T(8,128)(2,1)S(1)} %collective-permute-done.6.refs_3_), channel_id=1, source_target_pairs={{0,1},{1,2},{2,3},{3,4},{4,5},{5,6},{6,7},{7,8},{8,9},{9,10},{10,1... | collective-permute-start | bytes 1572872 | tf_op jit(solution)/shard_map/ppermute | solution.py:384
  90.0 5.8 %collective-permute-done.9.refs_2_ = bf16[128,2048]{1,0:T(8,128)(2,1)S(1)} collective-permute-done((bf16[128,2048]{1,0:T(8,128)(2,1)S(1)}, bf16[128,2048]{1,0:T(8,128)(2,1)S(1)}, u32[]{:S(2)}, u32[]{:S(2)}) %collective-permute-start.9) | collective-permute-done | bytes 524320 | tf_op jit(solution)/shard_map/ppermute | solution.py:385
  95.8 1.9 collective-permute-start.11
  97.8 3.5 %rows.5.refs_1_ = bf16[4,80,2048]{2,1,0:T(8,128)(2,1)} custom-call(bf16[4,320,512]{2,1,0:T(8,128)(2,1)} %get-tuple-element.31.picks_ref, f32[4,320,128]{2,1,0:T(8,128)} %get-tuple-element.32.scale_ref, bf16[128,2048]{1,0:T(8,128)(2,1)} %copy-done.12, bf16[128,2048]{1,0:T(8,128)(2,1)} %copy-done.19, bf16[128,2048]{1,0:T(8,128)(2,1)} %copy-done.17, ...), custom_call_target="tpu_custom_call" | custom-call | flops 700000000 | bytes 4194304 | tf_op jit(solution)/shard_map/rows/pallas_call | solution.py:125
  101.3 3.6 %collective-permute-start.10 = (bf16[128,2048]{1,0:T(8,128)(2,1)}, bf16[128,2048]{1,0:T(8,128)(2,1)}, u32[]{:S(2)}, u32[]{:S(2)}) collective-permute-start(bf16[128,2048]{1,0:T(8,128)(2,1)} %collective-permute-done.8.refs_1_), channel_id=1, source_target_pairs={{0,1},{1,2},{2,3},{3,4},{4,5},{5,6},{6,7},{7,8},{8,9},{9,10},{10,1... | collective-permute-start | bytes 1572872 | tf_op jit(solution)/shard_map/ppermute | solution.py:384
  104.9 4.0 %all-to-all-start.2 = ((bf16[4,320,768]{2,1,0:T(8,128)(2,1)}), bf16[4,320,768]{2,1,0:T(8,128)(2,1)S(1)}, u32[]{:S(2)}, u32[]{:S(2)}) async-start(bf16[4,320,768]{2,1,0:T(8,128)(2,1)} %bitcast.44), calls=%async_computation.2 | async-start | bytes 3932160 | tf_op jit(solution)/shard_map/all_to_all | solution.py:377
  108.9 2.9 %collective-permute-start.13 = (bf16[128,2048]{1,0:T(8,128)(2,1)S(1)}, bf16[128,2048]{1,0:T(8,128)(2,1)S(1)}, u32[]{:S(2)}, u32[]{:S(2)}) collective-permute-start(bf16[128,2048]{1,0:T(8,128)(2,1)S(1)} %collective-permute-done.11.refs_0_), channel_id=1, source_target_pairs={{0,15},{1,0},{2,1},{3,2},{4,3},{5,4},{6,5},{7,6},{8,7},{9,8},{10,9... | collective-permute-start | bytes 1572872 | tf_op jit(solution)/shard_map/ppermute | solution.py:385
  111.8 2.8 %collective-permute-done.10.refs_3_ = bf16[128,2048]{1,0:T(8,128)(2,1)} collective-permute-done((bf16[128,2048]{1,0:T(8,128)(2,1)}, bf16[128,2048]{1,0:T(8,128)(2,1)}, u32[]{:S(2)}, u32[]{:S(2)}) %collective-permute-start.10) | collective-permute-done | bytes 524320 | tf_op jit(solution)/shard_map/ppermute | solution.py:384
  114.7 3.0 %collective-permute-start.12 = (bf16[128,2048]{1,0:T(8,128)(2,1)}, bf16[128,2048]{1,0:T(8,128)(2,1)S(1)}, u32[]{:S(2)}, u32[]{:S(2)}) collective-permute-start(bf16[128,2048]{1,0:T(8,128)(2,1)} %collective-permute-done.10.refs_3_), channel_id=1, source_target_pairs={{0,1},{1,2},{2,3},{3,4},{4,5},{5,6},{6,7},{7,8},{8,9},{9,10},{10,1... | collective-permute-start | bytes 1572872 | tf_op jit(solution)/shard_map/ppermute | solution.py:384
  117.6 3.4 %rows.6.refs_2_ = bf16[4,80,2048]{2,1,0:T(8,128)(2,1)} custom-call(bf16[4,320,512]{2,1,0:T(8,128)(2,1)} %get-tuple-element.31.picks_ref, f32[4,320,128]{2,1,0:T(8,128)} %get-tuple-element.32.scale_ref, bf16[128,2048]{1,0:T(8,128)(2,1)} %copy-done.16, bf16[128,2048]{1,0:T(8,128)(2,1)} %collective-permute-done.8.refs_1_, bf16[128,2048]{1,0:T(8,128)(2,1)} %copy-done.18, ...), custom_call_target="tpu_custom_call" | custom-call | flops 700000000 | bytes 4194304 | tf_op jit(solution)/shard_map/rows/pallas_call | solution.py:125
  121.5 3.1 %collective-permute-start.15 = (bf16[64,2048]{1,0:T(8,128)(2,1)S(1)}, bf16[64,2048]{1,0:T(8,128)(2,1)}, u32[]{:S(2)}, u32[]{:S(2)}) collective-permute-start(bf16[64,2048]{1,0:T(8,128)(2,1)S(1)} %slice.7), channel_id=1, source_target_pairs={{0,15},{1,0},{2,1},{3,2},{4,3},{5,4},{6,5},{7,6},{8,7},{9,8},{10,9... | collective-permute-start | bytes 786440 | tf_op jit(solution)/shard_map/ppermute | solution.py:405
  124.6 2.4 collective-permute-done.12.refs_1_
  127.0 2.4 collective-permute-start.14
  129.4 5.6 %project.1.near_ref = bf16[4,96,320]{2,1,0:T(8,128)(2,1)} custom-call(bf16[4,8,112,2048]{3,2,1,0:T(8,128)(2,1)} %bitcast.41, bf16[320,320]{1,0:T(8,128)(2,1)} %get-tuple-element.47.order_ref, bf16[4,80,2048]{2,1,0:T(8,128)(2,1)} %rows.4.refs_0_, bf16[4,80,2048]{2,1,0:T(8,128)(2,1)} %rows.5.refs_1_, bf16[4,80,2048]{2,1,0:T(8,128)(2,1)} %rows.6.refs_2_), custom_call_target="tpu_custom_call" | custom-call | flops 1000000000 | bytes 6291456 | tf_op jit(solution)/shard_map/project/pallas_call | solution.py:158
  135.5 3.4 %rows.7.refs_3_.rows_ref = bf16[4,80,2048]{2,1,0:T(8,128)(2,1)} custom-call(bf16[4,320,512]{2,1,0:T(8,128)(2,1)} %get-tuple-element.31.picks_ref, f32[4,320,128]{2,1,0:T(8,128)} %get-tuple-element.32.scale_ref, bf16[128,2048]{1,0:T(8,128)(2,1)} %copy-done.15, bf16[128,2048]{1,0:T(8,128)(2,1)} %copy-done.9, bf16[128,2048]{1,0:T(8,128)(2,1)} %copy-done.8, ...), custom_call_target="tpu_custom_call" | custom-call | flops 700000000 | bytes 4194304 | tf_op jit(solution)/shard_map/rows/pallas_call | solution.py:125
  138.9 11.6 %back.1 = bf16[16,80,768]{2,1,0:T(8,128)(2,1)} custom-call(s32[1]{0:T(128)} %bitcast.z_ref, bf16[4,8,112,2048]{3,2,1,0:T(8,128)(2,1)} %bitcast.42, bf16[320,320]{1,0:T(8,128)(2,1)} %get-tuple-element.30.move_ref, bf16[4,80,2048]{2,1,0:T(8,128)(2,1)} %rows.4.refs_0_, bf16[4,80,2048]{2,1,0:T(8,128)(2,1)} %rows.5.refs_1_, bf16[4,80,2048]{2,1,0:T(8,128)(2,1)} %rows.6.refs_2_, ...), custom_call_target="tpu_custom_call" | custom-call | flops 4000000000 | bytes 20971520 | tf_op jit(solution)/shard_map/back/pallas_call | solution.py:220
  150.5 1.3 copy-done.4
  151.8 14.6 %all-to-all-start.1 = ((bf16[16,80,768]{2,1,0:T(8,128)(2,1)}), bf16[16,80,768]{2,1,0:T(8,128)(2,1)}, u32[]{:S(2)}, u32[]{:S(2)}) async-start(bf16[16,80,768]{2,1,0:T(8,128)(2,1)} %back.1), calls=%async_computation.1 | async-start | bytes 3932160 | tf_op jit(solution)/shard_map/all_to_all | solution.py:411
  166.4 5.6 %left.1 = f32[4,32,768]{2,1,0:T(8,128)} custom-call(bf16[4,96,320]{2,1,0:T(8,128)(2,1)} %project.1.near_ref, bf16[4,8,112,2048]{3,2,1,0:T(8,128)(2,1)} %bitcast.43, bf16[4,80,2048]{2,1,0:T(8,128)(2,1)} %rows.7.refs_3_.rows_ref, bf16[4,320,768]{2,1,0:T(8,128)(2,1)} %copy-done.4, bf16[320,320]{1,0:T(8,128)(2,1)} %get-tuple-element.47.order_ref), custom_call_target="tpu_custom_call" | custom-call | flops 1000000000 | bytes 6291456 | tf_op jit(solution)/shard_map/left/pallas_call | solution.py:182
  172.9 8.7 %collective-permute-start.16 = (f32[4,16,768]{2,1,0:T(8,128)S(1)}, f32[4,16,768]{2,1,0:T(8,128)S(1)}, u32[]{:S(2)}, u32[]{:S(2)}) collective-permute-start(f32[4,16,768]{2,1,0:T(8,128)S(1)} %constant_dynamic-slice_fusion.1), channel_id=1, source_target_pairs={{0,64},{64,0},{1,65},{65,1},{2,66},{66,2},{3,67},{67,3},{4,68},{68... | collective-permute-start | bytes 589832 | tf_op jit(solution)/shard_map/ppermute | solution.py:344
  183.7 4.8 %collective-permute-start.17 = (f32[4,16,768]{2,1,0:T(8,128)S(1)}, f32[4,16,768]{2,1,0:T(8,128)S(1)}, u32[]{:S(2)}, u32[]{:S(2)}) collective-permute-start(f32[4,16,768]{2,1,0:T(8,128)S(1)} %dynamic-slice_add_fusion.1), channel_id=1, source_target_pairs={{0,256},{128,384},{256,0},{384,128},{1,257},{129,385},{257,1},{385... | collective-permute-start | bytes 589832 | tf_op jit(solution)/shard_map/ppermute | solution.py:348
  188.5 2.3 collective-permute-start.18
  190.8 4.2 %collective-permute-start.19 = (f32[4,16,768]{2,1,0:T(8,128)S(1)}, f32[4,16,768]{2,1,0:T(8,128)S(1)}, u32[]{:S(2)}, u32[]{:S(2)}) collective-permute-start(f32[4,16,768]{2,1,0:T(8,128)S(1)} %dynamic-slice_add_fusion.1), channel_id=1, source_target_pairs={{0,384},{128,0},{256,128},{384,256},{1,385},{129,1},{257,129},{385... | collective-permute-start | bytes 589832 | tf_op jit(solution)/shard_map/ppermute | solution.py:348
  195.0 2.6 collective-permute-done.18
  198.3 4.7 %collective-permute-start.20 = (f32[4,16,768]{2,1,0:T(8,128)S(1)}, f32[4,16,768]{2,1,0:T(8,128)S(1)}, u32[]{:S(2)}, u32[]{:S(2)}) collective-permute-start(f32[4,16,768]{2,1,0:T(8,128)S(1)} %add_add_fusion.1), channel_id=1, source_target_pairs={{0,32},{16,48},{32,0},{48,16},{1,33},{17,49},{33,1},{49,17},{2,34}... | collective-permute-start | bytes 589832 | tf_op jit(solution)/shard_map/ppermute | solution.py:348
  203.0 2.3 collective-permute-start.21
  205.2 4.2 %collective-permute-start.22 = (f32[4,16,768]{2,1,0:T(8,128)S(1)}, f32[4,16,768]{2,1,0:T(8,128)S(1)}, u32[]{:S(2)}, u32[]{:S(2)}) collective-permute-start(f32[4,16,768]{2,1,0:T(8,128)S(1)} %add_add_fusion.1), channel_id=1, source_target_pairs={{0,48},{16,0},{32,16},{48,32},{1,49},{17,1},{33,17},{49,33},{2,50}... | collective-permute-start | bytes 589832 | tf_op jit(solution)/shard_map/ppermute | solution.py:348
  209.5 1.8 collective-permute-done.21
  212.1 5.2 %collective-permute-start.23 = (f32[4,16,768]{2,1,0:T(8,128)S(1)}, f32[4,16,768]{2,1,0:T(8,128)S(1)}, u32[]{:S(2)}, u32[]{:S(2)}) collective-permute-start(f32[4,16,768]{2,1,0:T(8,128)S(1)} %add_add_fusion.mine_ref), channel_id=1, source_target_pairs={{0,64},{64,0},{1,65},{65,1},{2,66},{66,2},{3,67},{67,3},{4,68},{68... | collective-permute-start | bytes 589832 | tf_op jit(solution)/shard_map/ppermute | solution.py:415
  218.2 3.5 %basis.1.basis_ref = f32[4,32,768]{2,1,0:T(8,128)S(1)} custom-call(s32[1]{0:T(128)} %bitcast.9.c_ref, f32[4,16,768]{2,1,0:T(8,128)S(1)} %add_add_fusion.mine_ref, f32[4,16,768]{2,1,0:T(8,128)S(1)} %collective-permute-done.23.other_ref), custom_call_target="tpu_custom_call" | custom-call | flops 10000000 | bytes 1048576 | tf_op jit(solution)/shard_map/basis/pallas_call | solution.py:330
  221.8 1.5 copy-done.5
  223.3 3.7 %right.1 = f32[4,32,2048]{2,1,0:T(8,128)S(1)} custom-call(f32[4,32,768]{2,1,0:T(8,128)S(1)} %basis.1.basis_ref, bf16[4,320,768]{2,1,0:T(8,128)(2,1)S(1)} %copy-done.5, bf16[320,320]{1,0:T(8,128)(2,1)S(1)} %copy-done.7, bf16[4,80,2048]{2,1,0:T(8,128)(2,1)S(1)} %copy-done, bf16[4,80,2048]{2,1,0:T(8,128)(2,1)S(1)} %copy-done.1, ...), custom_call_target="tpu_custom_call" | custom-call | flops 1000000000 | bytes 9437184 | tf_op jit(solution)/shard_map/right/pallas_call | solution.py:248
  228.1 2.3 collective-permute-start.24
  230.4 1.5 collective-permute-done.24
  231.9 1.1 dynamic-slice_add_fusion
  233.0 3.6 %collective-permute-start.25 = (f32[16,2048]{1,0:T(8,128)S(1)}, f32[16,2048]{1,0:T(8,128)S(1)}, u32[]{:S(2)}, u32[]{:S(2)}) collective-permute-start(f32[16,2048]{1,0:T(8,128)S(1)} %get-tuple-element.55), channel_id=1, source_target_pairs={{0,32},{16,48},{32,0},{48,16},{1,33},{17,49},{33,1},{49,17},{2,34}... | collective-permute-start | bytes 393224 | tf_op jit(solution)/shard_map/ppermute | solution.py:357
  236.6 4.3 %collective-permute-start.26 = (f32[16,2048]{1,0:T(8,128)S(1)}, f32[16,2048]{1,0:T(8,128)S(1)}, u32[]{:S(2)}, u32[]{:S(2)}) collective-permute-start(f32[16,2048]{1,0:T(8,128)S(1)} %get-tuple-element.57), channel_id=1, source_target_pairs={{0,16},{16,32},{32,48},{48,0},{1,17},{17,33},{33,49},{49,1},{2,18}... | collective-permute-start | bytes 393224 | tf_op jit(solution)/shard_map/ppermute | solution.py:357
  240.8 2.2 collective-permute-start.27
  244.2 2.8 collective-permute-done.27
  247.0 3.4 %collective-permute-start.28 = (f32[16,2048]{1,0:T(8,128)S(1)}, f32[16,2048]{1,0:T(8,128)S(1)}, u32[]{:S(2)}, u32[]{:S(2)}) collective-permute-start(f32[16,2048]{1,0:T(8,128)S(1)} %fusion.7), channel_id=1, source_target_pairs={{0,256},{128,384},{256,0},{384,128},{1,257},{129,385},{257,1},{385... | collective-permute-start | bytes 393224 | tf_op jit(solution)/shard_map/ppermute | solution.py:348
  250.4 3.8 %collective-permute-start.29 = (f32[16,2048]{1,0:T(8,128)S(1)}, f32[16,2048]{1,0:T(8,128)S(1)}, u32[]{:S(2)}, u32[]{:S(2)}) collective-permute-start(f32[16,2048]{1,0:T(8,128)S(1)} %fusion.7), channel_id=1, source_target_pairs={{0,128},{128,256},{256,384},{384,0},{1,129},{129,257},{257,385},{3... | collective-permute-start | bytes 393224 | tf_op jit(solution)/shard_map/ppermute | solution.py:348
  254.2 2.7 collective-permute-start.30
  257.9 2.2 collective-permute-done.30
  260.1 5.2 %collective-permute-start.31 = (f32[16,2048]{1,0:T(8,128)S(1)}, f32[16,2048]{1,0:T(8,128)S(1)}, u32[]{:S(2)}, u32[]{:S(2)}) collective-permute-start(f32[16,2048]{1,0:T(8,128)S(1)} %add_add_fusion.2), channel_id=1, source_target_pairs={{0,64},{64,0},{1,65},{65,1},{2,66},{66,2},{3,67},{67,3},{4,68},{68... | collective-permute-start | bytes 393224 | tf_op jit(solution)/shard_map/ppermute | solution.py:359
  266.9 5.4 %spread.1 = bf16[128,8,768]{2,1,0:T(8,128)(2,1)} custom-call(s32[1024,1]{1,0:T(8,128)S(1)} %reshape.39.place_ref, bf16[1280,768]{1,0:T(8,128)(2,1)} %bitcast.8.rows_ref), custom_call_target="tpu_custom_call" | custom-call | flops 2000000000 | bytes 4194304 | tf_op jit(solution)/shard_map/spread/pallas_call | solution.py:275
  (93 shorter events, 13.9 us)
Async XLA Ops:
  7.2 2.9 %copy-start.11 = (bf16[128,2048]{1,0:T(8,128)(2,1)S(1)}, bf16[128,2048]{1,0:T(8,128)(2,1)}, u32[]{:S(2)}) copy-start(bf16[128,2048]{1,0:T(8,128)(2,1)} %refs_0_.1) | copy-start | bytes 1572868
  7.2 16.8 %copy-start.22 = (s32[128,8]{0,1:T(8,128)S(1)}, s32[128,8]{0,1:T(8,128)}, u32[]{:S(2)}) copy-start(s32[128,8]{0,1:T(8,128)} %param.7) | copy-start | bytes 12292
  7.2 17.1 %copy-start.23 = (f32[128,8]{0,1:T(8,128)S(1)}, f32[128,8]{0,1:T(8,128)}, u32[]{:S(2)}) copy-start(f32[128,8]{0,1:T(8,128)} %param.8) | copy-start | bytes 12292
  7.2 122.2 %all-gather.2.cloned.1.call-start = ((), (), s32[]{:S(2)}) async-start(), calls=%async_computation.3 | async-start | bytes 15138816 | tf_op jit(solution)/shard_map/all_gather | solution.py:371
  10.0 35.3 %collective-permute-start = (bf16[128,2048]{1,0:T(8,128)(2,1)S(1)}, bf16[128,2048]{1,0:T(8,128)(2,1)S(1)}, u32[]{:S(2)}, u32[]{:S(2)}) collective-permute-start(bf16[128,2048]{1,0:T(8,128)(2,1)S(1)} %copy-done.11), channel_id=1, source_target_pairs={{0,1},{1,2},{2,3},{3,4},{4,5},{5,6},{6,7},{7,8},{8,9},{9,10},{10,1... | collective-permute-start | bytes 1572872 | tf_op jit(solution)/shard_map/ppermute | solution.py:384
  14.4 20.1 %collective-permute-start.1 = (bf16[128,2048]{1,0:T(8,128)(2,1)S(1)}, bf16[128,2048]{1,0:T(8,128)(2,1)S(1)}, u32[]{:S(2)}, u32[]{:S(2)}) collective-permute-start(bf16[128,2048]{1,0:T(8,128)(2,1)S(1)} %copy-done.11), channel_id=1, source_target_pairs={{0,15},{1,0},{2,1},{3,2},{4,3},{5,4},{6,5},{7,6},{8,7},{9,8},{10,9... | collective-permute-start | bytes 1572872 | tf_op jit(solution)/shard_map/ppermute | solution.py:385
  25.0 20.4 %all-to-all-start = ((f32[16,16,128]{2,1,0:T(8,128)}), f32[16,16,128]{2,1,0:T(8,128)S(1)}, u32[]{:S(2)}, u32[]{:S(2)}) async-start(f32[16,16,128]{2,1,0:T(8,128)} %broadcast_in_dim.38), calls=%async_computation | async-start | bytes 262144 | tf_op jit(solution)/shard_map/all_to_all | solution.py:374
  34.5 34.3 %copy-start.14 = (bf16[128,2048]{1,0:T(8,128)(2,1)}, bf16[128,2048]{1,0:T(8,128)(2,1)S(1)}, u32[]{:S(2)}) copy-start(bf16[128,2048]{1,0:T(8,128)(2,1)S(1)} %collective-permute-done.1.refs_2_) | copy-start | bytes 1572868
  34.5 16.9 %collective-permute-start.3 = (bf16[128,2048]{1,0:T(8,128)(2,1)S(1)}, bf16[128,2048]{1,0:T(8,128)(2,1)S(1)}, u32[]{:S(2)}, u32[]{:S(2)}) collective-permute-start(bf16[128,2048]{1,0:T(8,128)(2,1)S(1)} %collective-permute-done.1.refs_2_), channel_id=1, source_target_pairs={{0,15},{1,0},{2,1},{3,2},{4,3},{5,4},{6,5},{7,6},{8,7},{9,8},{10,9... | collective-permute-start | bytes 1572872 | tf_op jit(solution)/shard_map/ppermute | solution.py:385
  45.3 8.9 %copy-start.10 = (f32[16,16,128]{2,1,0:T(8,128)}, f32[16,16,128]{2,1,0:T(8,128)S(1)}, u32[]{:S(2)}) copy-start(f32[16,16,128]{2,1,0:T(8,128)S(1)} %all-to-all-done.meta_ref) | copy-start | bytes 393220
  45.3 23.4 %copy-start.13 = (bf16[128,2048]{1,0:T(8,128)(2,1)}, bf16[128,2048]{1,0:T(8,128)(2,1)S(1)}, u32[]{:S(2)}) copy-start(bf16[128,2048]{1,0:T(8,128)(2,1)S(1)} %collective-permute-done.refs_1_) | copy-start | bytes 1572868
  45.3 12.9 %collective-permute-start.2 = (bf16[128,2048]{1,0:T(8,128)(2,1)S(1)}, bf16[128,2048]{1,0:T(8,128)(2,1)S(1)}, u32[]{:S(2)}, u32[]{:S(2)}) collective-permute-start(bf16[128,2048]{1,0:T(8,128)(2,1)S(1)} %collective-permute-done.refs_1_), channel_id=1, source_target_pairs={{0,1},{1,2},{2,3},{3,4},{4,5},{5,6},{6,7},{7,8},{8,9},{9,10},{10,1... | collective-permute-start | bytes 1572872 | tf_op jit(solution)/shard_map/ppermute | solution.py:384
  51.4 20.8 %copy-start.12 = (bf16[128,2048]{1,0:T(8,128)(2,1)}, bf16[128,2048]{1,0:T(8,128)(2,1)S(1)}, u32[]{:S(2)}) copy-start(bf16[128,2048]{1,0:T(8,128)(2,1)S(1)} %collective-permute-done.3.refs_0_) | copy-start | bytes 1572868
  51.4 15.5 %collective-permute-start.5 = (bf16[128,2048]{1,0:T(8,128)(2,1)S(1)}, bf16[128,2048]{1,0:T(8,128)(2,1)S(1)}, u32[]{:S(2)}, u32[]{:S(2)}) collective-permute-start(bf16[128,2048]{1,0:T(8,128)(2,1)S(1)} %collective-permute-done.3.refs_0_), channel_id=1, source_target_pairs={{0,15},{1,0},{2,1},{3,2},{4,3},{5,4},{6,5},{7,6},{8,7},{9,8},{10,9... | collective-permute-start | bytes 1572872 | tf_op jit(solution)/shard_map/ppermute | solution.py:385
  58.2 10.6 %copy-start.20 = (bf16[128,2048]{1,0:T(8,128)(2,1)}, bf16[128,2048]{1,0:T(8,128)(2,1)S(1)}, u32[]{:S(2)}) copy-start(bf16[128,2048]{1,0:T(8,128)(2,1)S(1)} %collective-permute-done.2.refs_3_) | copy-start | bytes 1572868
  58.2 14.0 %collective-permute-start.4 = (bf16[128,2048]{1,0:T(8,128)(2,1)S(1)}, bf16[128,2048]{1,0:T(8,128)(2,1)S(1)}, u32[]{:S(2)}, u32[]{:S(2)}) collective-permute-start(bf16[128,2048]{1,0:T(8,128)(2,1)S(1)} %collective-permute-done.2.refs_3_), channel_id=1, source_target_pairs={{0,1},{1,2},{2,3},{3,4},{4,5},{5,6},{6,7},{7,8},{8,9},{9,10},{10,1... | collective-permute-start | bytes 1572872 | tf_op jit(solution)/shard_map/ppermute | solution.py:384
  66.9 5.3 %copy-start.17 = (bf16[128,2048]{1,0:T(8,128)(2,1)}, bf16[128,2048]{1,0:T(8,128)(2,1)S(1)}, u32[]{:S(2)}) copy-start(bf16[128,2048]{1,0:T(8,128)(2,1)S(1)} %collective-permute-done.5.refs_2_) | copy-start | bytes 1572868
  66.9 14.9 %collective-permute-start.7 = (bf16[128,2048]{1,0:T(8,128)(2,1)S(1)}, bf16[128,2048]{1,0:T(8,128)(2,1)S(1)}, u32[]{:S(2)}, u32[]{:S(2)}) collective-permute-start(bf16[128,2048]{1,0:T(8,128)(2,1)S(1)} %collective-permute-done.5.refs_2_), channel_id=1, source_target_pairs={{0,15},{1,0},{2,1},{3,2},{4,3},{5,4},{6,5},{7,6},{8,7},{9,8},{10,9... | collective-permute-start | bytes 1572872 | tf_op jit(solution)/shard_map/ppermute | solution.py:385
  72.2 25.5 %copy-start.19 = (bf16[128,2048]{1,0:T(8,128)(2,1)}, bf16[128,2048]{1,0:T(8,128)(2,1)S(1)}, u32[]{:S(2)}) copy-start(bf16[128,2048]{1,0:T(8,128)(2,1)S(1)} %collective-permute-done.4.refs_1_) | copy-start | bytes 1572868
  72.2 13.5 %collective-permute-start.6 = (bf16[128,2048]{1,0:T(8,128)(2,1)S(1)}, bf16[128,2048]{1,0:T(8,128)(2,1)S(1)}, u32[]{:S(2)}, u32[]{:S(2)}) collective-permute-start(bf16[128,2048]{1,0:T(8,128)(2,1)S(1)} %collective-permute-done.4.refs_1_), channel_id=1, source_target_pairs={{0,1},{1,2},{2,3},{3,4},{4,5},{5,6},{6,7},{7,8},{8,9},{9,10},{10,1... | collective-permute-start | bytes 1572872 | tf_op jit(solution)/shard_map/ppermute | solution.py:384
  81.7 19.6 %copy-start.16 = (bf16[128,2048]{1,0:T(8,128)(2,1)}, bf16[128,2048]{1,0:T(8,128)(2,1)S(1)}, u32[]{:S(2)}) copy-start(bf16[128,2048]{1,0:T(8,128)(2,1)S(1)} %collective-permute-done.7.refs_0_) | copy-start | bytes 1572868
  81.7 14.1 %collective-permute-start.9 = (bf16[128,2048]{1,0:T(8,128)(2,1)S(1)}, bf16[128,2048]{1,0:T(8,128)(2,1)S(1)}, u32[]{:S(2)}, u32[]{:S(2)}) collective-permute-start(bf16[128,2048]{1,0:T(8,128)(2,1)S(1)} %collective-permute-done.7.refs_0_), channel_id=1, source_target_pairs={{0,15},{1,0},{2,1},{3,2},{4,3},{5,4},{6,5},{7,6},{8,7},{9,8},{10,9... | collective-permute-start | bytes 1572872 | tf_op jit(solution)/shard_map/ppermute | solution.py:385
  85.8 12.0 %copy-start.21 = (bf16[128,2048]{1,0:T(8,128)(2,1)}, bf16[128,2048]{1,0:T(8,128)(2,1)S(1)}, u32[]{:S(2)}) copy-start(bf16[128,2048]{1,0:T(8,128)(2,1)S(1)} %collective-permute-done.6.refs_3_) | copy-start | bytes 1572868
  85.8 15.5 %collective-permute-start.8 = (bf16[128,2048]{1,0:T(8,128)(2,1)S(1)}, bf16[128,2048]{1,0:T(8,128)(2,1)}, u32[]{:S(2)}, u32[]{:S(2)}) collective-permute-start(bf16[128,2048]{1,0:T(8,128)(2,1)S(1)} %collective-permute-done.6.refs_3_), channel_id=1, source_target_pairs={{0,1},{1,2},{2,3},{3,4},{4,5},{5,6},{6,7},{7,8},{8,9},{9,10},{10,1... | collective-permute-start | bytes 1572872 | tf_op jit(solution)/shard_map/ppermute | solution.py:384
  95.8 5.5 %copy-start.18 = (bf16[128,2048]{1,0:T(8,128)(2,1)}, bf16[128,2048]{1,0:T(8,128)(2,1)S(1)}, u32[]{:S(2)}) copy-start(bf16[128,2048]{1,0:T(8,128)(2,1)S(1)} %collective-permute-done.9.refs_2_) | copy-start | bytes 1572868
  95.8 13.1 %collective-permute-start.11 = (bf16[128,2048]{1,0:T(8,128)(2,1)S(1)}, bf16[128,2048]{1,0:T(8,128)(2,1)S(1)}, u32[]{:S(2)}, u32[]{:S(2)}) collective-permute-start(bf16[128,2048]{1,0:T(8,128)(2,1)S(1)} %collective-permute-done.9.refs_2_), channel_id=1, source_target_pairs={{0,15},{1,0},{2,1},{3,2},{4,3},{5,4},{6,5},{7,6},{8,7},{9,8},{10,9... | collective-permute-start | bytes 1572872 | tf_op jit(solution)/shard_map/ppermute | solution.py:385
  101.3 13.4 %collective-permute-start.10 = (bf16[128,2048]{1,0:T(8,128)(2,1)}, bf16[128,2048]{1,0:T(8,128)(2,1)}, u32[]{:S(2)}, u32[]{:S(2)}) collective-permute-start(bf16[128,2048]{1,0:T(8,128)(2,1)} %collective-permute-done.8.refs_1_), channel_id=1, source_target_pairs={{0,1},{1,2},{2,3},{3,4},{4,5},{5,6},{6,7},{7,8},{8,9},{9,10},{10,1... | collective-permute-start | bytes 1572872 | tf_op jit(solution)/shard_map/ppermute | solution.py:384
  104.9 45.6 %all-to-all-start.2 = ((bf16[4,320,768]{2,1,0:T(8,128)(2,1)}), bf16[4,320,768]{2,1,0:T(8,128)(2,1)S(1)}, u32[]{:S(2)}, u32[]{:S(2)}) async-start(bf16[4,320,768]{2,1,0:T(8,128)(2,1)} %bitcast.44), calls=%async_computation.2 | async-start | bytes 3932160 | tf_op jit(solution)/shard_map/all_to_all | solution.py:377
  108.9 12.1 %copy-start.15 = (bf16[128,2048]{1,0:T(8,128)(2,1)}, bf16[128,2048]{1,0:T(8,128)(2,1)S(1)}, u32[]{:S(2)}) copy-start(bf16[128,2048]{1,0:T(8,128)(2,1)S(1)} %collective-permute-done.11.refs_0_) | copy-start | bytes 1572868
  108.9 12.5 %collective-permute-start.13 = (bf16[128,2048]{1,0:T(8,128)(2,1)S(1)}, bf16[128,2048]{1,0:T(8,128)(2,1)S(1)}, u32[]{:S(2)}, u32[]{:S(2)}) collective-permute-start(bf16[128,2048]{1,0:T(8,128)(2,1)S(1)} %collective-permute-done.11.refs_0_), channel_id=1, source_target_pairs={{0,15},{1,0},{2,1},{3,2},{4,3},{5,4},{6,5},{7,6},{8,7},{9,8},{10,9... | collective-permute-start | bytes 1572872 | tf_op jit(solution)/shard_map/ppermute | solution.py:385
  114.7 12.3 %collective-permute-start.12 = (bf16[128,2048]{1,0:T(8,128)(2,1)}, bf16[128,2048]{1,0:T(8,128)(2,1)S(1)}, u32[]{:S(2)}, u32[]{:S(2)}) collective-permute-start(bf16[128,2048]{1,0:T(8,128)(2,1)} %collective-permute-done.10.refs_3_), channel_id=1, source_target_pairs={{0,1},{1,2},{2,3},{3,4},{4,5},{5,6},{6,7},{7,8},{8,9},{9,10},{10,1... | collective-permute-start | bytes 1572872 | tf_op jit(solution)/shard_map/ppermute | solution.py:384
  121.5 13.5 %copy-start.8 = (bf16[128,2048]{1,0:T(8,128)(2,1)}, bf16[128,2048]{1,0:T(8,128)(2,1)S(1)}, u32[]{:S(2)}) copy-start(bf16[128,2048]{1,0:T(8,128)(2,1)S(1)} %collective-permute-done.13.refs_2_) | copy-start | bytes 1572868
  121.5 13.5 %collective-permute-start.15 = (bf16[64,2048]{1,0:T(8,128)(2,1)S(1)}, bf16[64,2048]{1,0:T(8,128)(2,1)}, u32[]{:S(2)}, u32[]{:S(2)}) collective-permute-start(bf16[64,2048]{1,0:T(8,128)(2,1)S(1)} %slice.7), channel_id=1, source_target_pairs={{0,15},{1,0},{2,1},{3,2},{4,3},{5,4},{6,5},{7,6},{8,7},{9,8},{10,9... | collective-permute-start | bytes 786440 | tf_op jit(solution)/shard_map/ppermute | solution.py:405
  127.0 8.0 %copy-start.9 = (bf16[128,2048]{1,0:T(8,128)(2,1)}, bf16[128,2048]{1,0:T(8,128)(2,1)S(1)}, u32[]{:S(2)}) copy-start(bf16[128,2048]{1,0:T(8,128)(2,1)S(1)} %collective-permute-done.12.refs_1_) | copy-start | bytes 1572868
  127.0 8.4 %collective-permute-start.14 = (bf16[64,2048]{1,0:T(8,128)(2,1)S(1)}, bf16[64,2048]{1,0:T(8,128)(2,1)}, u32[]{:S(2)}, u32[]{:S(2)}) collective-permute-start(bf16[64,2048]{1,0:T(8,128)(2,1)S(1)} %slice.6), channel_id=1, source_target_pairs={{0,1},{1,2},{2,3},{3,4},{4,5},{5,6},{6,7},{7,8},{8,9},{9,10},{10,1... | collective-permute-start | bytes 786440 | tf_op jit(solution)/shard_map/ppermute | solution.py:404
  150.5 1.3 copy-start.4
  151.8 115.1 %all-to-all-start.1 = ((bf16[16,80,768]{2,1,0:T(8,128)(2,1)}), bf16[16,80,768]{2,1,0:T(8,128)(2,1)}, u32[]{:S(2)}, u32[]{:S(2)}) async-start(bf16[16,80,768]{2,1,0:T(8,128)(2,1)} %back.1), calls=%async_computation.1 | async-start | bytes 3932160 | tf_op jit(solution)/shard_map/all_to_all | solution.py:411
  166.4 55.3 %copy-start.2 = (bf16[4,80,2048]{2,1,0:T(8,128)(2,1)S(1)}, bf16[4,80,2048]{2,1,0:T(8,128)(2,1)}, u32[]{:S(2)}) copy-start(bf16[4,80,2048]{2,1,0:T(8,128)(2,1)} %rows.6.refs_2_) | copy-start | bytes 3932164
  166.4 55.3 %copy-start.3 = (bf16[4,80,2048]{2,1,0:T(8,128)(2,1)S(1)}, bf16[4,80,2048]{2,1,0:T(8,128)(2,1)}, u32[]{:S(2)}) copy-start(bf16[4,80,2048]{2,1,0:T(8,128)(2,1)} %rows.7.refs_3_.rows_ref) | copy-start | bytes 3932164
  172.9 9.8 %collective-permute-start.16 = (f32[4,16,768]{2,1,0:T(8,128)S(1)}, f32[4,16,768]{2,1,0:T(8,128)S(1)}, u32[]{:S(2)}, u32[]{:S(2)}) collective-permute-start(f32[4,16,768]{2,1,0:T(8,128)S(1)} %constant_dynamic-slice_fusion.1), channel_id=1, source_target_pairs={{0,64},{64,0},{1,65},{65,1},{2,66},{66,2},{3,67},{67,3},{4,68},{68... | collective-permute-start | bytes 589832 | tf_op jit(solution)/shard_map/ppermute | solution.py:344
  181.7 40.1 %copy-start = (bf16[4,80,2048]{2,1,0:T(8,128)(2,1)S(1)}, bf16[4,80,2048]{2,1,0:T(8,128)(2,1)}, u32[]{:S(2)}) copy-start(bf16[4,80,2048]{2,1,0:T(8,128)(2,1)} %rows.4.refs_0_) | copy-start | bytes 3932164
  181.7 40.1 %copy-start.1 = (bf16[4,80,2048]{2,1,0:T(8,128)(2,1)S(1)}, bf16[4,80,2048]{2,1,0:T(8,128)(2,1)}, u32[]{:S(2)}) copy-start(bf16[4,80,2048]{2,1,0:T(8,128)(2,1)} %rows.5.refs_1_) | copy-start | bytes 3932164
  181.7 40.1 %copy-start.7 = (bf16[320,320]{1,0:T(8,128)(2,1)S(1)}, bf16[320,320]{1,0:T(8,128)(2,1)}, u32[]{:S(2)}) copy-start(bf16[320,320]{1,0:T(8,128)(2,1)} %get-tuple-element.47.order_ref) | copy-start | bytes 614404
  183.7 11.3 %collective-permute-start.17 = (f32[4,16,768]{2,1,0:T(8,128)S(1)}, f32[4,16,768]{2,1,0:T(8,128)S(1)}, u32[]{:S(2)}, u32[]{:S(2)}) collective-permute-start(f32[4,16,768]{2,1,0:T(8,128)S(1)} %dynamic-slice_add_fusion.1), channel_id=1, source_target_pairs={{0,256},{128,384},{256,0},{384,128},{1,257},{129,385},{257,1},{385... | collective-permute-start | bytes 589832 | tf_op jit(solution)/shard_map/ppermute | solution.py:348
  188.5 9.1 %collective-permute-start.18 = (f32[4,16,768]{2,1,0:T(8,128)S(1)}, f32[4,16,768]{2,1,0:T(8,128)S(1)}, u32[]{:S(2)}, u32[]{:S(2)}) collective-permute-start(f32[4,16,768]{2,1,0:T(8,128)S(1)} %dynamic-slice_add_fusion.1), channel_id=1, source_target_pairs={{0,128},{128,256},{256,384},{384,0},{1,129},{129,257},{257,385},{3... | collective-permute-start | bytes 589832 | tf_op jit(solution)/shard_map/ppermute | solution.py:348
  190.8 7.5 %collective-permute-start.19 = (f32[4,16,768]{2,1,0:T(8,128)S(1)}, f32[4,16,768]{2,1,0:T(8,128)S(1)}, u32[]{:S(2)}, u32[]{:S(2)}) collective-permute-start(f32[4,16,768]{2,1,0:T(8,128)S(1)} %dynamic-slice_add_fusion.1), channel_id=1, source_target_pairs={{0,384},{128,0},{256,128},{384,256},{1,385},{129,1},{257,129},{385... | collective-permute-start | bytes 589832 | tf_op jit(solution)/shard_map/ppermute | solution.py:348
  198.3 11.2 %collective-permute-start.20 = (f32[4,16,768]{2,1,0:T(8,128)S(1)}, f32[4,16,768]{2,1,0:T(8,128)S(1)}, u32[]{:S(2)}, u32[]{:S(2)}) collective-permute-start(f32[4,16,768]{2,1,0:T(8,128)S(1)} %add_add_fusion.1), channel_id=1, source_target_pairs={{0,32},{16,48},{32,0},{48,16},{1,33},{17,49},{33,1},{49,17},{2,34}... | collective-permute-start | bytes 589832 | tf_op jit(solution)/shard_map/ppermute | solution.py:348
  203.0 8.3 %collective-permute-start.21 = (f32[4,16,768]{2,1,0:T(8,128)S(1)}, f32[4,16,768]{2,1,0:T(8,128)S(1)}, u32[]{:S(2)}, u32[]{:S(2)}) collective-permute-start(f32[4,16,768]{2,1,0:T(8,128)S(1)} %add_add_fusion.1), channel_id=1, source_target_pairs={{0,16},{16,32},{32,48},{48,0},{1,17},{17,33},{33,49},{49,1},{2,18}... | collective-permute-start | bytes 589832 | tf_op jit(solution)/shard_map/ppermute | solution.py:348
  205.2 6.8 %collective-permute-start.22 = (f32[4,16,768]{2,1,0:T(8,128)S(1)}, f32[4,16,768]{2,1,0:T(8,128)S(1)}, u32[]{:S(2)}, u32[]{:S(2)}) collective-permute-start(f32[4,16,768]{2,1,0:T(8,128)S(1)} %add_add_fusion.1), channel_id=1, source_target_pairs={{0,48},{16,0},{32,16},{48,32},{1,49},{17,1},{33,17},{49,33},{2,50}... | collective-permute-start | bytes 589832 | tf_op jit(solution)/shard_map/ppermute | solution.py:348
  212.1 6.1 %collective-permute-start.23 = (f32[4,16,768]{2,1,0:T(8,128)S(1)}, f32[4,16,768]{2,1,0:T(8,128)S(1)}, u32[]{:S(2)}, u32[]{:S(2)}) collective-permute-start(f32[4,16,768]{2,1,0:T(8,128)S(1)} %add_add_fusion.mine_ref), channel_id=1, source_target_pairs={{0,64},{64,0},{1,65},{65,1},{2,66},{66,2},{3,67},{67,3},{4,68},{68... | collective-permute-start | bytes 589832 | tf_op jit(solution)/shard_map/ppermute | solution.py:415
  221.8 1.5 copy-start.5
  227.1 1.0 copy-start.6
  228.1 3.8 %collective-permute-start.24 = (f32[4,16,2048]{2,1,0:T(8,128)S(1)}, f32[4,16,2048]{2,1,0:T(8,128)S(1)}, u32[]{:S(2)}, u32[]{:S(2)}) collective-permute-start(f32[4,16,2048]{2,1,0:T(8,128)S(1)} %constant_dynamic-slice_fusion), channel_id=1, source_target_pairs={{0,64},{64,0},{1,65},{65,1},{2,66},{66,2},{3,67},{67,3},{4,68},{68... | collective-permute-start | bytes 1572872 | tf_op jit(solution)/shard_map/ppermute | solution.py:344
  233.0 10.1 %collective-permute-start.25 = (f32[16,2048]{1,0:T(8,128)S(1)}, f32[16,2048]{1,0:T(8,128)S(1)}, u32[]{:S(2)}, u32[]{:S(2)}) collective-permute-start(f32[16,2048]{1,0:T(8,128)S(1)} %get-tuple-element.55), channel_id=1, source_target_pairs={{0,32},{16,48},{32,0},{48,16},{1,33},{17,49},{33,1},{49,17},{2,34}... | collective-permute-start | bytes 393224 | tf_op jit(solution)/shard_map/ppermute | solution.py:357
  236.6 7.6 %collective-permute-start.26 = (f32[16,2048]{1,0:T(8,128)S(1)}, f32[16,2048]{1,0:T(8,128)S(1)}, u32[]{:S(2)}, u32[]{:S(2)}) collective-permute-start(f32[16,2048]{1,0:T(8,128)S(1)} %get-tuple-element.57), channel_id=1, source_target_pairs={{0,16},{16,32},{32,48},{48,0},{1,17},{17,33},{33,49},{49,1},{2,18}... | collective-permute-start | bytes 393224 | tf_op jit(solution)/shard_map/ppermute | solution.py:357
  240.8 6.1 %collective-permute-start.27 = (f32[16,2048]{1,0:T(8,128)S(1)}, f32[16,2048]{1,0:T(8,128)S(1)}, u32[]{:S(2)}, u32[]{:S(2)}) collective-permute-start(f32[16,2048]{1,0:T(8,128)S(1)} %get-tuple-element.56), channel_id=1, source_target_pairs={{0,48},{16,0},{32,16},{48,32},{1,49},{17,1},{33,17},{49,33},{2,50}... | collective-permute-start | bytes 393224 | tf_op jit(solution)/shard_map/ppermute | solution.py:357
  247.0 9.9 %collective-permute-start.28 = (f32[16,2048]{1,0:T(8,128)S(1)}, f32[16,2048]{1,0:T(8,128)S(1)}, u32[]{:S(2)}, u32[]{:S(2)}) collective-permute-start(f32[16,2048]{1,0:T(8,128)S(1)} %fusion.7), channel_id=1, source_target_pairs={{0,256},{128,384},{256,0},{384,128},{1,257},{129,385},{257,1},{385... | collective-permute-start | bytes 393224 | tf_op jit(solution)/shard_map/ppermute | solution.py:348
  250.4 7.5 %collective-permute-start.29 = (f32[16,2048]{1,0:T(8,128)S(1)}, f32[16,2048]{1,0:T(8,128)S(1)}, u32[]{:S(2)}, u32[]{:S(2)}) collective-permute-start(f32[16,2048]{1,0:T(8,128)S(1)} %fusion.7), channel_id=1, source_target_pairs={{0,128},{128,256},{256,384},{384,0},{1,129},{129,257},{257,385},{3... | collective-permute-start | bytes 393224 | tf_op jit(solution)/shard_map/ppermute | solution.py:348
  254.2 5.9 %collective-permute-start.30 = (f32[16,2048]{1,0:T(8,128)S(1)}, f32[16,2048]{1,0:T(8,128)S(1)}, u32[]{:S(2)}, u32[]{:S(2)}) collective-permute-start(f32[16,2048]{1,0:T(8,128)S(1)} %fusion.7), channel_id=1, source_target_pairs={{0,384},{128,0},{256,128},{384,256},{1,385},{129,1},{257,129},{385... | collective-permute-start | bytes 393224 | tf_op jit(solution)/shard_map/ppermute | solution.py:348
  260.1 6.1 %collective-permute-start.31 = (f32[16,2048]{1,0:T(8,128)S(1)}, f32[16,2048]{1,0:T(8,128)S(1)}, u32[]{:S(2)}, u32[]{:S(2)}) collective-permute-start(f32[16,2048]{1,0:T(8,128)S(1)} %add_add_fusion.2), channel_id=1, source_target_pairs={{0,64},{64,0},{1,65},{65,1},{2,66},{66,2},{3,67},{67,3},{4,68},{68... | collective-permute-start | bytes 393224 | tf_op jit(solution)/shard_map/ppermute | solution.py:359
Sparse Core Ops, SparseCore 0:
  11.2 88.8 all-gather.1

commit v5 on v4

--- a/solution.py
+++ b/solution.py
@@ -394,8 +394,11 @@
             rows.append(make_rows(g, picks, scale, blocks[g * GROUP : (g + 1) * GROUP]))
             beside = [rows[g]]
         now = (right, left)
-        right, _, *beside = lax.optimization_barrier((right, before[1], *beside))
-        left, _ = lax.optimization_barrier((left, before[0]))
+        if step < 6:
+            right, _, *beside = lax.optimization_barrier((right, before[1], *beside))
+            left, _ = lax.optimization_barrier((left, before[0]))
+        else:
+            right, left, *beside = lax.optimization_barrier((right, left, *beside))
         if step == 1:
             meta = beside[0]
         blocks += [*now]

time: 281 us -> 275 us (0.979)
  blocking collectives: 0 us -> 20.3 us
  waiting for transfers between devices: 51 us -> 35.5 us
  starting transfers between devices: 148 us -> 138 us
    all_to_all x0 -> x1, blocking collectives: none -> 20.3 us  [shards(): lax.all_to_all(jnp.broadcast_to(meta[None], (N_Z,) + meta.shape), 'z', sp...]
    ppermute x7, waiting for transfers between devices: 20.8 us -> 4.98 us  [shards(): left = lax.ppermute(left, 'z', turn(N_Z, -1))]
    all_to_all x1, starting transfers between devices: 14.6 us -> 6.24 us  [shards(): lax.all_to_all(back, 'z', split_axis=0, concat_axis=0, tiled=True)]
    all_to_all x1 -> x0, starting transfers between devices: 8.36 us -> none  [shards(): lax.all_to_all(jnp.broadcast_to(meta[None], (N_Z,) + meta.shape), 'z', sp...]
    ppermute x7, starting transfers between devices: 26.3 us -> 34.2 us  [shards(): left = lax.ppermute(left, 'z', turn(N_Z, -1))]
    ppermute x7, starting transfers between devices: 25.9 us -> 19.2 us  [shards(): right = lax.ppermute(right, 'z', turn(N_Z, 1))]
    ppermute x7, waiting for transfers between devices: 8.01 us -> 14.2 us  [shards(): right = lax.ppermute(right, 'z', turn(N_Z, 1))]
    all_to_all x1 -> x0, waiting for transfers between devices: 5.51 us -> none  [shards(): lax.all_to_all(jnp.broadcast_to(meta[None], (N_Z,) + meta.shape), 'z', sp...]
  transfers between devices with their start and end apart: 36 -> 35, of which waited for: 23 -> 19; matrix products, arithmetic and copies ran while one was open for 2% -> 2% of each run, Pallas kernels for 17% -> 17%
where the time goes in v5:
time: 275 us; the launch traced here: 273 us
  starting transfers between devices  138 us (50%)
  Pallas kernels  52.9 us (19%)
  waiting for transfers between devices  35.5 us (13%)
  blocking collectives  20.3 us (7%)
  between operations  14.8 us (5%)
  other arithmetic  6.44 us (2%)
  local copies, waits for them, and re-layouts  5.23 us (2%)
    ppermute x9, starting transfers between devices, ring_sum(): moved = [lax.ppermute(a, axis, turn(4, d)) for d in (2, 1, 3)]  34.2 us
    ppermute x7, starting transfers between devices, shards(): left = lax.ppermute(left, 'z', turn(N_Z, -1))  34.2 us
    all_to_all x1, blocking collectives, shards(): lax.all_to_all(jnp.broadcast_to(meta[None], (N_Z,) + meta.shape), 'z', sp...  20.3 us
    ppermute x7, starting transfers between devices, shards(): right = lax.ppermute(right, 'z', turn(N_Z, 1))  19.2 us
    ppermute x7, waiting for transfers between devices, shards(): right = lax.ppermute(right, 'z', turn(N_Z, 1))  14.2 us
    pallas_call x4, Pallas kernels, make_rows(): pl.pallas_call(rows_kernel, grid=(D // wide,), in_specs=[pl.BlockSpec((1,...  14.2 us
    ppermute x2, starting transfers between devices, half_sum(): return keep + lax.ppermute(send, 'c', turn(2, 1))  12.9 us
    pallas_call x1, Pallas kernels, back_rows(): pl.pallas_call(back_kernel, grid_spec=pltpu.PrefetchScalarGridSpec(num_sc...  11.6 us
  transfers between devices with their start and end apart: 35, of which 19 were waited for; matrix products, arithmetic and copies ran while one was open for 2% of the time, Pallas kernels for 17%

profile of v5, /device:TPU:1, one launch (start us, length us, event | category | flops | bytes accessed | tf_op | source)
XLA Modules:
  0.0 273.1 jit_solution(6615635287688799243)
XLA Ops:
  8.2 1.8 pad_maximum_fusion
  10.1 4.4 %collective-permute-start = (bf16[128,2048]{1,0:T(8,128)(2,1)S(1)}, bf16[128,2048]{1,0:T(8,128)(2,1)S(1)}, u32[]{:S(2)}, u32[]{:S(2)}) collective-permute-start(bf16[128,2048]{1,0:T(8,128)(2,1)S(1)} %copy-done.10), channel_id=1, source_target_pairs={{0,1},{1,2},{2,3},{3,4},{4,5},{5,6},{6,7},{7,8},{8,9},{9,10},{10,1... | collective-permute-start | bytes 1572872 | tf_op jit(solution)/shard_map/ppermute | solution.py:384
  14.4 9.5 %collective-permute-start.1 = (bf16[128,2048]{1,0:T(8,128)(2,1)S(1)}, bf16[128,2048]{1,0:T(8,128)(2,1)S(1)}, u32[]{:S(2)}, u32[]{:S(2)}) collective-permute-start(bf16[128,2048]{1,0:T(8,128)(2,1)S(1)} %copy-done.10), channel_id=1, source_target_pairs={{0,15},{1,0},{2,1},{3,2},{4,3},{5,4},{6,5},{7,6},{8,7},{9,8},{10,9... | collective-permute-start | bytes 1572872 | tf_op jit(solution)/shard_map/ppermute | solution.py:385
  24.3 20.3 %all_to_all.15.meta_ref = f32[16,16,128]{2,1,0:T(8,128)} all-to-all(f32[16,16,128]{2,1,0:T(8,128)S(1)} %broadcast_in_dim.38), channel_id=1, replica_groups=mesh['y'=4,'c'=2,'x'=4,'z'=16] {'z'}, dimensions={0} | all-to-all | bytes 262144 | tf_op jit(solution)/shard_map/all_to_all | solution.py:374
  44.6 2.9 %collective-permute-start.2 = (bf16[128,2048]{1,0:T(8,128)(2,1)S(1)}, bf16[128,2048]{1,0:T(8,128)(2,1)S(1)}, u32[]{:S(2)}, u32[]{:S(2)}) collective-permute-start(bf16[128,2048]{1,0:T(8,128)(2,1)S(1)} %collective-permute-done.refs_1_), channel_id=1, source_target_pairs={{0,1},{1,2},{2,3},{3,4},{4,5},{5,6},{6,7},{7,8},{8,9},{9,10},{10,1... | collective-permute-start | bytes 1572872 | tf_op jit(solution)/shard_map/ppermute | solution.py:384
  47.6 3.6 %collective-permute-start.3 = (bf16[128,2048]{1,0:T(8,128)(2,1)S(1)}, bf16[128,2048]{1,0:T(8,128)(2,1)S(1)}, u32[]{:S(2)}, u32[]{:S(2)}) collective-permute-start(bf16[128,2048]{1,0:T(8,128)(2,1)S(1)} %collective-permute-done.1.refs_2_), channel_id=1, source_target_pairs={{0,15},{1,0},{2,1},{3,2},{4,3},{5,4},{6,5},{7,6},{8,7},{9,8},{10,9... | collective-permute-start | bytes 1572872 | tf_op jit(solution)/shard_map/ppermute | solution.py:385
  51.1 3.3 %picks.1 = (bf16[4,320,512]{2,1,0:T(8,128)(2,1)}, f32[4,320,128]{2,1,0:T(8,128)}, bf16[320,320]{1,0:T(8,128)(2,1)}, bf16[320,320]{1,0:T(8,128)(2,1)}) custom-call(s32[1]{0:T(128)} %bitcast.z_ref, f32[16,16,128]{2,1,0:T(8,128)} %all_to_all.15.meta_ref), custom_call_target="tpu_custom_call" | custom-call | flops 10000000 | bytes 4194304 | tf_op jit(solution)/shard_map/picks/pallas_call | solution.py:96
  54.5 3.1 %collective-permute-done.2.refs_3_ = bf16[128,2048]{1,0:T(8,128)(2,1)S(1)} collective-permute-done((bf16[128,2048]{1,0:T(8,128)(2,1)S(1)}, bf16[128,2048]{1,0:T(8,128)(2,1)S(1)}, u32[]{:S(2)}, u32[]{:S(2)}) %collective-permute-start.2) | collective-permute-done | bytes 524320 | tf_op jit(solution)/shard_map/ppermute | solution.py:384
  57.6 1.9 collective-permute-start.4
  59.5 4.6 %collective-permute-start.5 = (bf16[128,2048]{1,0:T(8,128)(2,1)S(1)}, bf16[128,2048]{1,0:T(8,128)(2,1)S(1)}, u32[]{:S(2)}, u32[]{:S(2)}) collective-permute-start(bf16[128,2048]{1,0:T(8,128)(2,1)S(1)} %collective-permute-done.3.refs_0_), channel_id=1, source_target_pairs={{0,15},{1,0},{2,1},{3,2},{4,3},{5,4},{6,5},{7,6},{8,7},{9,8},{10,9... | collective-permute-start | bytes 1572872 | tf_op jit(solution)/shard_map/ppermute | solution.py:385
  64.1 3.8 %rows.4.refs_0_ = bf16[4,80,2048]{2,1,0:T(8,128)(2,1)} custom-call(bf16[4,320,512]{2,1,0:T(8,128)(2,1)} %get-tuple-element.31.picks_ref, f32[4,320,128]{2,1,0:T(8,128)} %get-tuple-element.32.scale_ref, bf16[128,2048]{1,0:T(8,128)(2,1)} %refs_0_.1, bf16[128,2048]{1,0:T(8,128)(2,1)} %copy-done.11, bf16[128,2048]{1,0:T(8,128)(2,1)} %copy-done.12, ...), custom_call_target="tpu_custom_call" | custom-call | flops 700000000 | bytes 4194304 | tf_op jit(solution)/shard_map/rows/pallas_call | solution.py:125
  67.9 1.8 collective-permute-done.4.refs_1_
  69.7 1.9 collective-permute-start.6
  71.6 4.6 %collective-permute-start.7 = (bf16[128,2048]{1,0:T(8,128)(2,1)S(1)}, bf16[128,2048]{1,0:T(8,128)(2,1)S(1)}, u32[]{:S(2)}, u32[]{:S(2)}) collective-permute-start(bf16[128,2048]{1,0:T(8,128)(2,1)S(1)} %collective-permute-done.5.refs_2_), channel_id=1, source_target_pairs={{0,15},{1,0},{2,1},{3,2},{4,3},{5,4},{6,5},{7,6},{8,7},{9,8},{10,9... | collective-permute-start | bytes 1572872 | tf_op jit(solution)/shard_map/ppermute | solution.py:385
  76.2 5.0 %collective-permute-done.6.refs_3_ = bf16[128,2048]{1,0:T(8,128)(2,1)S(1)} collective-permute-done((bf16[128,2048]{1,0:T(8,128)(2,1)S(1)}, bf16[128,2048]{1,0:T(8,128)(2,1)S(1)}, u32[]{:S(2)}, u32[]{:S(2)}) %collective-permute-start.6) | collective-permute-done | bytes 524320 | tf_op jit(solution)/shard_map/ppermute | solution.py:384
  81.2 1.9 collective-permute-start.8
  83.1 4.6 %collective-permute-start.9 = (bf16[128,2048]{1,0:T(8,128)(2,1)S(1)}, bf16[128,2048]{1,0:T(8,128)(2,1)S(1)}, u32[]{:S(2)}, u32[]{:S(2)}) collective-permute-start(bf16[128,2048]{1,0:T(8,128)(2,1)S(1)} %collective-permute-done.7.refs_0_), channel_id=1, source_target_pairs={{0,15},{1,0},{2,1},{3,2},{4,3},{5,4},{6,5},{7,6},{8,7},{9,8},{10,9... | collective-permute-start | bytes 1572872 | tf_op jit(solution)/shard_map/ppermute | solution.py:385
  87.8 3.6 %rows.5.refs_1_ = bf16[4,80,2048]{2,1,0:T(8,128)(2,1)} custom-call(bf16[4,320,512]{2,1,0:T(8,128)(2,1)} %get-tuple-element.31.picks_ref, f32[4,320,128]{2,1,0:T(8,128)} %get-tuple-element.32.scale_ref, bf16[128,2048]{1,0:T(8,128)(2,1)} %copy-done.13, bf16[128,2048]{1,0:T(8,128)(2,1)} %copy-done.17, bf16[128,2048]{1,0:T(8,128)(2,1)} %copy-done.19, ...), custom_call_target="tpu_custom_call" | custom-call | flops 700000000 | bytes 4194304 | tf_op jit(solution)/shard_map/rows/pallas_call | solution.py:125
  91.3 1.4 collective-permute-done.8.refs_1_
  92.7 1.9 collective-permute-start.10
  94.7 4.7 %collective-permute-start.11 = (bf16[128,2048]{1,0:T(8,128)(2,1)S(1)}, bf16[128,2048]{1,0:T(8,128)(2,1)S(1)}, u32[]{:S(2)}, u32[]{:S(2)}) collective-permute-start(bf16[128,2048]{1,0:T(8,128)(2,1)S(1)} %collective-permute-done.9.refs_2_), channel_id=1, source_target_pairs={{0,15},{1,0},{2,1},{3,2},{4,3},{5,4},{6,5},{7,6},{8,7},{9,8},{10,9... | collective-permute-start | bytes 1572872 | tf_op jit(solution)/shard_map/ppermute | solution.py:385
  99.4 3.9 %all-to-all-start.2 = ((bf16[4,320,768]{2,1,0:T(8,128)(2,1)}), bf16[4,320,768]{2,1,0:T(8,128)(2,1)S(1)}, u32[]{:S(2)}, u32[]{:S(2)}) async-start(bf16[4,320,768]{2,1,0:T(8,128)(2,1)} %bitcast.44), calls=%async_computation.2 | async-start | bytes 3932160 | tf_op jit(solution)/shard_map/all_to_all | solution.py:377
  103.4 1.2 collective-permute-done.10.refs_3_
  104.6 1.7 collective-permute-done.11.refs_0_
  106.3 4.3 %collective-permute-start.12 = (bf16[128,2048]{1,0:T(8,128)(2,1)}, bf16[128,2048]{1,0:T(8,128)(2,1)S(1)}, u32[]{:S(2)}, u32[]{:S(2)}) collective-permute-start(bf16[128,2048]{1,0:T(8,128)(2,1)} %collective-permute-done.10.refs_3_), channel_id=1, source_target_pairs={{0,1},{1,2},{2,3},{3,4},{4,5},{5,6},{6,7},{7,8},{8,9},{9,10},{10,1... | collective-permute-start | bytes 1572872 | tf_op jit(solution)/shard_map/ppermute | solution.py:384
  110.6 2.7 collective-permute-start.13
  113.3 3.4 %rows.6.refs_2_ = bf16[4,80,2048]{2,1,0:T(8,128)(2,1)} custom-call(bf16[4,320,512]{2,1,0:T(8,128)(2,1)} %get-tuple-element.31.picks_ref, f32[4,320,128]{2,1,0:T(8,128)} %get-tuple-element.32.scale_ref, bf16[128,2048]{1,0:T(8,128)(2,1)} %copy-done.15, bf16[128,2048]{1,0:T(8,128)(2,1)} %copy-done.16, bf16[128,2048]{1,0:T(8,128)(2,1)} %copy-done.18, ...), custom_call_target="tpu_custom_call" | custom-call | flops 700000000 | bytes 4194304 | tf_op jit(solution)/shard_map/rows/pallas_call | solution.py:125
  116.7 1.7 collective-permute-done.12.refs_1_
  118.4 3.2 %collective-permute-done.13.refs_2_ = bf16[128,2048]{1,0:T(8,128)(2,1)S(1)} collective-permute-done((bf16[128,2048]{1,0:T(8,128)(2,1)S(1)}, bf16[128,2048]{1,0:T(8,128)(2,1)S(1)}, u32[]{:S(2)}, u32[]{:S(2)}) %collective-permute-start.13) | collective-permute-done | bytes 524320 | tf_op jit(solution)/shard_map/ppermute | solution.py:385
  121.7 4.6 %collective-permute-start.14 = (bf16[64,2048]{1,0:T(8,128)(2,1)S(1)}, bf16[64,2048]{1,0:T(8,128)(2,1)}, u32[]{:S(2)}, u32[]{:S(2)}) collective-permute-start(bf16[64,2048]{1,0:T(8,128)(2,1)S(1)} %slice.6), channel_id=1, source_target_pairs={{0,1},{1,2},{2,3},{3,4},{4,5},{5,6},{6,7},{7,8},{8,9},{9,10},{10,1... | collective-permute-start | bytes 786440 | tf_op jit(solution)/shard_map/ppermute | solution.py:407
  126.3 1.9 collective-permute-start.15
  128.2 5.6 %project.1.near_ref = bf16[4,96,320]{2,1,0:T(8,128)(2,1)} custom-call(bf16[4,8,112,2048]{3,2,1,0:T(8,128)(2,1)} %bitcast.41, bf16[320,320]{1,0:T(8,128)(2,1)} %get-tuple-element.47.order_ref, bf16[4,80,2048]{2,1,0:T(8,128)(2,1)} %rows.4.refs_0_, bf16[4,80,2048]{2,1,0:T(8,128)(2,1)} %rows.5.refs_1_, bf16[4,80,2048]{2,1,0:T(8,128)(2,1)} %rows.6.refs_2_), custom_call_target="tpu_custom_call" | custom-call | flops 1000000000 | bytes 6291456 | tf_op jit(solution)/shard_map/project/pallas_call | solution.py:158
  133.8 3.5 %rows.7.refs_3_.rows_ref = bf16[4,80,2048]{2,1,0:T(8,128)(2,1)} custom-call(bf16[4,320,512]{2,1,0:T(8,128)(2,1)} %get-tuple-element.31.picks_ref, f32[4,320,128]{2,1,0:T(8,128)} %get-tuple-element.32.scale_ref, bf16[128,2048]{1,0:T(8,128)(2,1)} %copy-done.14, bf16[128,2048]{1,0:T(8,128)(2,1)} %copy-done.8, bf16[128,2048]{1,0:T(8,128)(2,1)} %copy-done.9, ...), custom_call_target="tpu_custom_call" | custom-call | flops 700000000 | bytes 4194304 | tf_op jit(solution)/shard_map/rows/pallas_call | solution.py:125
  137.3 11.6 %back.1 = bf16[16,80,768]{2,1,0:T(8,128)(2,1)} custom-call(s32[1]{0:T(128)} %bitcast.z_ref, bf16[4,8,112,2048]{3,2,1,0:T(8,128)(2,1)} %bitcast.42, bf16[320,320]{1,0:T(8,128)(2,1)} %get-tuple-element.30.move_ref, bf16[4,80,2048]{2,1,0:T(8,128)(2,1)} %rows.4.refs_0_, bf16[4,80,2048]{2,1,0:T(8,128)(2,1)} %rows.5.refs_1_, bf16[4,80,2048]{2,1,0:T(8,128)(2,1)} %rows.6.refs_2_, ...), custom_call_target="tpu_custom_call" | custom-call | flops 4000000000 | bytes 20971520 | tf_op jit(solution)/shard_map/back/pallas_call | solution.py:220
  148.9 1.3 copy-done.4
  150.2 6.2 %all-to-all-start.1 = ((bf16[16,80,768]{2,1,0:T(8,128)(2,1)}), bf16[16,80,768]{2,1,0:T(8,128)(2,1)}, u32[]{:S(2)}, u32[]{:S(2)}) async-start(bf16[16,80,768]{2,1,0:T(8,128)(2,1)} %back.1), calls=%async_computation.1 | async-start | bytes 3932160 | tf_op jit(solution)/shard_map/all_to_all | solution.py:414
  156.5 5.6 %left.1 = f32[4,32,768]{2,1,0:T(8,128)} custom-call(bf16[4,96,320]{2,1,0:T(8,128)(2,1)} %project.1.near_ref, bf16[4,8,112,2048]{3,2,1,0:T(8,128)(2,1)} %bitcast.43, bf16[4,80,2048]{2,1,0:T(8,128)(2,1)} %rows.7.refs_3_.rows_ref, bf16[4,320,768]{2,1,0:T(8,128)(2,1)} %copy-done.4, bf16[320,320]{1,0:T(8,128)(2,1)} %get-tuple-element.47.order_ref), custom_call_target="tpu_custom_call" | custom-call | flops 1000000000 | bytes 6291456 | tf_op jit(solution)/shard_map/left/pallas_call | solution.py:182
  163.0 10.6 %collective-permute-start.16 = (f32[4,16,768]{2,1,0:T(8,128)S(1)}, f32[4,16,768]{2,1,0:T(8,128)S(1)}, u32[]{:S(2)}, u32[]{:S(2)}) collective-permute-start(f32[4,16,768]{2,1,0:T(8,128)S(1)} %constant_dynamic-slice_fusion.1), channel_id=1, source_target_pairs={{0,64},{64,0},{1,65},{65,1},{2,66},{66,2},{3,67},{67,3},{4,68},{68... | collective-permute-start | bytes 589832 | tf_op jit(solution)/shard_map/ppermute | solution.py:344
  175.6 4.8 %collective-permute-start.17 = (f32[4,16,768]{2,1,0:T(8,128)S(1)}, f32[4,16,768]{2,1,0:T(8,128)S(1)}, u32[]{:S(2)}, u32[]{:S(2)}) collective-permute-start(f32[4,16,768]{2,1,0:T(8,128)S(1)} %dynamic-slice_add_fusion.1), channel_id=1, source_target_pairs={{0,256},{128,384},{256,0},{384,128},{1,257},{129,385},{257,1},{385... | collective-permute-start | bytes 589832 | tf_op jit(solution)/shard_map/ppermute | solution.py:348
  180.4 2.3 collective-permute-start.18
  182.7 4.2 %collective-permute-start.19 = (f32[4,16,768]{2,1,0:T(8,128)S(1)}, f32[4,16,768]{2,1,0:T(8,128)S(1)}, u32[]{:S(2)}, u32[]{:S(2)}) collective-permute-start(f32[4,16,768]{2,1,0:T(8,128)S(1)} %dynamic-slice_add_fusion.1), channel_id=1, source_target_pairs={{0,384},{128,0},{256,128},{384,256},{1,385},{129,1},{257,129},{385... | collective-permute-start | bytes 589832 | tf_op jit(solution)/shard_map/ppermute | solution.py:348
  186.9 2.5 collective-permute-done.18
  190.2 5.9 %collective-permute-start.20 = (f32[4,16,768]{2,1,0:T(8,128)S(1)}, f32[4,16,768]{2,1,0:T(8,128)S(1)}, u32[]{:S(2)}, u32[]{:S(2)}) collective-permute-start(f32[4,16,768]{2,1,0:T(8,128)S(1)} %add_add_fusion.1), channel_id=1, source_target_pairs={{0,32},{16,48},{32,0},{48,16},{1,33},{17,49},{33,1},{49,17},{2,34}... | collective-permute-start | bytes 589832 | tf_op jit(solution)/shard_map/ppermute | solution.py:348
  196.1 1.9 collective-permute-start.21
  198.0 4.6 %collective-permute-start.22 = (f32[4,16,768]{2,1,0:T(8,128)S(1)}, f32[4,16,768]{2,1,0:T(8,128)S(1)}, u32[]{:S(2)}, u32[]{:S(2)}) collective-permute-start(f32[4,16,768]{2,1,0:T(8,128)S(1)} %add_add_fusion.1), channel_id=1, source_target_pairs={{0,48},{16,0},{32,16},{48,32},{1,49},{17,1},{33,17},{49,33},{2,50}... | collective-permute-start | bytes 589832 | tf_op jit(solution)/shard_map/ppermute | solution.py:348
  202.6 1.5 collective-permute-done.21
  205.3 5.3 %collective-permute-start.23 = (f32[4,16,768]{2,1,0:T(8,128)S(1)}, f32[4,16,768]{2,1,0:T(8,128)S(1)}, u32[]{:S(2)}, u32[]{:S(2)}) collective-permute-start(f32[4,16,768]{2,1,0:T(8,128)S(1)} %add_add_fusion.mine_ref), channel_id=1, source_target_pairs={{0,64},{64,0},{1,65},{65,1},{2,66},{66,2},{3,67},{67,3},{4,68},{68... | collective-permute-start | bytes 589832 | tf_op jit(solution)/shard_map/ppermute | solution.py:418
  211.5 3.5 %basis.1.basis_ref = f32[4,32,768]{2,1,0:T(8,128)S(1)} custom-call(s32[1]{0:T(128)} %bitcast.9.c_ref, f32[4,16,768]{2,1,0:T(8,128)S(1)} %add_add_fusion.mine_ref, f32[4,16,768]{2,1,0:T(8,128)S(1)} %collective-permute-done.23.other_ref), custom_call_target="tpu_custom_call" | custom-call | flops 10000000 | bytes 1048576 | tf_op jit(solution)/shard_map/basis/pallas_call | solution.py:330
  215.1 1.5 copy-done.5
  216.6 3.7 %right.1 = f32[4,32,2048]{2,1,0:T(8,128)S(1)} custom-call(f32[4,32,768]{2,1,0:T(8,128)S(1)} %basis.1.basis_ref, bf16[4,320,768]{2,1,0:T(8,128)(2,1)S(1)} %copy-done.5, bf16[320,320]{1,0:T(8,128)(2,1)S(1)} %copy-done.7, bf16[4,80,2048]{2,1,0:T(8,128)(2,1)S(1)} %copy-done, bf16[4,80,2048]{2,1,0:T(8,128)(2,1)S(1)} %copy-done.1, ...), custom_call_target="tpu_custom_call" | custom-call | flops 1000000000 | bytes 9437184 | tf_op jit(solution)/shard_map/right/pallas_call | solution.py:248
  221.3 2.3 collective-permute-start.24
  223.6 1.5 collective-permute-done.24
  225.1 1.1 dynamic-slice_add_fusion
  226.3 3.6 %collective-permute-start.25 = (f32[16,2048]{1,0:T(8,128)S(1)}, f32[16,2048]{1,0:T(8,128)S(1)}, u32[]{:S(2)}, u32[]{:S(2)}) collective-permute-start(f32[16,2048]{1,0:T(8,128)S(1)} %get-tuple-element.55), channel_id=1, source_target_pairs={{0,32},{16,48},{32,0},{48,16},{1,33},{17,49},{33,1},{49,17},{2,34}... | collective-permute-start | bytes 393224 | tf_op jit(solution)/shard_map/ppermute | solution.py:357
  229.8 4.2 %collective-permute-start.26 = (f32[16,2048]{1,0:T(8,128)S(1)}, f32[16,2048]{1,0:T(8,128)S(1)}, u32[]{:S(2)}, u32[]{:S(2)}) collective-permute-start(f32[16,2048]{1,0:T(8,128)S(1)} %get-tuple-element.57), channel_id=1, source_target_pairs={{0,16},{16,32},{32,48},{48,0},{1,17},{17,33},{33,49},{49,1},{2,18}... | collective-permute-start | bytes 393224 | tf_op jit(solution)/shard_map/ppermute | solution.py:357
  234.1 2.2 collective-permute-start.27
  236.4 1.1 collective-permute-done.26
  237.4 2.8 %collective-permute-done.27 = f32[16,2048]{1,0:T(8,128)S(1)} collective-permute-done((f32[16,2048]{1,0:T(8,128)S(1)}, f32[16,2048]{1,0:T(8,128)S(1)}, u32[]{:S(2)}, u32[]{:S(2)}) %collective-permute-start.27) | collective-permute-done | bytes 131104 | tf_op jit(solution)/shard_map/ppermute | solution.py:357
  240.2 4.0 %collective-permute-start.28 = (f32[16,2048]{1,0:T(8,128)S(1)}, f32[16,2048]{1,0:T(8,128)S(1)}, u32[]{:S(2)}, u32[]{:S(2)}) collective-permute-start(f32[16,2048]{1,0:T(8,128)S(1)} %fusion.7), channel_id=1, source_target_pairs={{0,256},{128,384},{256,0},{384,128},{1,257},{129,385},{257,1},{385... | collective-permute-start | bytes 393224 | tf_op jit(solution)/shard_map/ppermute | solution.py:348
  244.3 3.8 %collective-permute-start.29 = (f32[16,2048]{1,0:T(8,128)S(1)}, f32[16,2048]{1,0:T(8,128)S(1)}, u32[]{:S(2)}, u32[]{:S(2)}) collective-permute-start(f32[16,2048]{1,0:T(8,128)S(1)} %fusion.7), channel_id=1, source_target_pairs={{0,128},{128,256},{256,384},{384,0},{1,129},{129,257},{257,385},{3... | collective-permute-start | bytes 393224 | tf_op jit(solution)/shard_map/ppermute | solution.py:348
  248.1 2.7 collective-permute-start.30
  251.2 2.7 collective-permute-done.30
  254.0 5.2 %collective-permute-start.31 = (f32[16,2048]{1,0:T(8,128)S(1)}, f32[16,2048]{1,0:T(8,128)S(1)}, u32[]{:S(2)}, u32[]{:S(2)}) collective-permute-start(f32[16,2048]{1,0:T(8,128)S(1)} %add_add_fusion.2), channel_id=1, source_target_pairs={{0,64},{64,0},{1,65},{65,1},{2,66},{66,2},{3,67},{67,3},{4,68},{68... | collective-permute-start | bytes 393224 | tf_op jit(solution)/shard_map/ppermute | solution.py:359
  260.8 5.4 %spread.1 = bf16[128,8,768]{2,1,0:T(8,128)(2,1)} custom-call(s32[1024,1]{1,0:T(8,128)S(1)} %reshape.39.place_ref, bf16[1280,768]{1,0:T(8,128)(2,1)} %bitcast.8.rows_ref), custom_call_target="tpu_custom_call" | custom-call | flops 2000000000 | bytes 4194304 | tf_op jit(solution)/shard_map/spread/pallas_call | solution.py:275
  (92 shorter events, 10.4 us)
Async XLA Ops:
  7.2 2.9 %copy-start.10 = (bf16[128,2048]{1,0:T(8,128)(2,1)S(1)}, bf16[128,2048]{1,0:T(8,128)(2,1)}, u32[]{:S(2)}) copy-start(bf16[128,2048]{1,0:T(8,128)(2,1)} %refs_0_.1) | copy-start | bytes 1572868
  7.2 16.8 %copy-start.22 = (s32[128,8]{0,1:T(8,128)S(1)}, s32[128,8]{0,1:T(8,128)}, u32[]{:S(2)}) copy-start(s32[128,8]{0,1:T(8,128)} %param.7) | copy-start | bytes 12292
  7.2 17.1 %copy-start.23 = (f32[128,8]{0,1:T(8,128)S(1)}, f32[128,8]{0,1:T(8,128)}, u32[]{:S(2)}) copy-start(f32[128,8]{0,1:T(8,128)} %param.8) | copy-start | bytes 12292
  7.2 121.0 %all-gather.2.cloned.1.call-start = ((), (), s32[]{:S(2)}) async-start(), calls=%async_computation.3 | async-start | bytes 15138816 | tf_op jit(solution)/shard_map/all_gather | solution.py:371
  10.1 34.6 %collective-permute-start = (bf16[128,2048]{1,0:T(8,128)(2,1)S(1)}, bf16[128,2048]{1,0:T(8,128)(2,1)S(1)}, u32[]{:S(2)}, u32[]{:S(2)}) collective-permute-start(bf16[128,2048]{1,0:T(8,128)(2,1)S(1)} %copy-done.10), channel_id=1, source_target_pairs={{0,1},{1,2},{2,3},{3,4},{4,5},{5,6},{6,7},{7,8},{8,9},{9,10},{10,1... | collective-permute-start | bytes 1572872 | tf_op jit(solution)/shard_map/ppermute | solution.py:384
  14.4 33.1 %collective-permute-start.1 = (bf16[128,2048]{1,0:T(8,128)(2,1)S(1)}, bf16[128,2048]{1,0:T(8,128)(2,1)S(1)}, u32[]{:S(2)}, u32[]{:S(2)}) collective-permute-start(bf16[128,2048]{1,0:T(8,128)(2,1)S(1)} %copy-done.10), channel_id=1, source_target_pairs={{0,15},{1,0},{2,1},{3,2},{4,3},{5,4},{6,5},{7,6},{8,7},{9,8},{10,9... | collective-permute-start | bytes 1572872 | tf_op jit(solution)/shard_map/ppermute | solution.py:385
  44.6 19.5 %copy-start.11 = (bf16[128,2048]{1,0:T(8,128)(2,1)}, bf16[128,2048]{1,0:T(8,128)(2,1)S(1)}, u32[]{:S(2)}) copy-start(bf16[128,2048]{1,0:T(8,128)(2,1)S(1)} %collective-permute-done.refs_1_) | copy-start | bytes 1572868
  44.6 12.9 %collective-permute-start.2 = (bf16[128,2048]{1,0:T(8,128)(2,1)S(1)}, bf16[128,2048]{1,0:T(8,128)(2,1)S(1)}, u32[]{:S(2)}, u32[]{:S(2)}) collective-permute-start(bf16[128,2048]{1,0:T(8,128)(2,1)S(1)} %collective-permute-done.refs_1_), channel_id=1, source_target_pairs={{0,1},{1,2},{2,3},{3,4},{4,5},{5,6},{6,7},{7,8},{8,9},{9,10},{10,1... | collective-permute-start | bytes 1572872 | tf_op jit(solution)/shard_map/ppermute | solution.py:384
  47.6 16.5 %copy-start.12 = (bf16[128,2048]{1,0:T(8,128)(2,1)}, bf16[128,2048]{1,0:T(8,128)(2,1)S(1)}, u32[]{:S(2)}) copy-start(bf16[128,2048]{1,0:T(8,128)(2,1)S(1)} %collective-permute-done.1.refs_2_) | copy-start | bytes 1572868
  47.6 11.9 %collective-permute-start.3 = (bf16[128,2048]{1,0:T(8,128)(2,1)S(1)}, bf16[128,2048]{1,0:T(8,128)(2,1)S(1)}, u32[]{:S(2)}, u32[]{:S(2)}) collective-permute-start(bf16[128,2048]{1,0:T(8,128)(2,1)S(1)} %collective-permute-done.1.refs_2_), channel_id=1, source_target_pairs={{0,15},{1,0},{2,1},{3,2},{4,3},{5,4},{6,5},{7,6},{8,7},{9,8},{10,9... | collective-permute-start | bytes 1572872 | tf_op jit(solution)/shard_map/ppermute | solution.py:385
  57.6 6.5 %copy-start.20 = (bf16[128,2048]{1,0:T(8,128)(2,1)}, bf16[128,2048]{1,0:T(8,128)(2,1)S(1)}, u32[]{:S(2)}) copy-start(bf16[128,2048]{1,0:T(8,128)(2,1)S(1)} %collective-permute-done.2.refs_3_) | copy-start | bytes 1572868
  57.6 12.1 %collective-permute-start.4 = (bf16[128,2048]{1,0:T(8,128)(2,1)S(1)}, bf16[128,2048]{1,0:T(8,128)(2,1)S(1)}, u32[]{:S(2)}, u32[]{:S(2)}) collective-permute-start(bf16[128,2048]{1,0:T(8,128)(2,1)S(1)} %collective-permute-done.2.refs_3_), channel_id=1, source_target_pairs={{0,1},{1,2},{2,3},{3,4},{4,5},{5,6},{6,7},{7,8},{8,9},{9,10},{10,1... | collective-permute-start | bytes 1572872 | tf_op jit(solution)/shard_map/ppermute | solution.py:384
  59.5 8.4 %copy-start.13 = (bf16[128,2048]{1,0:T(8,128)(2,1)}, bf16[128,2048]{1,0:T(8,128)(2,1)S(1)}, u32[]{:S(2)}) copy-start(bf16[128,2048]{1,0:T(8,128)(2,1)S(1)} %collective-permute-done.3.refs_0_) | copy-start | bytes 1572868
  59.5 12.1 %collective-permute-start.5 = (bf16[128,2048]{1,0:T(8,128)(2,1)S(1)}, bf16[128,2048]{1,0:T(8,128)(2,1)S(1)}, u32[]{:S(2)}, u32[]{:S(2)}) collective-permute-start(bf16[128,2048]{1,0:T(8,128)(2,1)S(1)} %collective-permute-done.3.refs_0_), channel_id=1, source_target_pairs={{0,15},{1,0},{2,1},{3,2},{4,3},{5,4},{6,5},{7,6},{8,7},{9,8},{10,9... | collective-permute-start | bytes 1572872 | tf_op jit(solution)/shard_map/ppermute | solution.py:385
  69.7 18.0 %copy-start.17 = (bf16[128,2048]{1,0:T(8,128)(2,1)}, bf16[128,2048]{1,0:T(8,128)(2,1)S(1)}, u32[]{:S(2)}) copy-start(bf16[128,2048]{1,0:T(8,128)(2,1)S(1)} %collective-permute-done.4.refs_1_) | copy-start | bytes 1572868
  69.7 11.5 %collective-permute-start.6 = (bf16[128,2048]{1,0:T(8,128)(2,1)S(1)}, bf16[128,2048]{1,0:T(8,128)(2,1)S(1)}, u32[]{:S(2)}, u32[]{:S(2)}) collective-permute-start(bf16[128,2048]{1,0:T(8,128)(2,1)S(1)} %collective-permute-done.4.refs_1_), channel_id=1, source_target_pairs={{0,1},{1,2},{2,3},{3,4},{4,5},{5,6},{6,7},{7,8},{8,9},{9,10},{10,1... | collective-permute-start | bytes 1572872 | tf_op jit(solution)/shard_map/ppermute | solution.py:384
  71.6 16.1 %copy-start.19 = (bf16[128,2048]{1,0:T(8,128)(2,1)}, bf16[128,2048]{1,0:T(8,128)(2,1)S(1)}, u32[]{:S(2)}) copy-start(bf16[128,2048]{1,0:T(8,128)(2,1)S(1)} %collective-permute-done.5.refs_2_) | copy-start | bytes 1572868
  71.6 11.5 %collective-permute-start.7 = (bf16[128,2048]{1,0:T(8,128)(2,1)S(1)}, bf16[128,2048]{1,0:T(8,128)(2,1)S(1)}, u32[]{:S(2)}, u32[]{:S(2)}) collective-permute-start(bf16[128,2048]{1,0:T(8,128)(2,1)S(1)} %collective-permute-done.5.refs_2_), channel_id=1, source_target_pairs={{0,15},{1,0},{2,1},{3,2},{4,3},{5,4},{6,5},{7,6},{8,7},{9,8},{10,9... | collective-permute-start | bytes 1572872 | tf_op jit(solution)/shard_map/ppermute | solution.py:385
  81.2 6.5 %copy-start.21 = (bf16[128,2048]{1,0:T(8,128)(2,1)}, bf16[128,2048]{1,0:T(8,128)(2,1)S(1)}, u32[]{:S(2)}) copy-start(bf16[128,2048]{1,0:T(8,128)(2,1)S(1)} %collective-permute-done.6.refs_3_) | copy-start | bytes 1572868
  81.2 11.5 %collective-permute-start.8 = (bf16[128,2048]{1,0:T(8,128)(2,1)S(1)}, bf16[128,2048]{1,0:T(8,128)(2,1)S(1)}, u32[]{:S(2)}, u32[]{:S(2)}) collective-permute-start(bf16[128,2048]{1,0:T(8,128)(2,1)S(1)} %collective-permute-done.6.refs_3_), channel_id=1, source_target_pairs={{0,1},{1,2},{2,3},{3,4},{4,5},{5,6},{6,7},{7,8},{8,9},{9,10},{10,1... | collective-permute-start | bytes 1572872 | tf_op jit(solution)/shard_map/ppermute | solution.py:384
  83.1 8.2 %copy-start.15 = (bf16[128,2048]{1,0:T(8,128)(2,1)}, bf16[128,2048]{1,0:T(8,128)(2,1)S(1)}, u32[]{:S(2)}) copy-start(bf16[128,2048]{1,0:T(8,128)(2,1)S(1)} %collective-permute-done.7.refs_0_) | copy-start | bytes 1572868
  83.1 11.5 %collective-permute-start.9 = (bf16[128,2048]{1,0:T(8,128)(2,1)S(1)}, bf16[128,2048]{1,0:T(8,128)(2,1)S(1)}, u32[]{:S(2)}, u32[]{:S(2)}) collective-permute-start(bf16[128,2048]{1,0:T(8,128)(2,1)S(1)} %collective-permute-done.7.refs_0_), channel_id=1, source_target_pairs={{0,15},{1,0},{2,1},{3,2},{4,3},{5,4},{6,5},{7,6},{8,7},{9,8},{10,9... | collective-permute-start | bytes 1572872 | tf_op jit(solution)/shard_map/ppermute | solution.py:385
  92.7 6.7 %copy-start.16 = (bf16[128,2048]{1,0:T(8,128)(2,1)}, bf16[128,2048]{1,0:T(8,128)(2,1)S(1)}, u32[]{:S(2)}) copy-start(bf16[128,2048]{1,0:T(8,128)(2,1)S(1)} %collective-permute-done.8.refs_1_) | copy-start | bytes 1572868
  92.7 11.8 %collective-permute-start.10 = (bf16[128,2048]{1,0:T(8,128)(2,1)S(1)}, bf16[128,2048]{1,0:T(8,128)(2,1)}, u32[]{:S(2)}, u32[]{:S(2)}) collective-permute-start(bf16[128,2048]{1,0:T(8,128)(2,1)S(1)} %collective-permute-done.8.refs_1_), channel_id=1, source_target_pairs={{0,1},{1,2},{2,3},{3,4},{4,5},{5,6},{6,7},{7,8},{8,9},{9,10},{10,1... | collective-permute-start | bytes 1572872 | tf_op jit(solution)/shard_map/ppermute | solution.py:384
  94.7 4.7 %copy-start.18 = (bf16[128,2048]{1,0:T(8,128)(2,1)}, bf16[128,2048]{1,0:T(8,128)(2,1)S(1)}, u32[]{:S(2)}) copy-start(bf16[128,2048]{1,0:T(8,128)(2,1)S(1)} %collective-permute-done.9.refs_2_) | copy-start | bytes 1572868
  94.7 11.7 %collective-permute-start.11 = (bf16[128,2048]{1,0:T(8,128)(2,1)S(1)}, bf16[128,2048]{1,0:T(8,128)(2,1)S(1)}, u32[]{:S(2)}, u32[]{:S(2)}) collective-permute-start(bf16[128,2048]{1,0:T(8,128)(2,1)S(1)} %collective-permute-done.9.refs_2_), channel_id=1, source_target_pairs={{0,15},{1,0},{2,1},{3,2},{4,3},{5,4},{6,5},{7,6},{8,7},{9,8},{10,9... | collective-permute-start | bytes 1572872 | tf_op jit(solution)/shard_map/ppermute | solution.py:385
  99.4 49.5 %all-to-all-start.2 = ((bf16[4,320,768]{2,1,0:T(8,128)(2,1)}), bf16[4,320,768]{2,1,0:T(8,128)(2,1)S(1)}, u32[]{:S(2)}, u32[]{:S(2)}) async-start(bf16[4,320,768]{2,1,0:T(8,128)(2,1)} %bitcast.44), calls=%async_computation.2 | async-start | bytes 3932160 | tf_op jit(solution)/shard_map/all_to_all | solution.py:377
  106.3 10.4 %copy-start.14 = (bf16[128,2048]{1,0:T(8,128)(2,1)}, bf16[128,2048]{1,0:T(8,128)(2,1)S(1)}, u32[]{:S(2)}) copy-start(bf16[128,2048]{1,0:T(8,128)(2,1)S(1)} %collective-permute-done.11.refs_0_) | copy-start | bytes 1572868
  106.3 12.1 %collective-permute-start.12 = (bf16[128,2048]{1,0:T(8,128)(2,1)}, bf16[128,2048]{1,0:T(8,128)(2,1)S(1)}, u32[]{:S(2)}, u32[]{:S(2)}) collective-permute-start(bf16[128,2048]{1,0:T(8,128)(2,1)} %collective-permute-done.10.refs_3_), channel_id=1, source_target_pairs={{0,1},{1,2},{2,3},{3,4},{4,5},{5,6},{6,7},{7,8},{8,9},{9,10},{10,1... | collective-permute-start | bytes 1572872 | tf_op jit(solution)/shard_map/ppermute | solution.py:384
  110.6 11.0 %collective-permute-start.13 = (bf16[128,2048]{1,0:T(8,128)(2,1)S(1)}, bf16[128,2048]{1,0:T(8,128)(2,1)S(1)}, u32[]{:S(2)}, u32[]{:S(2)}) collective-permute-start(bf16[128,2048]{1,0:T(8,128)(2,1)S(1)} %collective-permute-done.11.refs_0_), channel_id=1, source_target_pairs={{0,15},{1,0},{2,1},{3,2},{4,3},{5,4},{6,5},{7,6},{8,7},{9,8},{10,9... | collective-permute-start | bytes 1572872 | tf_op jit(solution)/shard_map/ppermute | solution.py:385
  118.4 15.4 %copy-start.8 = (bf16[128,2048]{1,0:T(8,128)(2,1)}, bf16[128,2048]{1,0:T(8,128)(2,1)S(1)}, u32[]{:S(2)}) copy-start(bf16[128,2048]{1,0:T(8,128)(2,1)S(1)} %collective-permute-done.12.refs_1_) | copy-start | bytes 1572868
  121.6 12.2 %copy-start.9 = (bf16[128,2048]{1,0:T(8,128)(2,1)}, bf16[128,2048]{1,0:T(8,128)(2,1)S(1)}, u32[]{:S(2)}) copy-start(bf16[128,2048]{1,0:T(8,128)(2,1)S(1)} %collective-permute-done.13.refs_2_) | copy-start | bytes 1572868
  121.7 12.2 %collective-permute-start.14 = (bf16[64,2048]{1,0:T(8,128)(2,1)S(1)}, bf16[64,2048]{1,0:T(8,128)(2,1)}, u32[]{:S(2)}, u32[]{:S(2)}) collective-permute-start(bf16[64,2048]{1,0:T(8,128)(2,1)S(1)} %slice.6), channel_id=1, source_target_pairs={{0,1},{1,2},{2,3},{3,4},{4,5},{5,6},{6,7},{7,8},{8,9},{9,10},{10,1... | collective-permute-start | bytes 786440 | tf_op jit(solution)/shard_map/ppermute | solution.py:407
  126.3 7.6 %collective-permute-start.15 = (bf16[64,2048]{1,0:T(8,128)(2,1)S(1)}, bf16[64,2048]{1,0:T(8,128)(2,1)}, u32[]{:S(2)}, u32[]{:S(2)}) collective-permute-start(bf16[64,2048]{1,0:T(8,128)(2,1)S(1)} %slice.7), channel_id=1, source_target_pairs={{0,15},{1,0},{2,1},{3,2},{4,3},{5,4},{6,5},{7,6},{8,7},{9,8},{10,9... | collective-permute-start | bytes 786440 | tf_op jit(solution)/shard_map/ppermute | solution.py:408
  148.9 1.3 copy-start.4
  150.2 110.6 %all-to-all-start.1 = ((bf16[16,80,768]{2,1,0:T(8,128)(2,1)}), bf16[16,80,768]{2,1,0:T(8,128)(2,1)}, u32[]{:S(2)}, u32[]{:S(2)}) async-start(bf16[16,80,768]{2,1,0:T(8,128)(2,1)} %back.1), calls=%async_computation.1 | async-start | bytes 3932160 | tf_op jit(solution)/shard_map/all_to_all | solution.py:414
  156.5 58.5 %copy-start.2 = (bf16[4,80,2048]{2,1,0:T(8,128)(2,1)S(1)}, bf16[4,80,2048]{2,1,0:T(8,128)(2,1)}, u32[]{:S(2)}) copy-start(bf16[4,80,2048]{2,1,0:T(8,128)(2,1)} %rows.6.refs_2_) | copy-start | bytes 3932164
  156.5 58.5 %copy-start.3 = (bf16[4,80,2048]{2,1,0:T(8,128)(2,1)S(1)}, bf16[4,80,2048]{2,1,0:T(8,128)(2,1)}, u32[]{:S(2)}) copy-start(bf16[4,80,2048]{2,1,0:T(8,128)(2,1)} %rows.7.refs_3_.rows_ref) | copy-start | bytes 3932164
  163.0 11.6 %collective-permute-start.16 = (f32[4,16,768]{2,1,0:T(8,128)S(1)}, f32[4,16,768]{2,1,0:T(8,128)S(1)}, u32[]{:S(2)}, u32[]{:S(2)}) collective-permute-start(f32[4,16,768]{2,1,0:T(8,128)S(1)} %constant_dynamic-slice_fusion.1), channel_id=1, source_target_pairs={{0,64},{64,0},{1,65},{65,1},{2,66},{66,2},{3,67},{67,3},{4,68},{68... | collective-permute-start | bytes 589832 | tf_op jit(solution)/shard_map/ppermute | solution.py:344
  173.6 41.4 %copy-start = (bf16[4,80,2048]{2,1,0:T(8,128)(2,1)S(1)}, bf16[4,80,2048]{2,1,0:T(8,128)(2,1)}, u32[]{:S(2)}) copy-start(bf16[4,80,2048]{2,1,0:T(8,128)(2,1)} %rows.4.refs_0_) | copy-start | bytes 3932164
  173.6 41.4 %copy-start.1 = (bf16[4,80,2048]{2,1,0:T(8,128)(2,1)S(1)}, bf16[4,80,2048]{2,1,0:T(8,128)(2,1)}, u32[]{:S(2)}) copy-start(bf16[4,80,2048]{2,1,0:T(8,128)(2,1)} %rows.5.refs_1_) | copy-start | bytes 3932164
  173.6 41.4 %copy-start.7 = (bf16[320,320]{1,0:T(8,128)(2,1)S(1)}, bf16[320,320]{1,0:T(8,128)(2,1)}, u32[]{:S(2)}) copy-start(bf16[320,320]{1,0:T(8,128)(2,1)} %get-tuple-element.47.order_ref) | copy-start | bytes 614404
  175.6 11.3 %collective-permute-start.17 = (f32[4,16,768]{2,1,0:T(8,128)S(1)}, f32[4,16,768]{2,1,0:T(8,128)S(1)}, u32[]{:S(2)}, u32[]{:S(2)}) collective-permute-start(f32[4,16,768]{2,1,0:T(8,128)S(1)} %dynamic-slice_add_fusion.1), channel_id=1, source_target_pairs={{0,256},{128,384},{256,0},{384,128},{1,257},{129,385},{257,1},{385... | collective-permute-start | bytes 589832 | tf_op jit(solution)/shard_map/ppermute | solution.py:348
  180.4 9.0 %collective-permute-start.18 = (f32[4,16,768]{2,1,0:T(8,128)S(1)}, f32[4,16,768]{2,1,0:T(8,128)S(1)}, u32[]{:S(2)}, u32[]{:S(2)}) collective-permute-start(f32[4,16,768]{2,1,0:T(8,128)S(1)} %dynamic-slice_add_fusion.1), channel_id=1, source_target_pairs={{0,128},{128,256},{256,384},{384,0},{1,129},{129,257},{257,385},{3... | collective-permute-start | bytes 589832 | tf_op jit(solution)/shard_map/ppermute | solution.py:348
  182.7 7.5 %collective-permute-start.19 = (f32[4,16,768]{2,1,0:T(8,128)S(1)}, f32[4,16,768]{2,1,0:T(8,128)S(1)}, u32[]{:S(2)}, u32[]{:S(2)}) collective-permute-start(f32[4,16,768]{2,1,0:T(8,128)S(1)} %dynamic-slice_add_fusion.1), channel_id=1, source_target_pairs={{0,384},{128,0},{256,128},{384,256},{1,385},{129,1},{257,129},{385... | collective-permute-start | bytes 589832 | tf_op jit(solution)/shard_map/ppermute | solution.py:348
  190.2 12.4 %collective-permute-start.20 = (f32[4,16,768]{2,1,0:T(8,128)S(1)}, f32[4,16,768]{2,1,0:T(8,128)S(1)}, u32[]{:S(2)}, u32[]{:S(2)}) collective-permute-start(f32[4,16,768]{2,1,0:T(8,128)S(1)} %add_add_fusion.1), channel_id=1, source_target_pairs={{0,32},{16,48},{32,0},{48,16},{1,33},{17,49},{33,1},{49,17},{2,34}... | collective-permute-start | bytes 589832 | tf_op jit(solution)/shard_map/ppermute | solution.py:348
  196.1 8.0 %collective-permute-start.21 = (f32[4,16,768]{2,1,0:T(8,128)S(1)}, f32[4,16,768]{2,1,0:T(8,128)S(1)}, u32[]{:S(2)}, u32[]{:S(2)}) collective-permute-start(f32[4,16,768]{2,1,0:T(8,128)S(1)} %add_add_fusion.1), channel_id=1, source_target_pairs={{0,16},{16,32},{32,48},{48,0},{1,17},{17,33},{33,49},{49,1},{2,18}... | collective-permute-start | bytes 589832 | tf_op jit(solution)/shard_map/ppermute | solution.py:348
  198.0 7.2 %collective-permute-start.22 = (f32[4,16,768]{2,1,0:T(8,128)S(1)}, f32[4,16,768]{2,1,0:T(8,128)S(1)}, u32[]{:S(2)}, u32[]{:S(2)}) collective-permute-start(f32[4,16,768]{2,1,0:T(8,128)S(1)} %add_add_fusion.1), channel_id=1, source_target_pairs={{0,48},{16,0},{32,16},{48,32},{1,49},{17,1},{33,17},{49,33},{2,50}... | collective-permute-start | bytes 589832 | tf_op jit(solution)/shard_map/ppermute | solution.py:348
  205.3 6.2 %collective-permute-start.23 = (f32[4,16,768]{2,1,0:T(8,128)S(1)}, f32[4,16,768]{2,1,0:T(8,128)S(1)}, u32[]{:S(2)}, u32[]{:S(2)}) collective-permute-start(f32[4,16,768]{2,1,0:T(8,128)S(1)} %add_add_fusion.mine_ref), channel_id=1, source_target_pairs={{0,64},{64,0},{1,65},{65,1},{2,66},{66,2},{3,67},{67,3},{4,68},{68... | collective-permute-start | bytes 589832 | tf_op jit(solution)/shard_map/ppermute | solution.py:418
  215.0 1.5 copy-start.5
  220.3 1.0 copy-start.6
  221.3 3.8 %collective-permute-start.24 = (f32[4,16,2048]{2,1,0:T(8,128)S(1)}, f32[4,16,2048]{2,1,0:T(8,128)S(1)}, u32[]{:S(2)}, u32[]{:S(2)}) collective-permute-start(f32[4,16,2048]{2,1,0:T(8,128)S(1)} %constant_dynamic-slice_fusion), channel_id=1, source_target_pairs={{0,64},{64,0},{1,65},{65,1},{2,66},{66,2},{3,67},{67,3},{4,68},{68... | collective-permute-start | bytes 1572872 | tf_op jit(solution)/shard_map/ppermute | solution.py:344
  226.3 10.1 %collective-permute-start.25 = (f32[16,2048]{1,0:T(8,128)S(1)}, f32[16,2048]{1,0:T(8,128)S(1)}, u32[]{:S(2)}, u32[]{:S(2)}) collective-permute-start(f32[16,2048]{1,0:T(8,128)S(1)} %get-tuple-element.55), channel_id=1, source_target_pairs={{0,32},{16,48},{32,0},{48,16},{1,33},{17,49},{33,1},{49,17},{2,34}... | collective-permute-start | bytes 393224 | tf_op jit(solution)/shard_map/ppermute | solution.py:357
  229.8 7.6 %collective-permute-start.26 = (f32[16,2048]{1,0:T(8,128)S(1)}, f32[16,2048]{1,0:T(8,128)S(1)}, u32[]{:S(2)}, u32[]{:S(2)}) collective-permute-start(f32[16,2048]{1,0:T(8,128)S(1)} %get-tuple-element.57), channel_id=1, source_target_pairs={{0,16},{16,32},{32,48},{48,0},{1,17},{17,33},{33,49},{49,1},{2,18}... | collective-permute-start | bytes 393224 | tf_op jit(solution)/shard_map/ppermute | solution.py:357
  234.1 6.1 %collective-permute-start.27 = (f32[16,2048]{1,0:T(8,128)S(1)}, f32[16,2048]{1,0:T(8,128)S(1)}, u32[]{:S(2)}, u32[]{:S(2)}) collective-permute-start(f32[16,2048]{1,0:T(8,128)S(1)} %get-tuple-element.56), channel_id=1, source_target_pairs={{0,48},{16,0},{32,16},{48,32},{1,49},{17,1},{33,17},{49,33},{2,50}... | collective-permute-start | bytes 393224 | tf_op jit(solution)/shard_map/ppermute | solution.py:357
  240.2 10.6 %collective-permute-start.28 = (f32[16,2048]{1,0:T(8,128)S(1)}, f32[16,2048]{1,0:T(8,128)S(1)}, u32[]{:S(2)}, u32[]{:S(2)}) collective-permute-start(f32[16,2048]{1,0:T(8,128)S(1)} %fusion.7), channel_id=1, source_target_pairs={{0,256},{128,384},{256,0},{384,128},{1,257},{129,385},{257,1},{385... | collective-permute-start | bytes 393224 | tf_op jit(solution)/shard_map/ppermute | solution.py:348
  244.3 6.9 %collective-permute-start.29 = (f32[16,2048]{1,0:T(8,128)S(1)}, f32[16,2048]{1,0:T(8,128)S(1)}, u32[]{:S(2)}, u32[]{:S(2)}) collective-permute-start(f32[16,2048]{1,0:T(8,128)S(1)} %fusion.7), channel_id=1, source_target_pairs={{0,128},{128,256},{256,384},{384,0},{1,129},{129,257},{257,385},{3... | collective-permute-start | bytes 393224 | tf_op jit(solution)/shard_map/ppermute | solution.py:348
  248.1 5.9 %collective-permute-start.30 = (f32[16,2048]{1,0:T(8,128)S(1)}, f32[16,2048]{1,0:T(8,128)S(1)}, u32[]{:S(2)}, u32[]{:S(2)}) collective-permute-start(f32[16,2048]{1,0:T(8,128)S(1)} %fusion.7), channel_id=1, source_target_pairs={{0,384},{128,0},{256,128},{384,256},{1,385},{129,1},{257,129},{385... | collective-permute-start | bytes 393224 | tf_op jit(solution)/shard_map/ppermute | solution.py:348
  254.0 6.1 %collective-permute-start.31 = (f32[16,2048]{1,0:T(8,128)S(1)}, f32[16,2048]{1,0:T(8,128)S(1)}, u32[]{:S(2)}, u32[]{:S(2)}) collective-permute-start(f32[16,2048]{1,0:T(8,128)S(1)} %add_add_fusion.2), channel_id=1, source_target_pairs={{0,64},{64,0},{1,65},{65,1},{2,66},{66,2},{3,67},{67,3},{4,68},{68... | collective-permute-start | bytes 393224 | tf_op jit(solution)/shard_map/ppermute | solution.py:359
Sparse Core Ops, SparseCore 0:
  11.2 88.8 all-gather.1

commit v6 on v5

--- a/solution.py
+++ b/solution.py
@@ -349,15 +349,19 @@
     return a + moved[0] + (moved[1] + moved[2])
 
 
-def sum_right(parts, x, c):
+def sum_right(parts, x, c, beside):
     half = half_sum(parts, c)
     total = lax.dynamic_index_in_dim(half, x, 0, keepdims=False)
     for d in (2, 1, 3):
         piece = lax.dynamic_index_in_dim(half, lax.rem(x + d, N_X), 0, keepdims=False)
         total = total + lax.ppermute(piece, "x", turn(N_X, d))
-    total = ring_sum(total, "y")
+    moved = [lax.ppermute(total, "y", turn(N_Y, d)) for d in (2, 1, 3)]
+    beside = beside()
+    moved, beside = lax.optimization_barrier((moved, beside))
+    total = total + moved[0] + (moved[1] + moved[2])
     other = lax.ppermute(total, "c", turn(2, 1))
-    return jnp.where(c == 0, jnp.concatenate([total, other]), jnp.concatenate([other, total]))
+    whole = jnp.where(c == 0, jnp.concatenate([total, other]), jnp.concatenate([other, total]))
+    return whole, beside
 
 
 def shards(grad_out, expert_ids, gates, hidden, w_down, q_start):
@@ -416,10 +420,14 @@
     p_half = half_sum(left_part(near, gathered, last_rows, stored, order), c)
     p_half = ring_sum(ring_sum(p_half, "y"), "x")
     basis = orthonormal(c.reshape(1), p_half, lax.ppermute(p_half, "c", turn(2, 1)))
-    q_sum = sum_right(right_part(basis, stored, order, rows), x, c)
+    place = places(expert_ids)
+    q_sum, grad_hidden = sum_right(
+        right_part(basis, stored, order, rows),
+        x,
+        c,
+        lambda: spread(place, returned.reshape(N_Z * N_X * CAP, FF)),
+    )
     p_basis = lax.dynamic_index_in_dim(basis, x, 0, keepdims=False).T * math.sqrt(FF)
-    place = places(expert_ids)
-    grad_hidden = spread(place, returned.reshape(N_Z * N_X * CAP, FF))
     return (grad_hidden, p_basis[None], (q_sum.T / N_REP)[None])
 
 

time: 275 us -> 271 us (0.985)
  waiting for transfers between devices: 35.5 us -> 32.4 us
    ppermute x0 -> x3, starting transfers between devices: none -> 10.5 us  [sum_right(): moved = [lax.ppermute(total, 'y', turn(N_Y, d)) for d in (2, 1, 3)]]
    ppermute x9 -> x6, starting transfers between devices: 34.2 us -> 23.7 us  [ring_sum(): moved = [lax.ppermute(a, axis, turn(4, d)) for d in (2, 1, 3)]]
    ppermute x9 -> x6, waiting for transfers between devices: 8.99 us -> 5.85 us  [ring_sum(): moved = [lax.ppermute(a, axis, turn(4, d)) for d in (2, 1, 3)]]
  transfers between devices with their start and end apart: 35 -> 35, of which waited for: 19 -> 18; matrix products, arithmetic and copies ran while one was open for 2% -> 2% of each run, Pallas kernels for 17% -> 20%
where the time goes in v6:
time: 271 us; the launch traced here: 269 us
  starting transfers between devices  137 us (51%)
  Pallas kernels  53 us (20%)
  waiting for transfers between devices  32.4 us (12%)
  blocking collectives  20.3 us (7%)
  between operations  14.8 us (5%)
  other arithmetic  6.44 us (2%)
  local copies, waits for them, and re-layouts  5.23 us (2%)
    ppermute x7, starting transfers between devices, shards(): left = lax.ppermute(left, 'z', turn(N_Z, -1))  34.2 us
    ppermute x6, starting transfers between devices, ring_sum(): moved = [lax.ppermute(a, axis, turn(4, d)) for d in (2, 1, 3)]  23.7 us
    all_to_all x1, blocking collectives, shards(): lax.all_to_all(jnp.broadcast_to(meta[None], (N_Z,) + meta.shape), 'z', sp...  20.3 us
    ppermute x7, starting transfers between devices, shards(): right = lax.ppermute(right, 'z', turn(N_Z, 1))  19.2 us
    ppermute x7, waiting for transfers between devices, shards(): right = lax.ppermute(right, 'z', turn(N_Z, 1))  14.2 us
    pallas_call x4, Pallas kernels, make_rows(): pl.pallas_call(rows_kernel, grid=(D // wide,), in_specs=[pl.BlockSpec((1,...  14.2 us
    ppermute x2, starting transfers between devices, half_sum(): return keep + lax.ppermute(send, 'c', turn(2, 1))  12.9 us
    pallas_call x1, Pallas kernels, back_rows(): pl.pallas_call(back_kernel, grid_spec=pltpu.PrefetchScalarGridSpec(num_sc...  11.6 us
  transfers between devices with their start and end apart: 35, of which 18 were waited for; matrix products, arithmetic and copies ran while one was open for 2% of the time, Pallas kernels for 20%

profile of v6, /device:TPU:1, one launch (start us, length us, event | category | flops | bytes accessed | tf_op | source)
XLA Modules:
  0.0 269.3 jit_solution(3017754581587926265)
XLA Ops:
  8.2 1.8 pad_maximum_fusion
  10.1 4.4 %collective-permute-start.2 = (bf16[128,2048]{1,0:T(8,128)(2,1)S(1)}, bf16[128,2048]{1,0:T(8,128)(2,1)S(1)}, u32[]{:S(2)}, u32[]{:S(2)}) collective-permute-start(bf16[128,2048]{1,0:T(8,128)(2,1)S(1)} %copy-done.10), channel_id=1, source_target_pairs={{0,1},{1,2},{2,3},{3,4},{4,5},{5,6},{6,7},{7,8},{8,9},{9,10},{10,1... | collective-permute-start | bytes 1572872 | tf_op jit(solution)/shard_map/ppermute | solution.py:388
  14.4 9.5 %collective-permute-start = (bf16[128,2048]{1,0:T(8,128)(2,1)S(1)}, bf16[128,2048]{1,0:T(8,128)(2,1)S(1)}, u32[]{:S(2)}, u32[]{:S(2)}) collective-permute-start(bf16[128,2048]{1,0:T(8,128)(2,1)S(1)} %copy-done.10), channel_id=1, source_target_pairs={{0,15},{1,0},{2,1},{3,2},{4,3},{5,4},{6,5},{7,6},{8,7},{9,8},{10,9... | collective-permute-start | bytes 1572872 | tf_op jit(solution)/shard_map/ppermute | solution.py:389
  24.3 20.3 %all_to_all.15.meta_ref = f32[16,16,128]{2,1,0:T(8,128)} all-to-all(f32[16,16,128]{2,1,0:T(8,128)S(1)} %broadcast_in_dim.34), channel_id=1, replica_groups=mesh['y'=4,'c'=2,'x'=4,'z'=16] {'z'}, dimensions={0} | all-to-all | bytes 262144 | tf_op jit(solution)/shard_map/all_to_all | solution.py:378
  44.6 2.9 %collective-permute-start.4 = (bf16[128,2048]{1,0:T(8,128)(2,1)S(1)}, bf16[128,2048]{1,0:T(8,128)(2,1)S(1)}, u32[]{:S(2)}, u32[]{:S(2)}) collective-permute-start(bf16[128,2048]{1,0:T(8,128)(2,1)S(1)} %collective-permute-done.2.refs_1_), channel_id=1, source_target_pairs={{0,1},{1,2},{2,3},{3,4},{4,5},{5,6},{6,7},{7,8},{8,9},{9,10},{10,1... | collective-permute-start | bytes 1572872 | tf_op jit(solution)/shard_map/ppermute | solution.py:388
  47.6 3.6 %collective-permute-start.1 = (bf16[128,2048]{1,0:T(8,128)(2,1)S(1)}, bf16[128,2048]{1,0:T(8,128)(2,1)S(1)}, u32[]{:S(2)}, u32[]{:S(2)}) collective-permute-start(bf16[128,2048]{1,0:T(8,128)(2,1)S(1)} %collective-permute-done.refs_2_), channel_id=1, source_target_pairs={{0,15},{1,0},{2,1},{3,2},{4,3},{5,4},{6,5},{7,6},{8,7},{9,8},{10,9... | collective-permute-start | bytes 1572872 | tf_op jit(solution)/shard_map/ppermute | solution.py:389
  51.1 3.3 %picks.1 = (bf16[4,320,512]{2,1,0:T(8,128)(2,1)}, f32[4,320,128]{2,1,0:T(8,128)}, bf16[320,320]{1,0:T(8,128)(2,1)}, bf16[320,320]{1,0:T(8,128)(2,1)}) custom-call(s32[1]{0:T(128)} %bitcast.3.z_ref, f32[16,16,128]{2,1,0:T(8,128)} %all_to_all.15.meta_ref), custom_call_target="tpu_custom_call" | custom-call | flops 10000000 | bytes 4194304 | tf_op jit(solution)/shard_map/picks/pallas_call | solution.py:96
  54.5 3.1 %collective-permute-done.4.refs_3_ = bf16[128,2048]{1,0:T(8,128)(2,1)S(1)} collective-permute-done((bf16[128,2048]{1,0:T(8,128)(2,1)S(1)}, bf16[128,2048]{1,0:T(8,128)(2,1)S(1)}, u32[]{:S(2)}, u32[]{:S(2)}) %collective-permute-start.4) | collective-permute-done | bytes 524320 | tf_op jit(solution)/shard_map/ppermute | solution.py:388
  57.6 1.9 collective-permute-start.6
  59.5 4.6 %collective-permute-start.3 = (bf16[128,2048]{1,0:T(8,128)(2,1)S(1)}, bf16[128,2048]{1,0:T(8,128)(2,1)S(1)}, u32[]{:S(2)}, u32[]{:S(2)}) collective-permute-start(bf16[128,2048]{1,0:T(8,128)(2,1)S(1)} %collective-permute-done.1.refs_0_), channel_id=1, source_target_pairs={{0,15},{1,0},{2,1},{3,2},{4,3},{5,4},{6,5},{7,6},{8,7},{9,8},{10,9... | collective-permute-start | bytes 1572872 | tf_op jit(solution)/shard_map/ppermute | solution.py:389
  64.1 3.8 %rows.4.refs_0_ = bf16[4,80,2048]{2,1,0:T(8,128)(2,1)} custom-call(bf16[4,320,512]{2,1,0:T(8,128)(2,1)} %get-tuple-element.37.picks_ref, f32[4,320,128]{2,1,0:T(8,128)} %get-tuple-element.40.scale_ref, bf16[128,2048]{1,0:T(8,128)(2,1)} %refs_0_.1, bf16[128,2048]{1,0:T(8,128)(2,1)} %copy-done.11, bf16[128,2048]{1,0:T(8,128)(2,1)} %copy-done.12, ...), custom_call_target="tpu_custom_call" | custom-call | flops 700000000 | bytes 4194304 | tf_op jit(solution)/shard_map/rows/pallas_call | solution.py:125
  67.9 1.8 collective-permute-done.6.refs_1_
  69.7 1.9 collective-permute-start.8
  71.6 4.6 %collective-permute-start.5 = (bf16[128,2048]{1,0:T(8,128)(2,1)S(1)}, bf16[128,2048]{1,0:T(8,128)(2,1)S(1)}, u32[]{:S(2)}, u32[]{:S(2)}) collective-permute-start(bf16[128,2048]{1,0:T(8,128)(2,1)S(1)} %collective-permute-done.3.refs_2_), channel_id=1, source_target_pairs={{0,15},{1,0},{2,1},{3,2},{4,3},{5,4},{6,5},{7,6},{8,7},{9,8},{10,9... | collective-permute-start | bytes 1572872 | tf_op jit(solution)/shard_map/ppermute | solution.py:389
  76.2 5.0 %collective-permute-done.8.refs_3_ = bf16[128,2048]{1,0:T(8,128)(2,1)S(1)} collective-permute-done((bf16[128,2048]{1,0:T(8,128)(2,1)S(1)}, bf16[128,2048]{1,0:T(8,128)(2,1)S(1)}, u32[]{:S(2)}, u32[]{:S(2)}) %collective-permute-start.8) | collective-permute-done | bytes 524320 | tf_op jit(solution)/shard_map/ppermute | solution.py:388
  81.2 1.9 collective-permute-start.10
  83.1 4.6 %collective-permute-start.7 = (bf16[128,2048]{1,0:T(8,128)(2,1)S(1)}, bf16[128,2048]{1,0:T(8,128)(2,1)S(1)}, u32[]{:S(2)}, u32[]{:S(2)}) collective-permute-start(bf16[128,2048]{1,0:T(8,128)(2,1)S(1)} %collective-permute-done.5.refs_0_), channel_id=1, source_target_pairs={{0,15},{1,0},{2,1},{3,2},{4,3},{5,4},{6,5},{7,6},{8,7},{9,8},{10,9... | collective-permute-start | bytes 1572872 | tf_op jit(solution)/shard_map/ppermute | solution.py:389
  87.8 3.6 %rows.5.refs_1_ = bf16[4,80,2048]{2,1,0:T(8,128)(2,1)} custom-call(bf16[4,320,512]{2,1,0:T(8,128)(2,1)} %get-tuple-element.37.picks_ref, f32[4,320,128]{2,1,0:T(8,128)} %get-tuple-element.40.scale_ref, bf16[128,2048]{1,0:T(8,128)(2,1)} %copy-done.13, bf16[128,2048]{1,0:T(8,128)(2,1)} %copy-done.17, bf16[128,2048]{1,0:T(8,128)(2,1)} %copy-done.19, ...), custom_call_target="tpu_custom_call" | custom-call | flops 700000000 | bytes 4194304 | tf_op jit(solution)/shard_map/rows/pallas_call | solution.py:125
  91.3 1.4 collective-permute-done.10.refs_1_
  92.7 1.9 collective-permute-start.11
  94.7 4.7 %collective-permute-start.9 = (bf16[128,2048]{1,0:T(8,128)(2,1)S(1)}, bf16[128,2048]{1,0:T(8,128)(2,1)S(1)}, u32[]{:S(2)}, u32[]{:S(2)}) collective-permute-start(bf16[128,2048]{1,0:T(8,128)(2,1)S(1)} %collective-permute-done.7.refs_2_), channel_id=1, source_target_pairs={{0,15},{1,0},{2,1},{3,2},{4,3},{5,4},{6,5},{7,6},{8,7},{9,8},{10,9... | collective-permute-start | bytes 1572872 | tf_op jit(solution)/shard_map/ppermute | solution.py:389
  99.4 3.9 %all-to-all-start.1 = ((bf16[4,320,768]{2,1,0:T(8,128)(2,1)}), bf16[4,320,768]{2,1,0:T(8,128)(2,1)S(1)}, u32[]{:S(2)}, u32[]{:S(2)}) async-start(bf16[4,320,768]{2,1,0:T(8,128)(2,1)} %bitcast.44), calls=%async_computation.1 | async-start | bytes 3932160 | tf_op jit(solution)/shard_map/all_to_all | solution.py:381
  103.4 1.2 collective-permute-done.11.refs_3_
  104.6 1.7 collective-permute-done.9.refs_0_
  106.3 4.3 %collective-permute-start.12 = (bf16[128,2048]{1,0:T(8,128)(2,1)}, bf16[128,2048]{1,0:T(8,128)(2,1)S(1)}, u32[]{:S(2)}, u32[]{:S(2)}) collective-permute-start(bf16[128,2048]{1,0:T(8,128)(2,1)} %collective-permute-done.11.refs_3_), channel_id=1, source_target_pairs={{0,1},{1,2},{2,3},{3,4},{4,5},{5,6},{6,7},{7,8},{8,9},{9,10},{10,1... | collective-permute-start | bytes 1572872 | tf_op jit(solution)/shard_map/ppermute | solution.py:388
  110.6 2.7 collective-permute-start.13
  113.3 3.4 %rows.6.refs_2_ = bf16[4,80,2048]{2,1,0:T(8,128)(2,1)} custom-call(bf16[4,320,512]{2,1,0:T(8,128)(2,1)} %get-tuple-element.37.picks_ref, f32[4,320,128]{2,1,0:T(8,128)} %get-tuple-element.40.scale_ref, bf16[128,2048]{1,0:T(8,128)(2,1)} %copy-done.15, bf16[128,2048]{1,0:T(8,128)(2,1)} %copy-done.16, bf16[128,2048]{1,0:T(8,128)(2,1)} %copy-done.18, ...), custom_call_target="tpu_custom_call" | custom-call | flops 700000000 | bytes 4194304 | tf_op jit(solution)/shard_map/rows/pallas_call | solution.py:125
  116.7 1.7 collective-permute-done.12.refs_1_
  118.4 3.2 %collective-permute-done.13.refs_2_ = bf16[128,2048]{1,0:T(8,128)(2,1)S(1)} collective-permute-done((bf16[128,2048]{1,0:T(8,128)(2,1)S(1)}, bf16[128,2048]{1,0:T(8,128)(2,1)S(1)}, u32[]{:S(2)}, u32[]{:S(2)}) %collective-permute-start.13) | collective-permute-done | bytes 524320 | tf_op jit(solution)/shard_map/ppermute | solution.py:389
  121.7 4.6 %collective-permute-start.14 = (bf16[64,2048]{1,0:T(8,128)(2,1)S(1)}, bf16[64,2048]{1,0:T(8,128)(2,1)}, u32[]{:S(2)}, u32[]{:S(2)}) collective-permute-start(bf16[64,2048]{1,0:T(8,128)(2,1)S(1)} %slice.6), channel_id=1, source_target_pairs={{0,1},{1,2},{2,3},{3,4},{4,5},{5,6},{6,7},{7,8},{8,9},{9,10},{10,1... | collective-permute-start | bytes 786440 | tf_op jit(solution)/shard_map/ppermute | solution.py:411
  126.3 1.9 collective-permute-start.15
  128.2 5.6 %project.1.near_ref = bf16[4,96,320]{2,1,0:T(8,128)(2,1)} custom-call(bf16[4,8,112,2048]{3,2,1,0:T(8,128)(2,1)} %bitcast.41, bf16[320,320]{1,0:T(8,128)(2,1)} %get-tuple-element.50.order_ref, bf16[4,80,2048]{2,1,0:T(8,128)(2,1)} %rows.4.refs_0_, bf16[4,80,2048]{2,1,0:T(8,128)(2,1)} %rows.5.refs_1_, bf16[4,80,2048]{2,1,0:T(8,128)(2,1)} %rows.6.refs_2_), custom_call_target="tpu_custom_call" | custom-call | flops 1000000000 | bytes 6291456 | tf_op jit(solution)/shard_map/project/pallas_call | solution.py:158
  133.8 3.5 %rows.7.refs_3_.rows_ref = bf16[4,80,2048]{2,1,0:T(8,128)(2,1)} custom-call(bf16[4,320,512]{2,1,0:T(8,128)(2,1)} %get-tuple-element.37.picks_ref, f32[4,320,128]{2,1,0:T(8,128)} %get-tuple-element.40.scale_ref, bf16[128,2048]{1,0:T(8,128)(2,1)} %copy-done.14, bf16[128,2048]{1,0:T(8,128)(2,1)} %copy-done.8, bf16[128,2048]{1,0:T(8,128)(2,1)} %copy-done.9, ...), custom_call_target="tpu_custom_call" | custom-call | flops 700000000 | bytes 4194304 | tf_op jit(solution)/shard_map/rows/pallas_call | solution.py:125
  137.3 11.6 %back.1 = bf16[16,80,768]{2,1,0:T(8,128)(2,1)} custom-call(s32[1]{0:T(128)} %bitcast.3.z_ref, bf16[4,8,112,2048]{3,2,1,0:T(8,128)(2,1)} %bitcast.42, bf16[320,320]{1,0:T(8,128)(2,1)} %get-tuple-element.57.move_ref, bf16[4,80,2048]{2,1,0:T(8,128)(2,1)} %rows.4.refs_0_, bf16[4,80,2048]{2,1,0:T(8,128)(2,1)} %rows.5.refs_1_, bf16[4,80,2048]{2,1,0:T(8,128)(2,1)} %rows.6.refs_2_, ...), custom_call_target="tpu_custom_call" | custom-call | flops 4000000000 | bytes 20971520 | tf_op jit(solution)/shard_map/back/pallas_call | solution.py:220
  148.9 1.3 copy-done.4
  150.2 6.2 %all-to-all-start.2 = ((bf16[16,80,768]{2,1,0:T(8,128)(2,1)}), bf16[16,80,768]{2,1,0:T(8,128)(2,1)}, u32[]{:S(2)}, u32[]{:S(2)}) async-start(bf16[16,80,768]{2,1,0:T(8,128)(2,1)} %back.1), calls=%async_computation.2 | async-start | bytes 3932160 | tf_op jit(solution)/shard_map/all_to_all | solution.py:418
  156.5 5.6 %left.1 = f32[4,32,768]{2,1,0:T(8,128)} custom-call(bf16[4,96,320]{2,1,0:T(8,128)(2,1)} %project.1.near_ref, bf16[4,8,112,2048]{3,2,1,0:T(8,128)(2,1)} %bitcast.43, bf16[4,80,2048]{2,1,0:T(8,128)(2,1)} %rows.7.refs_3_.rows_ref, bf16[4,320,768]{2,1,0:T(8,128)(2,1)} %copy-done.4, bf16[320,320]{1,0:T(8,128)(2,1)} %get-tuple-element.50.order_ref), custom_call_target="tpu_custom_call" | custom-call | flops 1000000000 | bytes 6291456 | tf_op jit(solution)/shard_map/left/pallas_call | solution.py:182
  163.0 10.6 %collective-permute-start.16 = (f32[4,16,768]{2,1,0:T(8,128)S(1)}, f32[4,16,768]{2,1,0:T(8,128)S(1)}, u32[]{:S(2)}, u32[]{:S(2)}) collective-permute-start(f32[4,16,768]{2,1,0:T(8,128)S(1)} %constant_dynamic-slice_fusion.1), channel_id=1, source_target_pairs={{0,64},{64,0},{1,65},{65,1},{2,66},{66,2},{3,67},{67,3},{4,68},{68... | collective-permute-start | bytes 589832 | tf_op jit(solution)/shard_map/ppermute | solution.py:344
  173.6 1.0 collective-permute-done.16
  175.6 4.8 %collective-permute-start.17 = (f32[4,16,768]{2,1,0:T(8,128)S(1)}, f32[4,16,768]{2,1,0:T(8,128)S(1)}, u32[]{:S(2)}, u32[]{:S(2)}) collective-permute-start(f32[4,16,768]{2,1,0:T(8,128)S(1)} %dynamic-slice_add_fusion.1), channel_id=1, source_target_pairs={{0,256},{128,384},{256,0},{384,128},{1,257},{129,385},{257,1},{385... | collective-permute-start | bytes 589832 | tf_op jit(solution)/shard_map/ppermute | solution.py:348
  180.4 2.3 collective-permute-start.18
  182.7 4.2 %collective-permute-start.19 = (f32[4,16,768]{2,1,0:T(8,128)S(1)}, f32[4,16,768]{2,1,0:T(8,128)S(1)}, u32[]{:S(2)}, u32[]{:S(2)}) collective-permute-start(f32[4,16,768]{2,1,0:T(8,128)S(1)} %dynamic-slice_add_fusion.1), channel_id=1, source_target_pairs={{0,384},{128,0},{256,128},{384,256},{1,385},{129,1},{257,129},{385... | collective-permute-start | bytes 589832 | tf_op jit(solution)/shard_map/ppermute | solution.py:348
  186.9 2.5 collective-permute-done.18
  190.2 5.9 %collective-permute-start.20 = (f32[4,16,768]{2,1,0:T(8,128)S(1)}, f32[4,16,768]{2,1,0:T(8,128)S(1)}, u32[]{:S(2)}, u32[]{:S(2)}) collective-permute-start(f32[4,16,768]{2,1,0:T(8,128)S(1)} %add_add_fusion.1), channel_id=1, source_target_pairs={{0,32},{16,48},{32,0},{48,16},{1,33},{17,49},{33,1},{49,17},{2,34}... | collective-permute-start | bytes 589832 | tf_op jit(solution)/shard_map/ppermute | solution.py:348
  196.1 1.9 collective-permute-start.21
  198.0 4.6 %collective-permute-start.22 = (f32[4,16,768]{2,1,0:T(8,128)S(1)}, f32[4,16,768]{2,1,0:T(8,128)S(1)}, u32[]{:S(2)}, u32[]{:S(2)}) collective-permute-start(f32[4,16,768]{2,1,0:T(8,128)S(1)} %add_add_fusion.1), channel_id=1, source_target_pairs={{0,48},{16,0},{32,16},{48,32},{1,49},{17,1},{33,17},{49,33},{2,50}... | collective-permute-start | bytes 589832 | tf_op jit(solution)/shard_map/ppermute | solution.py:348
  202.6 1.5 collective-permute-done.21
  204.1 1.1 collective-permute-done.22
  205.3 5.3 %collective-permute-start.23 = (f32[4,16,768]{2,1,0:T(8,128)S(1)}, f32[4,16,768]{2,1,0:T(8,128)S(1)}, u32[]{:S(2)}, u32[]{:S(2)}) collective-permute-start(f32[4,16,768]{2,1,0:T(8,128)S(1)} %add_add_fusion.mine_ref), channel_id=1, source_target_pairs={{0,64},{64,0},{1,65},{65,1},{2,66},{66,2},{3,67},{67,3},{4,68},{68... | collective-permute-start | bytes 589832 | tf_op jit(solution)/shard_map/ppermute | solution.py:422
  211.5 3.5 %basis.1.basis_ref = f32[4,32,768]{2,1,0:T(8,128)S(1)} custom-call(s32[1]{0:T(128)} %bitcast.c_ref, f32[4,16,768]{2,1,0:T(8,128)S(1)} %add_add_fusion.mine_ref, f32[4,16,768]{2,1,0:T(8,128)S(1)} %collective-permute-done.23.other_ref), custom_call_target="tpu_custom_call" | custom-call | flops 10000000 | bytes 1048576 | tf_op jit(solution)/shard_map/basis/pallas_call | solution.py:330
  215.1 1.5 copy-done.5
  216.6 3.7 %right.1 = f32[4,32,2048]{2,1,0:T(8,128)S(1)} custom-call(f32[4,32,768]{2,1,0:T(8,128)S(1)} %basis.1.basis_ref, bf16[4,320,768]{2,1,0:T(8,128)(2,1)S(1)} %copy-done.5, bf16[320,320]{1,0:T(8,128)(2,1)S(1)} %copy-done.7, bf16[4,80,2048]{2,1,0:T(8,128)(2,1)S(1)} %copy-done, bf16[4,80,2048]{2,1,0:T(8,128)(2,1)S(1)} %copy-done.1, ...), custom_call_target="tpu_custom_call" | custom-call | flops 1000000000 | bytes 9437184 | tf_op jit(solution)/shard_map/right/pallas_call | solution.py:248
  221.3 2.3 collective-permute-start.24
  223.6 1.5 collective-permute-done.24
  225.1 1.1 dynamic-slice_add_fusion
  226.3 3.6 %collective-permute-start.25 = (f32[16,2048]{1,0:T(8,128)S(1)}, f32[16,2048]{1,0:T(8,128)S(1)}, u32[]{:S(2)}, u32[]{:S(2)}) collective-permute-start(f32[16,2048]{1,0:T(8,128)S(1)} %get-tuple-element.63), channel_id=1, source_target_pairs={{0,32},{16,48},{32,0},{48,16},{1,33},{17,49},{33,1},{49,17},{2,34}... | collective-permute-start | bytes 393224 | tf_op jit(solution)/shard_map/ppermute | solution.py:357
  229.8 4.2 %collective-permute-start.26 = (f32[16,2048]{1,0:T(8,128)S(1)}, f32[16,2048]{1,0:T(8,128)S(1)}, u32[]{:S(2)}, u32[]{:S(2)}) collective-permute-start(f32[16,2048]{1,0:T(8,128)S(1)} %get-tuple-element.65), channel_id=1, source_target_pairs={{0,16},{16,32},{32,48},{48,0},{1,17},{17,33},{33,49},{49,1},{2,18}... | collective-permute-start | bytes 393224 | tf_op jit(solution)/shard_map/ppermute | solution.py:357
  234.1 2.2 collective-permute-start.27
  237.4 2.8 %collective-permute-done.27 = f32[16,2048]{1,0:T(8,128)S(1)} collective-permute-done((f32[16,2048]{1,0:T(8,128)S(1)}, f32[16,2048]{1,0:T(8,128)S(1)}, u32[]{:S(2)}, u32[]{:S(2)}) %collective-permute-start.27) | collective-permute-done | bytes 131104 | tf_op jit(solution)/shard_map/ppermute | solution.py:357
  240.2 4.0 %collective-permute-start.28 = (f32[16,2048]{1,0:T(8,128)S(1)}, f32[16,2048]{1,0:T(8,128)S(1)}, u32[]{:S(2)}, u32[]{:S(2)}) collective-permute-start(f32[16,2048]{1,0:T(8,128)S(1)} %fusion.7), channel_id=1, source_target_pairs={{0,256},{128,384},{256,0},{384,128},{1,257},{129,385},{257,1},{385... | collective-permute-start | bytes 393224 | tf_op jit(solution)/shard_map/ppermute | solution.py:358
  244.3 3.8 %collective-permute-start.29 = (f32[16,2048]{1,0:T(8,128)S(1)}, f32[16,2048]{1,0:T(8,128)S(1)}, u32[]{:S(2)}, u32[]{:S(2)}) collective-permute-start(f32[16,2048]{1,0:T(8,128)S(1)} %fusion.7), channel_id=1, source_target_pairs={{0,128},{128,256},{256,384},{384,0},{1,129},{129,257},{257,385},{3... | collective-permute-start | bytes 393224 | tf_op jit(solution)/shard_map/ppermute | solution.py:358
  248.1 2.7 %collective-permute-start.30 = (f32[16,2048]{1,0:T(8,128)S(1)}, f32[16,2048]{1,0:T(8,128)S(1)}, u32[]{:S(2)}, u32[]{:S(2)}) collective-permute-start(f32[16,2048]{1,0:T(8,128)S(1)} %fusion.7), channel_id=1, source_target_pairs={{0,384},{128,0},{256,128},{384,256},{1,385},{129,1},{257,129},{385... | collective-permute-start | bytes 393224 | tf_op jit(solution)/shard_map/ppermute | solution.py:358
  250.8 5.4 %spread.1 = bf16[128,8,768]{2,1,0:T(8,128)(2,1)} custom-call(s32[1024,1]{1,0:T(8,128)S(1)} %reshape.39.place_ref, bf16[1280,768]{1,0:T(8,128)(2,1)} %bitcast.14.rows_ref), custom_call_target="tpu_custom_call" | custom-call | flops 2000000000 | bytes 4194304 | tf_op jit(solution)/shard_map/spread/pallas_call | solution.py:275
  256.3 4.4 %collective-permute-start.31 = (f32[16,2048]{1,0:T(8,128)S(1)}, f32[16,2048]{1,0:T(8,128)S(1)}, u32[]{:S(2)}, u32[]{:S(2)}) collective-permute-start(f32[16,2048]{1,0:T(8,128)S(1)} %add_add_fusion.2), channel_id=1, source_target_pairs={{0,64},{64,0},{1,65},{65,1},{2,66},{66,2},{3,67},{67,3},{4,68},{68... | collective-permute-start | bytes 393224 | tf_op jit(solution)/shard_map/ppermute | solution.py:362
  (92 shorter events, 9.0 us)
Async XLA Ops:
  7.2 2.9 %copy-start.10 = (bf16[128,2048]{1,0:T(8,128)(2,1)S(1)}, bf16[128,2048]{1,0:T(8,128)(2,1)}, u32[]{:S(2)}) copy-start(bf16[128,2048]{1,0:T(8,128)(2,1)} %refs_0_.1) | copy-start | bytes 1572868
  7.2 16.8 %copy-start.22 = (s32[128,8]{0,1:T(8,128)S(1)}, s32[128,8]{0,1:T(8,128)}, u32[]{:S(2)}) copy-start(s32[128,8]{0,1:T(8,128)} %param.7) | copy-start | bytes 12292
  7.2 17.1 %copy-start.23 = (f32[128,8]{0,1:T(8,128)S(1)}, f32[128,8]{0,1:T(8,128)}, u32[]{:S(2)}) copy-start(f32[128,8]{0,1:T(8,128)} %param.8) | copy-start | bytes 12292
  7.2 121.0 %all-gather.2.cloned.1.call-start = ((), (), s32[]{:S(2)}) async-start(), calls=%async_computation.3 | async-start | bytes 15138816 | tf_op jit(solution)/shard_map/all_gather | solution.py:375
  10.1 34.6 %collective-permute-start.2 = (bf16[128,2048]{1,0:T(8,128)(2,1)S(1)}, bf16[128,2048]{1,0:T(8,128)(2,1)S(1)}, u32[]{:S(2)}, u32[]{:S(2)}) collective-permute-start(bf16[128,2048]{1,0:T(8,128)(2,1)S(1)} %copy-done.10), channel_id=1, source_target_pairs={{0,1},{1,2},{2,3},{3,4},{4,5},{5,6},{6,7},{7,8},{8,9},{9,10},{10,1... | collective-permute-start | bytes 1572872 | tf_op jit(solution)/shard_map/ppermute | solution.py:388
  14.4 33.1 %collective-permute-start = (bf16[128,2048]{1,0:T(8,128)(2,1)S(1)}, bf16[128,2048]{1,0:T(8,128)(2,1)S(1)}, u32[]{:S(2)}, u32[]{:S(2)}) collective-permute-start(bf16[128,2048]{1,0:T(8,128)(2,1)S(1)} %copy-done.10), channel_id=1, source_target_pairs={{0,15},{1,0},{2,1},{3,2},{4,3},{5,4},{6,5},{7,6},{8,7},{9,8},{10,9... | collective-permute-start | bytes 1572872 | tf_op jit(solution)/shard_map/ppermute | solution.py:389
  44.6 19.5 %copy-start.11 = (bf16[128,2048]{1,0:T(8,128)(2,1)}, bf16[128,2048]{1,0:T(8,128)(2,1)S(1)}, u32[]{:S(2)}) copy-start(bf16[128,2048]{1,0:T(8,128)(2,1)S(1)} %collective-permute-done.2.refs_1_) | copy-start | bytes 1572868
  44.6 12.9 %collective-permute-start.4 = (bf16[128,2048]{1,0:T(8,128)(2,1)S(1)}, bf16[128,2048]{1,0:T(8,128)(2,1)S(1)}, u32[]{:S(2)}, u32[]{:S(2)}) collective-permute-start(bf16[128,2048]{1,0:T(8,128)(2,1)S(1)} %collective-permute-done.2.refs_1_), channel_id=1, source_target_pairs={{0,1},{1,2},{2,3},{3,4},{4,5},{5,6},{6,7},{7,8},{8,9},{9,10},{10,1... | collective-permute-start | bytes 1572872 | tf_op jit(solution)/shard_map/ppermute | solution.py:388
  47.6 16.5 %copy-start.12 = (bf16[128,2048]{1,0:T(8,128)(2,1)}, bf16[128,2048]{1,0:T(8,128)(2,1)S(1)}, u32[]{:S(2)}) copy-start(bf16[128,2048]{1,0:T(8,128)(2,1)S(1)} %collective-permute-done.refs_2_) | copy-start | bytes 1572868
  47.6 11.9 %collective-permute-start.1 = (bf16[128,2048]{1,0:T(8,128)(2,1)S(1)}, bf16[128,2048]{1,0:T(8,128)(2,1)S(1)}, u32[]{:S(2)}, u32[]{:S(2)}) collective-permute-start(bf16[128,2048]{1,0:T(8,128)(2,1)S(1)} %collective-permute-done.refs_2_), channel_id=1, source_target_pairs={{0,15},{1,0},{2,1},{3,2},{4,3},{5,4},{6,5},{7,6},{8,7},{9,8},{10,9... | collective-permute-start | bytes 1572872 | tf_op jit(solution)/shard_map/ppermute | solution.py:389
  57.6 6.5 %copy-start.20 = (bf16[128,2048]{1,0:T(8,128)(2,1)}, bf16[128,2048]{1,0:T(8,128)(2,1)S(1)}, u32[]{:S(2)}) copy-start(bf16[128,2048]{1,0:T(8,128)(2,1)S(1)} %collective-permute-done.4.refs_3_) | copy-start | bytes 1572868
  57.6 12.1 %collective-permute-start.6 = (bf16[128,2048]{1,0:T(8,128)(2,1)S(1)}, bf16[128,2048]{1,0:T(8,128)(2,1)S(1)}, u32[]{:S(2)}, u32[]{:S(2)}) collective-permute-start(bf16[128,2048]{1,0:T(8,128)(2,1)S(1)} %collective-permute-done.4.refs_3_), channel_id=1, source_target_pairs={{0,1},{1,2},{2,3},{3,4},{4,5},{5,6},{6,7},{7,8},{8,9},{9,10},{10,1... | collective-permute-start | bytes 1572872 | tf_op jit(solution)/shard_map/ppermute | solution.py:388
  59.5 8.4 %copy-start.13 = (bf16[128,2048]{1,0:T(8,128)(2,1)}, bf16[128,2048]{1,0:T(8,128)(2,1)S(1)}, u32[]{:S(2)}) copy-start(bf16[128,2048]{1,0:T(8,128)(2,1)S(1)} %collective-permute-done.1.refs_0_) | copy-start | bytes 1572868
  59.5 12.1 %collective-permute-start.3 = (bf16[128,2048]{1,0:T(8,128)(2,1)S(1)}, bf16[128,2048]{1,0:T(8,128)(2,1)S(1)}, u32[]{:S(2)}, u32[]{:S(2)}) collective-permute-start(bf16[128,2048]{1,0:T(8,128)(2,1)S(1)} %collective-permute-done.1.refs_0_), channel_id=1, source_target_pairs={{0,15},{1,0},{2,1},{3,2},{4,3},{5,4},{6,5},{7,6},{8,7},{9,8},{10,9... | collective-permute-start | bytes 1572872 | tf_op jit(solution)/shard_map/ppermute | solution.py:389
  69.7 18.0 %copy-start.17 = (bf16[128,2048]{1,0:T(8,128)(2,1)}, bf16[128,2048]{1,0:T(8,128)(2,1)S(1)}, u32[]{:S(2)}) copy-start(bf16[128,2048]{1,0:T(8,128)(2,1)S(1)} %collective-permute-done.6.refs_1_) | copy-start | bytes 1572868
  69.7 11.5 %collective-permute-start.8 = (bf16[128,2048]{1,0:T(8,128)(2,1)S(1)}, bf16[128,2048]{1,0:T(8,128)(2,1)S(1)}, u32[]{:S(2)}, u32[]{:S(2)}) collective-permute-start(bf16[128,2048]{1,0:T(8,128)(2,1)S(1)} %collective-permute-done.6.refs_1_), channel_id=1, source_target_pairs={{0,1},{1,2},{2,3},{3,4},{4,5},{5,6},{6,7},{7,8},{8,9},{9,10},{10,1... | collective-permute-start | bytes 1572872 | tf_op jit(solution)/shard_map/ppermute | solution.py:388
  71.6 16.1 %copy-start.19 = (bf16[128,2048]{1,0:T(8,128)(2,1)}, bf16[128,2048]{1,0:T(8,128)(2,1)S(1)}, u32[]{:S(2)}) copy-start(bf16[128,2048]{1,0:T(8,128)(2,1)S(1)} %collective-permute-done.3.refs_2_) | copy-start | bytes 1572868
  71.6 11.5 %collective-permute-start.5 = (bf16[128,2048]{1,0:T(8,128)(2,1)S(1)}, bf16[128,2048]{1,0:T(8,128)(2,1)S(1)}, u32[]{:S(2)}, u32[]{:S(2)}) collective-permute-start(bf16[128,2048]{1,0:T(8,128)(2,1)S(1)} %collective-permute-done.3.refs_2_), channel_id=1, source_target_pairs={{0,15},{1,0},{2,1},{3,2},{4,3},{5,4},{6,5},{7,6},{8,7},{9,8},{10,9... | collective-permute-start | bytes 1572872 | tf_op jit(solution)/shard_map/ppermute | solution.py:389
  81.2 6.5 %copy-start.21 = (bf16[128,2048]{1,0:T(8,128)(2,1)}, bf16[128,2048]{1,0:T(8,128)(2,1)S(1)}, u32[]{:S(2)}) copy-start(bf16[128,2048]{1,0:T(8,128)(2,1)S(1)} %collective-permute-done.8.refs_3_) | copy-start | bytes 1572868
  81.2 11.5 %collective-permute-start.10 = (bf16[128,2048]{1,0:T(8,128)(2,1)S(1)}, bf16[128,2048]{1,0:T(8,128)(2,1)S(1)}, u32[]{:S(2)}, u32[]{:S(2)}) collective-permute-start(bf16[128,2048]{1,0:T(8,128)(2,1)S(1)} %collective-permute-done.8.refs_3_), channel_id=1, source_target_pairs={{0,1},{1,2},{2,3},{3,4},{4,5},{5,6},{6,7},{7,8},{8,9},{9,10},{10,1... | collective-permute-start | bytes 1572872 | tf_op jit(solution)/shard_map/ppermute | solution.py:388
  83.1 8.2 %copy-start.15 = (bf16[128,2048]{1,0:T(8,128)(2,1)}, bf16[128,2048]{1,0:T(8,128)(2,1)S(1)}, u32[]{:S(2)}) copy-start(bf16[128,2048]{1,0:T(8,128)(2,1)S(1)} %collective-permute-done.5.refs_0_) | copy-start | bytes 1572868
  83.1 11.5 %collective-permute-start.7 = (bf16[128,2048]{1,0:T(8,128)(2,1)S(1)}, bf16[128,2048]{1,0:T(8,128)(2,1)S(1)}, u32[]{:S(2)}, u32[]{:S(2)}) collective-permute-start(bf16[128,2048]{1,0:T(8,128)(2,1)S(1)} %collective-permute-done.5.refs_0_), channel_id=1, source_target_pairs={{0,15},{1,0},{2,1},{3,2},{4,3},{5,4},{6,5},{7,6},{8,7},{9,8},{10,9... | collective-permute-start | bytes 1572872 | tf_op jit(solution)/shard_map/ppermute | solution.py:389
  92.7 6.7 %copy-start.16 = (bf16[128,2048]{1,0:T(8,128)(2,1)}, bf16[128,2048]{1,0:T(8,128)(2,1)S(1)}, u32[]{:S(2)}) copy-start(bf16[128,2048]{1,0:T(8,128)(2,1)S(1)} %collective-permute-done.10.refs_1_) | copy-start | bytes 1572868
  92.7 11.8 %collective-permute-start.11 = (bf16[128,2048]{1,0:T(8,128)(2,1)S(1)}, bf16[128,2048]{1,0:T(8,128)(2,1)}, u32[]{:S(2)}, u32[]{:S(2)}) collective-permute-start(bf16[128,2048]{1,0:T(8,128)(2,1)S(1)} %collective-permute-done.10.refs_1_), channel_id=1, source_target_pairs={{0,1},{1,2},{2,3},{3,4},{4,5},{5,6},{6,7},{7,8},{8,9},{9,10},{10,1... | collective-permute-start | bytes 1572872 | tf_op jit(solution)/shard_map/ppermute | solution.py:388
  94.7 4.7 %copy-start.18 = (bf16[128,2048]{1,0:T(8,128)(2,1)}, bf16[128,2048]{1,0:T(8,128)(2,1)S(1)}, u32[]{:S(2)}) copy-start(bf16[128,2048]{1,0:T(8,128)(2,1)S(1)} %collective-permute-done.7.refs_2_) | copy-start | bytes 1572868
  94.7 11.7 %collective-permute-start.9 = (bf16[128,2048]{1,0:T(8,128)(2,1)S(1)}, bf16[128,2048]{1,0:T(8,128)(2,1)S(1)}, u32[]{:S(2)}, u32[]{:S(2)}) collective-permute-start(bf16[128,2048]{1,0:T(8,128)(2,1)S(1)} %collective-permute-done.7.refs_2_), channel_id=1, source_target_pairs={{0,15},{1,0},{2,1},{3,2},{4,3},{5,4},{6,5},{7,6},{8,7},{9,8},{10,9... | collective-permute-start | bytes 1572872 | tf_op jit(solution)/shard_map/ppermute | solution.py:389
  99.4 49.5 %all-to-all-start.1 = ((bf16[4,320,768]{2,1,0:T(8,128)(2,1)}), bf16[4,320,768]{2,1,0:T(8,128)(2,1)S(1)}, u32[]{:S(2)}, u32[]{:S(2)}) async-start(bf16[4,320,768]{2,1,0:T(8,128)(2,1)} %bitcast.44), calls=%async_computation.1 | async-start | bytes 3932160 | tf_op jit(solution)/shard_map/all_to_all | solution.py:381
  106.3 10.4 %copy-start.14 = (bf16[128,2048]{1,0:T(8,128)(2,1)}, bf16[128,2048]{1,0:T(8,128)(2,1)S(1)}, u32[]{:S(2)}) copy-start(bf16[128,2048]{1,0:T(8,128)(2,1)S(1)} %collective-permute-done.9.refs_0_) | copy-start | bytes 1572868
  106.3 12.1 %collective-permute-start.12 = (bf16[128,2048]{1,0:T(8,128)(2,1)}, bf16[128,2048]{1,0:T(8,128)(2,1)S(1)}, u32[]{:S(2)}, u32[]{:S(2)}) collective-permute-start(bf16[128,2048]{1,0:T(8,128)(2,1)} %collective-permute-done.11.refs_3_), channel_id=1, source_target_pairs={{0,1},{1,2},{2,3},{3,4},{4,5},{5,6},{6,7},{7,8},{8,9},{9,10},{10,1... | collective-permute-start | bytes 1572872 | tf_op jit(solution)/shard_map/ppermute | solution.py:388
  110.6 11.0 %collective-permute-start.13 = (bf16[128,2048]{1,0:T(8,128)(2,1)S(1)}, bf16[128,2048]{1,0:T(8,128)(2,1)S(1)}, u32[]{:S(2)}, u32[]{:S(2)}) collective-permute-start(bf16[128,2048]{1,0:T(8,128)(2,1)S(1)} %collective-permute-done.9.refs_0_), channel_id=1, source_target_pairs={{0,15},{1,0},{2,1},{3,2},{4,3},{5,4},{6,5},{7,6},{8,7},{9,8},{10,9... | collective-permute-start | bytes 1572872 | tf_op jit(solution)/shard_map/ppermute | solution.py:389
  118.4 15.4 %copy-start.8 = (bf16[128,2048]{1,0:T(8,128)(2,1)}, bf16[128,2048]{1,0:T(8,128)(2,1)S(1)}, u32[]{:S(2)}) copy-start(bf16[128,2048]{1,0:T(8,128)(2,1)S(1)} %collective-permute-done.12.refs_1_) | copy-start | bytes 1572868
  121.6 12.2 %copy-start.9 = (bf16[128,2048]{1,0:T(8,128)(2,1)}, bf16[128,2048]{1,0:T(8,128)(2,1)S(1)}, u32[]{:S(2)}) copy-start(bf16[128,2048]{1,0:T(8,128)(2,1)S(1)} %collective-permute-done.13.refs_2_) | copy-start | bytes 1572868
  121.7 12.2 %collective-permute-start.14 = (bf16[64,2048]{1,0:T(8,128)(2,1)S(1)}, bf16[64,2048]{1,0:T(8,128)(2,1)}, u32[]{:S(2)}, u32[]{:S(2)}) collective-permute-start(bf16[64,2048]{1,0:T(8,128)(2,1)S(1)} %slice.6), channel_id=1, source_target_pairs={{0,1},{1,2},{2,3},{3,4},{4,5},{5,6},{6,7},{7,8},{8,9},{9,10},{10,1... | collective-permute-start | bytes 786440 | tf_op jit(solution)/shard_map/ppermute | solution.py:411
  126.3 7.6 %collective-permute-start.15 = (bf16[64,2048]{1,0:T(8,128)(2,1)S(1)}, bf16[64,2048]{1,0:T(8,128)(2,1)}, u32[]{:S(2)}, u32[]{:S(2)}) collective-permute-start(bf16[64,2048]{1,0:T(8,128)(2,1)S(1)} %slice.7), channel_id=1, source_target_pairs={{0,15},{1,0},{2,1},{3,2},{4,3},{5,4},{6,5},{7,6},{8,7},{9,8},{10,9... | collective-permute-start | bytes 786440 | tf_op jit(solution)/shard_map/ppermute | solution.py:412
  148.9 1.3 copy-start.4
  150.2 100.6 %all-to-all-start.2 = ((bf16[16,80,768]{2,1,0:T(8,128)(2,1)}), bf16[16,80,768]{2,1,0:T(8,128)(2,1)}, u32[]{:S(2)}, u32[]{:S(2)}) async-start(bf16[16,80,768]{2,1,0:T(8,128)(2,1)} %back.1), calls=%async_computation.2 | async-start | bytes 3932160 | tf_op jit(solution)/shard_map/all_to_all | solution.py:418
  156.5 58.5 %copy-start.2 = (bf16[4,80,2048]{2,1,0:T(8,128)(2,1)S(1)}, bf16[4,80,2048]{2,1,0:T(8,128)(2,1)}, u32[]{:S(2)}) copy-start(bf16[4,80,2048]{2,1,0:T(8,128)(2,1)} %rows.6.refs_2_) | copy-start | bytes 3932164
  156.5 58.5 %copy-start.3 = (bf16[4,80,2048]{2,1,0:T(8,128)(2,1)S(1)}, bf16[4,80,2048]{2,1,0:T(8,128)(2,1)}, u32[]{:S(2)}) copy-start(bf16[4,80,2048]{2,1,0:T(8,128)(2,1)} %rows.7.refs_3_.rows_ref) | copy-start | bytes 3932164
  163.0 11.6 %collective-permute-start.16 = (f32[4,16,768]{2,1,0:T(8,128)S(1)}, f32[4,16,768]{2,1,0:T(8,128)S(1)}, u32[]{:S(2)}, u32[]{:S(2)}) collective-permute-start(f32[4,16,768]{2,1,0:T(8,128)S(1)} %constant_dynamic-slice_fusion.1), channel_id=1, source_target_pairs={{0,64},{64,0},{1,65},{65,1},{2,66},{66,2},{3,67},{67,3},{4,68},{68... | collective-permute-start | bytes 589832 | tf_op jit(solution)/shard_map/ppermute | solution.py:344
  173.6 41.4 %copy-start = (bf16[4,80,2048]{2,1,0:T(8,128)(2,1)S(1)}, bf16[4,80,2048]{2,1,0:T(8,128)(2,1)}, u32[]{:S(2)}) copy-start(bf16[4,80,2048]{2,1,0:T(8,128)(2,1)} %rows.4.refs_0_) | copy-start | bytes 3932164
  173.6 41.4 %copy-start.1 = (bf16[4,80,2048]{2,1,0:T(8,128)(2,1)S(1)}, bf16[4,80,2048]{2,1,0:T(8,128)(2,1)}, u32[]{:S(2)}) copy-start(bf16[4,80,2048]{2,1,0:T(8,128)(2,1)} %rows.5.refs_1_) | copy-start | bytes 3932164
  173.6 41.4 %copy-start.7 = (bf16[320,320]{1,0:T(8,128)(2,1)S(1)}, bf16[320,320]{1,0:T(8,128)(2,1)}, u32[]{:S(2)}) copy-start(bf16[320,320]{1,0:T(8,128)(2,1)} %get-tuple-element.50.order_ref) | copy-start | bytes 614404
  175.6 11.3 %collective-permute-start.17 = (f32[4,16,768]{2,1,0:T(8,128)S(1)}, f32[4,16,768]{2,1,0:T(8,128)S(1)}, u32[]{:S(2)}, u32[]{:S(2)}) collective-permute-start(f32[4,16,768]{2,1,0:T(8,128)S(1)} %dynamic-slice_add_fusion.1), channel_id=1, source_target_pairs={{0,256},{128,384},{256,0},{384,128},{1,257},{129,385},{257,1},{385... | collective-permute-start | bytes 589832 | tf_op jit(solution)/shard_map/ppermute | solution.py:348
  180.4 9.0 %collective-permute-start.18 = (f32[4,16,768]{2,1,0:T(8,128)S(1)}, f32[4,16,768]{2,1,0:T(8,128)S(1)}, u32[]{:S(2)}, u32[]{:S(2)}) collective-permute-start(f32[4,16,768]{2,1,0:T(8,128)S(1)} %dynamic-slice_add_fusion.1), channel_id=1, source_target_pairs={{0,128},{128,256},{256,384},{384,0},{1,129},{129,257},{257,385},{3... | collective-permute-start | bytes 589832 | tf_op jit(solution)/shard_map/ppermute | solution.py:348
  182.7 7.5 %collective-permute-start.19 = (f32[4,16,768]{2,1,0:T(8,128)S(1)}, f32[4,16,768]{2,1,0:T(8,128)S(1)}, u32[]{:S(2)}, u32[]{:S(2)}) collective-permute-start(f32[4,16,768]{2,1,0:T(8,128)S(1)} %dynamic-slice_add_fusion.1), channel_id=1, source_target_pairs={{0,384},{128,0},{256,128},{384,256},{1,385},{129,1},{257,129},{385... | collective-permute-start | bytes 589832 | tf_op jit(solution)/shard_map/ppermute | solution.py:348
  190.2 12.4 %collective-permute-start.20 = (f32[4,16,768]{2,1,0:T(8,128)S(1)}, f32[4,16,768]{2,1,0:T(8,128)S(1)}, u32[]{:S(2)}, u32[]{:S(2)}) collective-permute-start(f32[4,16,768]{2,1,0:T(8,128)S(1)} %add_add_fusion.1), channel_id=1, source_target_pairs={{0,32},{16,48},{32,0},{48,16},{1,33},{17,49},{33,1},{49,17},{2,34}... | collective-permute-start | bytes 589832 | tf_op jit(solution)/shard_map/ppermute | solution.py:348
  196.1 8.0 %collective-permute-start.21 = (f32[4,16,768]{2,1,0:T(8,128)S(1)}, f32[4,16,768]{2,1,0:T(8,128)S(1)}, u32[]{:S(2)}, u32[]{:S(2)}) collective-permute-start(f32[4,16,768]{2,1,0:T(8,128)S(1)} %add_add_fusion.1), channel_id=1, source_target_pairs={{0,16},{16,32},{32,48},{48,0},{1,17},{17,33},{33,49},{49,1},{2,18}... | collective-permute-start | bytes 589832 | tf_op jit(solution)/shard_map/ppermute | solution.py:348
  198.0 7.2 %collective-permute-start.22 = (f32[4,16,768]{2,1,0:T(8,128)S(1)}, f32[4,16,768]{2,1,0:T(8,128)S(1)}, u32[]{:S(2)}, u32[]{:S(2)}) collective-permute-start(f32[4,16,768]{2,1,0:T(8,128)S(1)} %add_add_fusion.1), channel_id=1, source_target_pairs={{0,48},{16,0},{32,16},{48,32},{1,49},{17,1},{33,17},{49,33},{2,50}... | collective-permute-start | bytes 589832 | tf_op jit(solution)/shard_map/ppermute | solution.py:348
  205.3 6.2 %collective-permute-start.23 = (f32[4,16,768]{2,1,0:T(8,128)S(1)}, f32[4,16,768]{2,1,0:T(8,128)S(1)}, u32[]{:S(2)}, u32[]{:S(2)}) collective-permute-start(f32[4,16,768]{2,1,0:T(8,128)S(1)} %add_add_fusion.mine_ref), channel_id=1, source_target_pairs={{0,64},{64,0},{1,65},{65,1},{2,66},{66,2},{3,67},{67,3},{4,68},{68... | collective-permute-start | bytes 589832 | tf_op jit(solution)/shard_map/ppermute | solution.py:422
  215.0 1.5 copy-start.5
  220.3 1.0 copy-start.6
  221.3 3.8 %collective-permute-start.24 = (f32[4,16,2048]{2,1,0:T(8,128)S(1)}, f32[4,16,2048]{2,1,0:T(8,128)S(1)}, u32[]{:S(2)}, u32[]{:S(2)}) collective-permute-start(f32[4,16,2048]{2,1,0:T(8,128)S(1)} %constant_dynamic-slice_fusion), channel_id=1, source_target_pairs={{0,64},{64,0},{1,65},{65,1},{2,66},{66,2},{3,67},{67,3},{4,68},{68... | collective-permute-start | bytes 1572872 | tf_op jit(solution)/shard_map/ppermute | solution.py:344
  226.3 10.4 %collective-permute-start.25 = (f32[16,2048]{1,0:T(8,128)S(1)}, f32[16,2048]{1,0:T(8,128)S(1)}, u32[]{:S(2)}, u32[]{:S(2)}) collective-permute-start(f32[16,2048]{1,0:T(8,128)S(1)} %get-tuple-element.63), channel_id=1, source_target_pairs={{0,32},{16,48},{32,0},{48,16},{1,33},{17,49},{33,1},{49,17},{2,34}... | collective-permute-start | bytes 393224 | tf_op jit(solution)/shard_map/ppermute | solution.py:357
  229.8 7.6 %collective-permute-start.26 = (f32[16,2048]{1,0:T(8,128)S(1)}, f32[16,2048]{1,0:T(8,128)S(1)}, u32[]{:S(2)}, u32[]{:S(2)}) collective-permute-start(f32[16,2048]{1,0:T(8,128)S(1)} %get-tuple-element.65), channel_id=1, source_target_pairs={{0,16},{16,32},{32,48},{48,0},{1,17},{17,33},{33,49},{49,1},{2,18}... | collective-permute-start | bytes 393224 | tf_op jit(solution)/shard_map/ppermute | solution.py:357
  234.1 6.1 %collective-permute-start.27 = (f32[16,2048]{1,0:T(8,128)S(1)}, f32[16,2048]{1,0:T(8,128)S(1)}, u32[]{:S(2)}, u32[]{:S(2)}) collective-permute-start(f32[16,2048]{1,0:T(8,128)S(1)} %get-tuple-element.64), channel_id=1, source_target_pairs={{0,48},{16,0},{32,16},{48,32},{1,49},{17,1},{33,17},{49,33},{2,50}... | collective-permute-start | bytes 393224 | tf_op jit(solution)/shard_map/ppermute | solution.py:357
  240.2 16.0 %collective-permute-start.28 = (f32[16,2048]{1,0:T(8,128)S(1)}, f32[16,2048]{1,0:T(8,128)S(1)}, u32[]{:S(2)}, u32[]{:S(2)}) collective-permute-start(f32[16,2048]{1,0:T(8,128)S(1)} %fusion.7), channel_id=1, source_target_pairs={{0,256},{128,384},{256,0},{384,128},{1,257},{129,385},{257,1},{385... | collective-permute-start | bytes 393224 | tf_op jit(solution)/shard_map/ppermute | solution.py:358
  244.3 12.0 %collective-permute-start.29 = (f32[16,2048]{1,0:T(8,128)S(1)}, f32[16,2048]{1,0:T(8,128)S(1)}, u32[]{:S(2)}, u32[]{:S(2)}) collective-permute-start(f32[16,2048]{1,0:T(8,128)S(1)} %fusion.7), channel_id=1, source_target_pairs={{0,128},{128,256},{256,384},{384,0},{1,129},{129,257},{257,385},{3... | collective-permute-start | bytes 393224 | tf_op jit(solution)/shard_map/ppermute | solution.py:358
  248.1 8.2 %collective-permute-start.30 = (f32[16,2048]{1,0:T(8,128)S(1)}, f32[16,2048]{1,0:T(8,128)S(1)}, u32[]{:S(2)}, u32[]{:S(2)}) collective-permute-start(f32[16,2048]{1,0:T(8,128)S(1)} %fusion.7), channel_id=1, source_target_pairs={{0,384},{128,0},{256,128},{384,256},{1,385},{129,1},{257,129},{385... | collective-permute-start | bytes 393224 | tf_op jit(solution)/shard_map/ppermute | solution.py:358
  256.3 5.4 %collective-permute-start.31 = (f32[16,2048]{1,0:T(8,128)S(1)}, f32[16,2048]{1,0:T(8,128)S(1)}, u32[]{:S(2)}, u32[]{:S(2)}) collective-permute-start(f32[16,2048]{1,0:T(8,128)S(1)} %add_add_fusion.2), channel_id=1, source_target_pairs={{0,64},{64,0},{1,65},{65,1},{2,66},{66,2},{3,67},{67,3},{4,68},{68... | collective-permute-start | bytes 393224 | tf_op jit(solution)/shard_map/ppermute | solution.py:362
Sparse Core Ops, SparseCore 0:
  11.2 88.8 all-gather.1
